TPU v7x, 32 devices: a whole 2x2x4 slice. The times are simulated.
32 devices in a mesh: dp: 8 (over z, core), fsdp: 4 (over y, x).
Axes of the slice: x: 2, y: 2, z: 4, core: 2. Of those that a mesh axis runs over, the one named last changes fastest.
Arguments:
- frames: bfloat16 [32, 512, 1024], P(('dp', 'fsdp')), may hold values from -6 to 6
- segment_ids: int32 [32, 512], P(('dp', 'fsdp')), may hold values from 0 to 2, never falling along the last dimension, each value on 1 to 256 neighbouring positions
- out_grad: bfloat16 [32, 512, 1024], P(('dp', 'fsdp')), may hold values from -6 to 6
- blocks: float32 [23, 1024, 1024], P(None, 'fsdp'), may hold values from -0.75 to 0.75
- small_params: float32 [17, 1024], replicated, may hold values from -1.5 to 1.6
- owners: int32 [23], replicated, may hold values from 0 to 7, as said below
- left_bases: float32 [24, 1024, 1024], P('dp', 'fsdp'), may hold values from -1 to 1, as said below
- right_bases: float32 [24, 1024, 1024], P('dp'), may hold values from -1 to 1, as said below
- block_first: float32 [24, 1024, 1024], P('dp', 'fsdp'), may hold values from -224 to 224
- block_second: float32 [24, 1024, 1024], P('dp', 'fsdp'), may hold values from 1638.4 to 6553.6
- small_first: float32 [17, 1024], replicated, may hold values from -384 to 384
- small_second: float32 [17, 1024], replicated, may hold values from 4096 to 16384
Outputs:
- layer_out: bfloat16 [32, 512, 1024], P(('dp', 'fsdp'))
- frames_grad: float32 [32, 512, 1024], P(('dp', 'fsdp'))
- block_grads: float32 [24, 1024, 1024], P('dp', 'fsdp')
- first_new: float32 [24, 1024, 1024], P('dp', 'fsdp')
- second_new: float32 [24, 1024, 1024], P('dp', 'fsdp')
- block_weights: float32 [24, 1024, 1024], P('dp', 'fsdp')
- small_grads: float32 [17, 1024], replicated
- small_weights: float32 [17, 1024], replicated
- small_first_new: float32 [17, 1024], replicated
- small_second_new: float32 [17, 1024], replicated
Inputs may be any that keep to these rules, and one draw needn't show every extreme that they name: owners[b] is the index along dp of the group that updates block b; no index is named more than 3 times, and at least one index exactly 3 times. `left_bases`: each slot's matrix is orthogonal. `right_bases`: each slot's matrix is orthogonal.
All inputs are finite; a program needn't handle non-finite values.
Results may differ from a plain program's by a relative error of at most 0.018.
Values may be sent and summed in bfloat16 or wider, within the bound.
No kernel may reach another device: no remote copies, remote signals or barrier semaphores. Data moves between devices by JAX's collectives and lax.ppermute only.
A program may use at most 576 MiB of HBM per device.

v0:
```python
import jax
import jax.numpy as jnp
from jax import lax
from jax.sharding import PartitionSpec as P

D = 1024
HEADS = 8
FF = 4096
KERNEL = 5
LENGTH = 512
HEAD = 128


EPS_NORM = 1e-05
EPS_ADAM = 1e-08
LEARN_RATE = 0.02
SMALL_RATE = 0.3
DECAY_WEIGHT = 0.01
BETA_DECAY = 0.5
MASKED = -1000000000.0
HIGHEST = lax.Precision.HIGHEST


def norm_apply(values, scale_row, shift_row):
    average = jnp.mean(values, axis=-1, keepdims=True)
    centered = values - average
    variance = jnp.mean(centered * centered, axis=-1, keepdims=True)
    return centered * lax.rsqrt(variance + EPS_NORM) * scale_row + shift_row


def swish(values):
    return values * jax.nn.sigmoid(values)


def depthwise(gated_rows, kernel_taps, segment_ids):
    length = gated_rows.shape[1]
    margin = KERNEL // 2
    padded = jnp.pad(gated_rows, ((0, 0), (margin, margin), (0, 0)))
    segment_pad = jnp.pad(segment_ids, ((0, 0), (margin, margin)), constant_values=-1)
    summed = jnp.zeros_like(gated_rows)
    for offset in range(KERNEL):
        matched = (segment_pad[:, offset : offset + length] == segment_ids)[:, :, None]
        summed = summed + kernel_taps[offset] * jnp.where(
            matched, padded[:, offset : offset + length], 0.0
        )
    return summed


def slot_tables(owners, groups, count_blocks):
    capacity = (count_blocks + groups - 1) // groups
    block_index = jnp.arange(count_blocks, dtype=jnp.int32)
    earlier = (owners[None, :] == owners[:, None]) & (block_index[None, :] < block_index[:, None])
    ranking = jnp.sum(earlier.astype(jnp.int32), axis=1)
    slot_of = owners * capacity + ranking
    matches = slot_of[None, :] == jnp.arange(capacity * groups, dtype=jnp.int32)[:, None]
    slot_used = jnp.sum(matches.astype(jnp.int32), axis=1)
    slot_block = jnp.sum(jnp.where(matches, block_index[None, :], 0), axis=1)
    return (slot_block, slot_used)


def gated_conv(before, kernel_taps, segment_ids):
    rows_here = segment_ids.shape[0]
    gated_rows = before[:, 0] * jax.nn.sigmoid(before[:, 1])
    shaped = gated_rows.reshape(rows_here, -1, gated_rows.shape[-1])
    return depthwise(shaped, kernel_taps, segment_ids).reshape(gated_rows.shape)


def feed_forward(hidden, scale_row, shift_row, weight_in, weight_out):
    normed, norm_pullback = jax.vjp(norm_apply, hidden, scale_row, shift_row)
    normed_low = normed.astype(jnp.bfloat16)
    lifted = jnp.einsum("td,jdh->tjh", normed_low, weight_in, preferred_element_type=jnp.float32)
    activated, swish_pullback = jax.vjp(swish, lifted)
    activated_low = activated.astype(jnp.bfloat16)
    result = jnp.einsum(
        "tjh,jhe->te", activated_low, weight_out, preferred_element_type=jnp.float32
    )
    return (hidden + 0.5 * result, (norm_pullback, normed_low, swish_pullback, activated_low))


def feed_backward(gradient, saved, weight_in, weight_out):
    norm_pullback, normed_low, swish_pullback, activated_low = saved
    result_low = (0.5 * gradient).astype(jnp.bfloat16)
    out_weight_grad = jnp.einsum(
        "tjh,te->jhe", activated_low, result_low, preferred_element_type=jnp.float32
    )
    activated_grad = jnp.einsum(
        "te,jhe->tjh", result_low, weight_out, preferred_element_type=jnp.float32
    )
    (lifted_grad,) = swish_pullback(activated_grad)
    lifted_low = lifted_grad.astype(jnp.bfloat16)
    in_weight_grad = jnp.einsum(
        "td,tjh->jdh", normed_low, lifted_low, preferred_element_type=jnp.float32
    )
    normed_grad = jnp.einsum(
        "tjh,jdh->td", lifted_low, weight_in, preferred_element_type=jnp.float32
    )
    hidden_grad, scale_grad, shift_grad = norm_pullback(normed_grad)
    return (gradient + hidden_grad, scale_grad, shift_grad, in_weight_grad, out_weight_grad)


def masked_scores(queries, keys_row, segment_row):
    scores = jnp.einsum("qhe,khe->hqk", queries, keys_row, preferred_element_type=jnp.float32)
    matched = (segment_row[:, None] == segment_row[None, :])[None]
    return jnp.where(matched, scores, MASKED)


def attend_forward(arrays):
    queries, keys_row, values_row, segment_row = arrays
    scores = masked_scores(queries, keys_row, segment_row)
    highest = jnp.max(scores, axis=-1, keepdims=True)
    exponent = jnp.exp(scores - highest)
    summed = jnp.sum(exponent, axis=-1, keepdims=True)
    attention = (exponent / summed).astype(jnp.bfloat16)
    context = jnp.einsum("hqk,khe->qhe", attention, values_row, preferred_element_type=jnp.float32)
    return (context, (highest + jnp.log(summed))[..., 0])


def attend_backward(arrays):
    queries, keys_row, values_row, segment_row, log_total, context_grad = arrays
    scores = masked_scores(queries, keys_row, segment_row)
    attention = jnp.exp(scores - log_total[..., None])
    attention_grad = jnp.einsum(
        "qhe,khe->hqk", context_grad, values_row, preferred_element_type=jnp.float32
    )
    score_grad = attention * (
        attention_grad - jnp.sum(attention_grad * attention, axis=-1, keepdims=True)
    )
    score_low = score_grad.astype(jnp.bfloat16)
    query_grad = jnp.einsum("hqk,khe->qhe", score_low, keys_row, preferred_element_type=jnp.float32)
    key_grad = jnp.einsum("hqk,qhe->khe", score_low, queries, preferred_element_type=jnp.float32)
    value_grad = jnp.einsum(
        "hqk,qhe->khe",
        attention.astype(jnp.bfloat16),
        context_grad,
        preferred_element_type=jnp.float32,
    )
    return (query_grad, key_grad, value_grad)


def per_device(
    frames,
    segment_ids,
    out_grad,
    blocks,
    small_params,
    owners,
    left_bases,
    right_bases,
    block_first,
    block_second,
    small_first,
    small_second,
):
    rows_here = frames.shape[0]
    tokens = rows_here * LENGTH
    n_blocks = blocks.shape[0]
    rows_own = blocks.shape[1]
    per_in = FF // D
    base_attn = 2 * per_in
    base_last = base_attn + 7
    scale_head = HEAD ** (-0.5)
    count_all = tokens * lax.axis_size(("dp", "fsdp"))
    weights = lax.all_gather(blocks.astype(jnp.bfloat16), "fsdp", axis=1, tiled=True)
    weight_in1 = weights[0:per_in]
    weight_out1 = weights[per_in:base_attn]
    weight_attn = weights[base_attn : base_attn + 3]
    weight_proj = weights[base_attn + 3]
    weight_point = weights[base_attn + 4 : base_attn + 6]
    weight_back = weights[base_attn + 6]
    weight_in2 = weights[base_last : base_last + per_in]
    weight_out2 = weights[base_last + per_in : base_last + 2 * per_in]
    gains = small_params[0:5]
    shifts = small_params[5:10]
    bn_gain = small_params[10]
    bn_shift = small_params[11]
    kernel_taps = small_params[12 : 12 + KERNEL]
    start_x = frames.astype(jnp.float32).reshape(tokens, D)
    first_x, first_saved = feed_forward(start_x, gains[0], shifts[0], weight_in1, weight_out1)
    normed, attn_pullback = jax.vjp(norm_apply, first_x, gains[1], shifts[1])
    attn_low = normed.astype(jnp.bfloat16)
    projected = jnp.einsum("td,jdh->tjh", attn_low, weight_attn, preferred_element_type=jnp.float32)
    split_shape = (rows_here, LENGTH, HEADS, HEAD)
    queries = (projected[:, 0] * scale_head).astype(jnp.bfloat16).reshape(split_shape)
    keys_all = projected[:, 1].astype(jnp.bfloat16).reshape(split_shape)
    values_all = projected[:, 2].astype(jnp.bfloat16).reshape(split_shape)
    context, log_total = lax.map(attend_forward, (queries, keys_all, values_all, segment_ids))
    context_low = context.reshape(tokens, D).astype(jnp.bfloat16)
    second_x = first_x + jnp.dot(context_low, weight_proj, preferred_element_type=jnp.float32)
    normed, conv_pullback = jax.vjp(norm_apply, second_x, gains[2], shifts[2])
    conv_low = normed.astype(jnp.bfloat16)
    before = jnp.einsum("td,jdh->tjh", conv_low, weight_point, preferred_element_type=jnp.float32)
    convolved, gated_pullback = jax.vjp(
        lambda pre_in, taps_in: gated_conv(pre_in, taps_in, segment_ids), before, kernel_taps
    )
    stat_sum, stat_square = lax.psum(
        (jnp.sum(convolved, axis=0), jnp.sum(convolved * convolved, axis=0)), ("dp", "fsdp")
    )
    average = stat_sum / count_all
    inverse_dev = lax.rsqrt(stat_square / count_all - average * average + EPS_NORM)
    standard = (convolved - average) * inverse_dev
    activated, bn_swish_pullback = jax.vjp(swish, standard * bn_gain + bn_shift)
    activated_low = activated.astype(jnp.bfloat16)
    third_x = second_x + jnp.dot(activated_low, weight_back, preferred_element_type=jnp.float32)
    fourth_x, last_saved = feed_forward(third_x, gains[3], shifts[3], weight_in2, weight_out2)
    layer_value, final_pullback = jax.vjp(norm_apply, fourth_x, gains[4], shifts[4])
    layer_out = layer_value.astype(jnp.bfloat16).reshape(rows_here, LENGTH, D)
    grad_x, final_gain, final_shift = final_pullback(
        out_grad.astype(jnp.float32).reshape(tokens, D)
    )
    grad_x, ffn2_gain, ffn2_shift, grad_in2, grad_out2 = feed_backward(
        grad_x, last_saved, weight_in2, weight_out2
    )
    branch_low = grad_x.astype(jnp.bfloat16)
    grad_back = jnp.einsum(
        "td,te->de", activated_low, branch_low, preferred_element_type=jnp.float32
    )
    acted_grad = jnp.einsum(
        "te,de->td", branch_low, weight_back, preferred_element_type=jnp.float32
    )
    (bn_grad,) = bn_swish_pullback(acted_grad)
    shift_sum, gain_sum = lax.psum(
        (jnp.sum(bn_grad, axis=0), jnp.sum(bn_grad * standard, axis=0)), ("dp", "fsdp")
    )
    conv_grad = (
        bn_gain
        * inverse_dev
        * (bn_grad - shift_sum / count_all - standard * (gain_sum / count_all))
    )
    before_grad, taps_grad = gated_pullback(conv_grad)
    before_low = before_grad.astype(jnp.bfloat16)
    grad_point = jnp.einsum("td,tjh->jdh", conv_low, before_low, preferred_element_type=jnp.float32)
    normed_grad = jnp.einsum(
        "tjh,jdh->td", before_low, weight_point, preferred_element_type=jnp.float32
    )
    part_x, conv_gain, conv_shift = conv_pullback(normed_grad)
    grad_x = grad_x + part_x
    branch_low = grad_x.astype(jnp.bfloat16)
    grad_proj = jnp.einsum("td,te->de", context_low, branch_low, preferred_element_type=jnp.float32)
    context_grad = jnp.einsum(
        "te,de->td", branch_low, weight_proj, preferred_element_type=jnp.float32
    )
    context_grad = context_grad.astype(jnp.bfloat16).reshape(split_shape)
    query_grad, key_grad, value_grad = lax.map(
        attend_backward, (queries, keys_all, values_all, segment_ids, log_total, context_grad)
    )
    stacked_low = jnp.stack(
        [
            query_grad.reshape(tokens, D) * scale_head,
            key_grad.reshape(tokens, D),
            value_grad.reshape(tokens, D),
        ],
        axis=1,
    ).astype(jnp.bfloat16)
    grad_attn = jnp.einsum("td,tjh->jdh", attn_low, stacked_low, preferred_element_type=jnp.float32)
    normed_grad = jnp.einsum(
        "tjh,jdh->td", stacked_low, weight_attn, preferred_element_type=jnp.float32
    )
    part_x, attn_gain, attn_shift = attn_pullback(normed_grad)
    grad_x = grad_x + part_x
    grad_x, ffn1_gain, ffn1_shift, grad_in1, grad_out1 = feed_backward(
        grad_x, first_saved, weight_in1, weight_out1
    )
    frames_grad = grad_x.reshape(rows_here, LENGTH, D)
    local_small = jnp.concatenate(
        [
            jnp.stack([ffn1_gain, attn_gain, conv_gain, ffn2_gain, final_gain]),
            jnp.stack([ffn1_shift, attn_shift, conv_shift, ffn2_shift, final_shift]),
            taps_grad,
        ],
        axis=0,
    )
    summed_small = lax.psum(local_small, ("dp", "fsdp"))
    small_grads = jnp.concatenate(
        [summed_small[0:10], gain_sum[None], shift_sum[None], summed_small[10:]], axis=0
    )
    grad_all = jnp.concatenate(
        [
            grad_in1,
            grad_out1,
            grad_attn,
            grad_proj[None],
            grad_point,
            grad_back[None],
            grad_in2,
            grad_out2,
        ],
        axis=0,
    )
    n_dp = lax.axis_size("dp")
    n_fsdp = lax.axis_size("fsdp")
    capacity = (n_blocks + n_dp - 1) // n_dp
    slot_block, slot_used = slot_tables(owners, n_dp, n_blocks)
    split_blocks = grad_all.reshape(n_blocks, n_fsdp, rows_own, D)
    shard_index = jnp.broadcast_to(jnp.arange(n_fsdp, dtype=jnp.int32)[None, :], (n_dp, n_fsdp))
    block_table = slot_block.reshape(n_dp, capacity)
    used_table = slot_used.reshape(n_dp, capacity).astype(jnp.float32)
    owned_list = []
    for slot_rank in range(capacity):
        rank_block = jnp.broadcast_to(block_table[:, slot_rank : slot_rank + 1], (n_dp, n_fsdp))
        rank_used = used_table[:, slot_rank][:, None, None, None]
        picked = split_blocks[rank_block, shard_index] * rank_used
        owned_list.append(
            lax.psum_scatter(
                picked.reshape(n_dp * n_fsdp, rows_own, D),
                ("dp", "fsdp"),
                scatter_dimension=0,
                tiled=True,
            )
        )
    owned = jnp.concatenate(owned_list, axis=0)
    my_slots = lax.axis_index("dp") * capacity + jnp.arange(capacity, dtype=jnp.int32)
    my_blocks = jnp.take(slot_block, my_slots)
    my_used = jnp.take(slot_used, my_slots).astype(jnp.float32)[:, None, None]
    masters = jnp.take(blocks, my_blocks, axis=0)
    first_list = []
    second_list = []
    weight_list = []
    for slot_here in range(capacity):
        left_rows = left_bases[slot_here]
        right_basis = right_bases[slot_here]
        product = jnp.dot(owned[slot_here], right_basis, precision=HIGHEST)

        def rotate_term(start, count, left_rows=left_rows, product=product):
            return jnp.einsum("rc,rd->cd", left_rows, product, precision=HIGHEST)

        rotated = lax.psum_scatter(
            rotate_term(jnp.int32(0), lax.axis_size("fsdp") * rows_own).astype(jnp.bfloat16),
            "fsdp",
            scatter_dimension=0,
            tiled=True,
        ).astype(jnp.float32)
        first_step = BETA_DECAY * block_first[slot_here] + (1.0 - BETA_DECAY) * rotated
        second_step = BETA_DECAY * block_second[slot_here] + (1.0 - BETA_DECAY) * rotated * rotated
        direction = first_step / (jnp.sqrt(second_step) + EPS_ADAM)

        def back_term(carry, piece, start, left_rows=left_rows):
            return carry + jnp.dot(left_rows, piece, precision=HIGHEST)

        mixed = back_term(
            jnp.zeros((rows_own, D), jnp.float32),
            lax.all_gather(direction.astype(jnp.bfloat16), "fsdp", axis=0, tiled=True).astype(
                jnp.float32
            ),
            jnp.int32(0),
        )
        update = jnp.einsum("rd,ed->re", mixed, right_basis, precision=HIGHEST)
        master = masters[slot_here]
        first_list.append(first_step)
        second_list.append(second_step)
        weight_list.append(master - LEARN_RATE * (update + DECAY_WEIGHT * master))
    first_new = jnp.stack(first_list) * my_used
    second_new = jnp.stack(second_list) * my_used
    block_weights = jnp.stack(weight_list) * my_used
    small_first_new = BETA_DECAY * small_first + (1.0 - BETA_DECAY) * small_grads
    small_second_new = BETA_DECAY * small_second + (1.0 - BETA_DECAY) * small_grads * small_grads
    small_weights = small_params - SMALL_RATE * small_first_new / (
        jnp.sqrt(small_second_new) + EPS_ADAM
    )
    return (
        layer_out,
        frames_grad,
        owned,
        first_new,
        second_new,
        block_weights,
        small_grads,
        small_weights,
        small_first_new,
        small_second_new,
    )


def solution(mesh):
    placed = (
        P(("dp", "fsdp"), None, None),
        P(("dp", "fsdp"), None),
        P(("dp", "fsdp"), None, None),
        P(None, "fsdp", None),
        P(),
        P(),
        P("dp", "fsdp", None),
        P("dp", None, None),
        P("dp", "fsdp", None),
        P("dp", "fsdp", None),
        P(),
        P(),
    )
    return jax.shard_map(
        per_device,
        mesh=mesh,
        in_specs=placed,
        out_specs=(
            P(("dp", "fsdp"), None, None),
            P(("dp", "fsdp"), None, None),
            P("dp", "fsdp", None),
            P("dp", "fsdp", None),
            P("dp", "fsdp", None),
            P("dp", "fsdp", None),
            P(),
            P(),
            P(),
            P(),
        ),
        check_vma=False,
    )
```

profile of v0, /device:TPU:0, one launch (start us, length us, event | category | flops | bytes accessed | tf_op | source)
XLA Modules:
  0.0 3255.9 jit_solution(8151860871585922635)
XLA Ops:
  7.2 13.1 convert_element_type.161
  26.6 416.2 %all-gather.5.cloned.1.call-done = bf16[23,1024,1024]{2,1,0:T(8,128)(2,1)} async-done(((bf16[23,256,1024]{2,1,0:T(8,128)(2,1)}), bf16[23,1024,1024]{2,1,0:T(8,128)(2,1)}) %all-gather.5.cloned.1.call-update) | async-done | bytes 48234512 | tf_op jit(solution)/shard_map/all_gather | solution.py:163
  442.7 7.2 fusion.21
  450.0 11.1 fusion.245
  461.6 8.3 fusion.246
  487.2 5.0 fusion.54
  496.7 39.8 %all-reduce.15 = (f32[1024]{0:T(1024)S(1)}, f32[1024]{0:T(1024)S(1)}) all-reduce(f32[1024]{0:T(1024)S(1)} %fusion.96, f32[1024]{0:T(1024)S(1)} %get-tuple-element.147), channel_id=1, replica_groups=mesh['dp'=8,'fsdp'=4] {'dp','fsdp'}, use_global_device_ids=true, to_apply=%region_11.12 | all-reduce | flops 2048 | bytes 16384 | tf_op jit(solution)/shard_map/psum | solution.py:195
  536.5 3.8 fusion.248
  540.7 7.5 fusion.13
  548.2 11.1 fusion.249
  563.9 10.5 fusion.2
  574.4 9.6 fusion.94
  585.1 5.8 fusion.234
  590.9 41.3 %all-reduce.14 = (f32[1024]{0:T(1024)S(1)}, f32[1024]{0:T(1024)S(1)}) all-reduce(f32[1024]{0:T(1024)S(1)} %get-tuple-element.112, f32[1024]{0:T(1024)S(1)} %get-tuple-element.111), channel_id=1, replica_groups=mesh['dp'=8,'fsdp'=4] {'dp','fsdp'}, use_global_device_ids=true, to_apply=%region_23.24 | all-reduce | flops 2048 | bytes 16384 | tf_op jit(solution)/shard_map/psum | solution.py:221
  632.2 4.9 fusion.87
  645.6 5.6 fusion.93
  653.1 4.7 fusion.108
  660.1 6.9 fusion.110
  667.0 5.1 multiply_reduce_fusion
  680.8 6.0 fusion.200
  686.9 10.9 fusion.221
  697.8 8.5 fusion.201
  712.7 11.0 fusion.149
  723.7 7.4 fusion.92
  733.5 8.3 fusion.233
  741.9 10.1 fusion.5
  752.0 7.1 fusion.228
  759.2 6.3 constant_dynamic-update-slice_fusion.5
  766.9 12.2 constant_dynamic-update-slice_fusion.4
  779.1 11.9 constant_dynamic-update-slice_fusion.3
  794.2 9.5 constant_dynamic-update-slice_fusion.2
  807.0 8.5 constant_dynamic-update-slice_fusion.1
  817.3 6.0 constant_dynamic-update-slice_fusion
  823.4 22.9 gather_fusion.2
  846.3 24.4 broadcast_multiply_fusion
  871.6 24.7 gather_fusion.1
  896.3 24.6 broadcast_multiply_fusion.1
  921.9 23.3 gather_fusion
  945.1 24.4 broadcast_multiply_fusion.2
  969.7 608.8 %reduce-scatter.11.cloned.1.call-done = f32[1,256,1024]{2,1,0:T(8,128)} async-done(((f32[32,256,1024]{2,1,0:T(8,128)}), f32[1,256,1024]{2,1,0:T(8,128)}) %reduce-scatter.11.cloned.1.call-update) | async-done | bytes 1048592 | tf_op jit(solution)/shard_map/reduce_scatter | solution.py:303
  1578.5 6.2 fusion.32
  1584.7 4.7 convert_bitcast_fusion.2
  1589.5 699.3 %reduce-scatter.9.cloned.1.call-done = f32[1,256,1024]{2,1,0:T(8,128)} async-done(((f32[32,256,1024]{2,1,0:T(8,128)}), f32[1,256,1024]{2,1,0:T(8,128)}) %reduce-scatter.9.cloned.1.call-update) | async-done | bytes 1048592 | tf_op jit(solution)/shard_map/reduce_scatter | solution.py:303
  2288.7 6.0 fusion.36
  2294.7 4.7 convert_bitcast_fusion.3
  2299.5 699.3 %reduce-scatter.7.cloned.1.call-done = f32[1,256,1024]{2,1,0:T(8,128)} async-done(((f32[32,256,1024]{2,1,0:T(8,128)}), f32[1,256,1024]{2,1,0:T(8,128)}) %reduce-scatter.7.cloned.1.call-update) | async-done | bytes 1048592 | tf_op jit(solution)/shard_map/reduce_scatter | solution.py:303
  2998.8 6.0 fusion.40
  3004.8 4.9 convert_bitcast_fusion.4
  3014.0 3.7 fusion.242
  3018.1 19.6 reduce-scatter.17.cloned.1.call-done
  3041.9 10.6 gather_fusion.3
  3065.3 11.2 reduce-scatter.15.cloned.1.call-done
  3086.8 9.5 bitcast_reduce_fusion
  3096.3 18.4 reduce-scatter.13.cloned.1.call-done
  3120.6 39.9 %psum.39 = f32[15,1024]{1,0:T(8,128)S(1)} all-reduce(f32[15,1024]{1,0:T(8,128)S(1)} %concatenate.45), channel_id=1, replica_groups=mesh['dp'=8,'fsdp'=4] {'dp','fsdp'}, use_global_device_ids=true, to_apply=%region_55.57 | all-reduce | flops 15360 | bytes 122880 | tf_op jit(solution)/shard_map/psum | solution.py:272
  3162.3 4.6 add_bitcast_fusion
  3168.8 4.7 fusion.160
  3173.5 15.9 all-gather.9.cloned.1.call-done
  3189.4 3.8 fusion.164
  3193.2 6.6 fusion.134
  3199.8 6.7 fusion.140
  3206.5 20.1 all-gather.7.cloned.1.call-done
  3226.6 3.8 fusion.168
  3230.5 5.5 fusion.146
  (423 shorter events, 129.7 us)
Async XLA Ops:
  7.2 435.5 %all-gather.5.cloned.1.call-start = ((), (), s32[]{:S(2)}) async-start(), calls=%async_computation.6 | async-start | bytes 60293120 | tf_op jit(solution)/shard_map/all_gather | solution.py:163
  20.3 1558.2 %reduce-scatter.11.cloned.1.call-start = ((), (), s32[]{:S(2)}) async-start(), calls=%async_computation.9 | async-start | bytes 34603008 | tf_op jit(solution)/shard_map/reduce_scatter | solution.py:303
  21.2 428.7 %copy-start = (s32[24]{0:T(128)}, s32[24]{0:T(128)S(1)}, u32[]{:S(2)}) copy-start(s32[24]{0:T(128)S(1)} %get-tuple-element.124) | copy-start | bytes 292
  21.3 428.7 %copy-start.2 = (s32[24]{0:T(128)}, s32[24]{0:T(128)S(1)}, u32[]{:S(2)}) copy-start(s32[24]{0:T(128)S(1)} %get-tuple-element.123) | copy-start | bytes 292
  24.9 612.2 %copy-start.101 = (pred[512]{0:T(512)(128)(4,1)}, pred[512]{0:T(512)(128)(4,1)S(1)}, u32[]{:S(2)}) copy-start(pred[512]{0:T(512)(128)(4,1)S(1)} %get-tuple-element.119) | copy-start | bytes 1540
  25.0 612.2 %copy-start.103 = (pred[512]{0:T(512)(128)(4,1)}, pred[512]{0:T(512)(128)(4,1)S(1)}, u32[]{:S(2)}) copy-start(pred[512]{0:T(512)(128)(4,1)S(1)} %get-tuple-element.120) | copy-start | bytes 1540
  25.0 612.2 %copy-start.105 = (pred[512]{0:T(512)(128)(4,1)}, pred[512]{0:T(512)(128)(4,1)S(1)}, u32[]{:S(2)}) copy-start(pred[512]{0:T(512)(128)(4,1)S(1)} %get-tuple-element.121) | copy-start | bytes 1540
  25.0 612.2 %copy-start.107 = (pred[512]{0:T(512)(128)(4,1)}, pred[512]{0:T(512)(128)(4,1)S(1)}, u32[]{:S(2)}) copy-start(pred[512]{0:T(512)(128)(4,1)S(1)} %get-tuple-element.122) | copy-start | bytes 1540
  25.2 424.7 %copy-start.73 = (f32[512]{0:T(512)}, f32[512]{0:T(512)S(1)}, u32[]{:S(2)}) copy-start(f32[512]{0:T(512)S(1)} %broadcast_multiply_fusion.10) | copy-start | bytes 6148
  26.2 423.7 %copy-start.76 = (f32[512]{0:T(512)}, f32[512]{0:T(512)S(1)}, u32[]{:S(2)}) copy-start(f32[512]{0:T(512)S(1)} %fusion.207) | copy-start | bytes 6148
  26.3 423.7 %copy-start.70 = (f32[1,1024]{1,0:T(1,128)}, f32[1,1024]{1,0:T(1,128)S(1)}, u32[]{:S(2)}) copy-start(f32[1,1024]{1,0:T(1,128)S(1)} %get-tuple-element.188) | copy-start | bytes 12292
  26.3 423.7 %copy-start.89 = (f32[1,1024]{1,0:T(1,128)}, f32[1,1024]{1,0:T(1,128)S(1)}, u32[]{:S(2)}) copy-start(f32[1,1024]{1,0:T(1,128)S(1)} %get-tuple-element.187) | copy-start | bytes 12292
  26.3 435.2 %copy-start.97 = (f32[1,1024]{1,0:T(1,128)}, f32[1,1024]{1,0:T(1,128)S(1)}, u32[]{:S(2)}) copy-start(f32[1,1024]{1,0:T(1,128)S(1)} %get-tuple-element.186) | copy-start | bytes 12292
  26.3 435.2 %copy-start.115 = (f32[1,1024]{1,0:T(1,128)}, f32[1,1024]{1,0:T(1,128)S(1)}, u32[]{:S(2)}) copy-start(f32[1,1024]{1,0:T(1,128)S(1)} %get-tuple-element.185) | copy-start | bytes 12292
  450.0 11.1 copy-start.122
  540.3 43.8 %copy-start.20 = (f32[512,1024]{1,0:T(8,128)}, f32[512,1024]{1,0:T(8,128)S(1)}, u32[]{:S(2)}) copy-start(f32[512,1024]{1,0:T(8,128)S(1)} %get-tuple-element.205) | copy-start | bytes 6291460
  548.2 11.2 copy-start.123
  563.9 20.9 copy-start.37
  653.1 137.9 %copy-start.7 = (f32[512,1024]{1,0:T(8,128)}, f32[512,1024]{1,0:T(8,128)S(1)}, u32[]{:S(2)}) copy-start(f32[512,1024]{1,0:T(8,128)S(1)} %add_add_fusion.6) | copy-start | bytes 6291460
  660.1 12.0 slice-start
  680.8 17.0 slice-start.12
  686.9 11.0 copy-start.38
  686.9 11.0 slice-start.13
  712.6 11.1 copy-start.33
  712.6 11.1 copy-start.64
  712.6 11.1 copy-start.65
  712.7 20.9 slice-start.10
  723.7 9.8 slice-start.11
  741.8 10.2 copy-start.10
  741.8 10.2 copy-start.71
  741.8 10.2 copy-start.74
  741.8 10.2 copy-start.77
  741.8 10.2 copy-start.90
  779.1 11.9 copy-start.62
  791.0 15.9 slice-start.2
  794.2 12.7 slice-start.3
  794.2 12.7 slice-start.4
  794.2 12.7 slice-start.5
  803.7 11.7 slice-start.6
  807.0 10.3 slice-start.9
  823.4 22.9 copy-start.117
  870.7 1418.0 %reduce-scatter.9.cloned.1.call-start = ((), (), s32[]{:S(2)}) async-start(), calls=%async_computation.8 | async-start | bytes 34603008 | tf_op jit(solution)/shard_map/reduce_scatter | solution.py:303
  920.9 2077.9 %reduce-scatter.7.cloned.1.call-start = ((), (), s32[]{:S(2)}) async-start(), calls=%async_computation.7 | async-start | bytes 34603008 | tf_op jit(solution)/shard_map/reduce_scatter | solution.py:303
  969.6 615.0 %copy-start.27 = (f32[3,256,1024]{2,1,0:T(8,128)S(1)}, f32[3,256,1024]{2,1,0:T(8,128)}, u32[]{:S(2)}) copy-start(f32[3,256,1024]{2,1,0:T(8,128)} %param.20) | copy-start | bytes 9437188
  969.6 2068.0 %reduce-scatter.17.cloned.1.call-start = ((), (), s32[]{:S(2)}) async-start(), calls=%async_computation.12 | async-start | bytes 2621440 | tf_op jit(solution)/shard_map/reduce_scatter | solution.py:326
  1589.4 1487.1 %reduce-scatter.15.cloned.1.call-start = ((), (), s32[]{:S(2)}) async-start(), calls=%async_computation.11 | async-start | bytes 2621440 | tf_op jit(solution)/shard_map/reduce_scatter | solution.py:326
  2299.5 815.2 %reduce-scatter.13.cloned.1.call-start = ((), (), s32[]{:S(2)}) async-start(), calls=%async_computation.10 | async-start | bytes 2621440 | tf_op jit(solution)/shard_map/reduce_scatter | solution.py:326
  3009.7 159.1 %all-gather.11.cloned.1.call-start = ((), (), s32[]{:S(2)}) async-start(), calls=%async_computation.15 | async-start | bytes 2621440 | tf_op jit(solution)/shard_map/all_gather | solution.py:341
  3018.0 22.6 copy-start.1
  3018.1 23.2 copy-start.3
  3040.5 148.8 %all-gather.9.cloned.1.call-start = ((), (), s32[]{:S(2)}) async-start(), calls=%async_computation.14 | async-start | bytes 2621440 | tf_op jit(solution)/shard_map/all_gather | solution.py:341
  3080.0 146.6 %all-gather.7.cloned.1.call-start = ((), (), s32[]{:S(2)}) async-start(), calls=%async_computation.13 | async-start | bytes 2621440 | tf_op jit(solution)/shard_map/all_gather | solution.py:341
  3086.7 27.9 copy-start.41
  3086.8 27.9 copy-start.42
  3096.3 21.4 copy-start.95
  3096.3 21.4 copy-start.81
  3096.3 21.4 copy-start.78
  3117.5 43.0 %copy-start.68 = (f32[17,1024]{1,0:T(8,128)S(1)}, f32[17,1024]{1,0:T(8,128)}, u32[]{:S(2)}) copy-start(f32[17,1024]{1,0:T(8,128)} %param.18) | copy-start | bytes 208900
  3117.6 43.0 %copy-start.69 = (f32[17,1024]{1,0:T(8,128)S(1)}, f32[17,1024]{1,0:T(8,128)}, u32[]{:S(2)}) copy-start(f32[17,1024]{1,0:T(8,128)} %param.24) | copy-start | bytes 208900
  3117.6 43.0 %copy-start.92 = (f32[1024]{0:T(1024)S(1)}, f32[1024]{0:T(1024)}, u32[]{:S(2)}) copy-start(f32[1024]{0:T(1024)} %copy-done.91) | copy-start | bytes 12292
  3117.6 43.0 %copy-start.94 = (f32[1024]{0:T(1024)S(1)}, f32[1024]{0:T(1024)}, u32[]{:S(2)}) copy-start(f32[1024]{0:T(1024)} %copy-done.93) | copy-start | bytes 12292
  3117.7 44.6 %copy-start.8 = (f32[512,1024]{1,0:T(8,128)S(1)}, f32[512,1024]{1,0:T(8,128)}, u32[]{:S(2)}) copy-start(f32[512,1024]{1,0:T(8,128)} %copy-done.7) | copy-start | bytes 6291460
  3117.7 44.6 %copy-start.87 = (f32[512]{0:T(512)S(1)}, f32[512]{0:T(512)}, u32[]{:S(2)}) copy-start(f32[512]{0:T(512)} %copy-done.86) | copy-start | bytes 6148
  3173.5 19.7 copy-start.26
  (84 other events, 366.6 us)
Sparse Core Ops, SparseCore 0:
  20.4 422.2 all-gather.4
  870.9 707.5 reduce-scatter.10
  1580.8 707.8 reduce-scatter.8
  2290.9 707.8 reduce-scatter.6
  3002.2 35.3 reduce-scatter.16
  3041.3 35.1 reduce-scatter.14
  3079.5 35.1 reduce-scatter.12
  3116.7 35.4 all-gather.10
  3154.2 35.1 all-gather.8
  3191.2 35.1 all-gather.6
where the time goes:
time: 3270 us; the launch traced here: 3260 us
  waiting for transfers between devices  2510 us (77%)
  matrix products  263 us (8%)
  local copies, waits for them, and re-layouts  205 us (6%)
  other arithmetic  142 us (4%)
  blocking collectives  121 us (4%)
    reduce_scatter x3, waiting for transfers between devices, per_device(): lax.psum_scatter(picked.reshape(n_dp * n_fsdp, rows_own, D), ('dp', 'fsdp...  2010 us
    all_gather x1, waiting for transfers between devices, per_device(): lax.all_gather(blocks.astype(jnp.bfloat16), 'fsdp', axis=1, tiled=True)  416 us
    unnamed x292, local copies, waits for them, and re-layouts  91.5 us
    mul x3, other arithmetic, per_device(): picked = split_blocks[rank_block, shard_index] * rank_used  73.4 us
    gather x3, local copies, waits for them, and re-layouts, per_device(): picked = split_blocks[rank_block, shard_index] * rank_used  70.9 us
  transfers between devices with their start and end apart: 10, of which 9 were waited for; matrix products, arithmetic and copies ran while one was open for 7% of the time, Pallas kernels for 0%

commit v1 on v0

v1 whole, which is shorter than its diff:
```python
import jax
import jax.numpy as jnp
from jax import lax
from jax.sharding import PartitionSpec as P

D = 1024
HEADS = 8
FF = 4096
KERNEL = 5
LENGTH = 512
HEAD = 128

EPS_NORM = 1e-05
EPS_ADAM = 1e-08
LEARN_RATE = 0.02
SMALL_RATE = 0.3
DECAY_WEIGHT = 0.01
BETA_DECAY = 0.5
MASKED = -1000000000.0
AXES = ("dp", "fsdp")
BF = jnp.bfloat16
F32 = jnp.float32


def bits_of(size):
    return [1 << k for k in range(size.bit_length() - 1)]


def swap(value, dp_mask, fsdp_mask):
    n_dp, n_fsdp = lax.axis_size("dp"), lax.axis_size("fsdp")
    pairs = [
        (d * n_fsdp + f, (d ^ dp_mask) * n_fsdp + (f ^ fsdp_mask))
        for d in range(n_dp)
        for f in range(n_fsdp)
    ]
    return lax.ppermute(value, AXES, pairs)


def total(value):
    for mask in bits_of(lax.axis_size("fsdp")):
        value = value + swap(value, 0, mask)
    for mask in bits_of(lax.axis_size("dp")):
        value = value + swap(value, mask, 0)
    return value


def after(value, *earlier):
    return lax.optimization_barrier((value, *earlier))[0]


def pick(value, axis, index):
    return lax.dynamic_index_in_dim(value, index, axis, keepdims=False)


def place(value, shape, starts):
    return value, shape, starts


def norm_apply(values, scale_row, shift_row):
    average = jnp.mean(values, axis=-1, keepdims=True)
    centered = values - average
    variance = jnp.mean(centered * centered, axis=-1, keepdims=True)
    return centered * lax.rsqrt(variance + EPS_NORM) * scale_row + shift_row


def swish(values):
    return values * jax.nn.sigmoid(values)


def depthwise(gated_rows, kernel_taps, segment_ids):
    length = gated_rows.shape[1]
    margin = KERNEL // 2
    padded = jnp.pad(gated_rows, ((0, 0), (margin, margin), (0, 0)))
    segment_pad = jnp.pad(segment_ids, ((0, 0), (margin, margin)), constant_values=-1)
    summed = jnp.zeros_like(gated_rows)
    for offset in range(KERNEL):
        matched = (segment_pad[:, offset : offset + length] == segment_ids)[:, :, None]
        summed = summed + kernel_taps[offset] * jnp.where(
            matched, padded[:, offset : offset + length], 0.0
        )
    return summed


def slot_tables(owners, groups, count_blocks):
    capacity = (count_blocks + groups - 1) // groups
    block_index = jnp.arange(count_blocks, dtype=jnp.int32)
    earlier = (owners[None, :] == owners[:, None]) & (block_index[None, :] < block_index[:, None])
    ranking = jnp.sum(earlier.astype(jnp.int32), axis=1)
    slot_of = owners * capacity + ranking
    return slot_of[None, :] == jnp.arange(capacity * groups, dtype=jnp.int32)[:, None]


def gated_conv(pre_a, pre_g, kernel_taps, segment_ids):
    rows_here = segment_ids.shape[0]
    gated_rows = pre_a * jax.nn.sigmoid(pre_g)
    shaped = gated_rows.reshape(rows_here, -1, gated_rows.shape[-1])
    return depthwise(shaped, kernel_taps, segment_ids).reshape(gated_rows.shape)


def masked_scores(queries, keys_row, segment_row):
    scores = jnp.einsum("qhe,khe->hqk", queries, keys_row, preferred_element_type=F32)
    matched = (segment_row[:, None] == segment_row[None, :])[None]
    return jnp.where(matched, scores, MASKED)


def attend_forward(arrays):
    queries, keys_row, values_row, segment_row = arrays
    scores = masked_scores(queries, keys_row, segment_row)
    highest = jnp.max(scores, axis=-1, keepdims=True)
    exponent = jnp.exp(scores - highest)
    summed = jnp.sum(exponent, axis=-1, keepdims=True)
    attention = (exponent / summed).astype(BF)
    context = jnp.einsum("hqk,khe->qhe", attention, values_row, preferred_element_type=F32)
    return (context, (highest + jnp.log(summed))[..., 0])


def attend_backward(arrays):
    queries, keys_row, values_row, segment_row, log_total, context_grad = arrays
    scores = masked_scores(queries, keys_row, segment_row)
    attention = jnp.exp(scores - log_total[..., None])
    attention_grad = jnp.einsum(
        "qhe,khe->hqk", context_grad, values_row, preferred_element_type=F32
    )
    score_grad = attention * (
        attention_grad - jnp.sum(attention_grad * attention, axis=-1, keepdims=True)
    )
    score_low = score_grad.astype(BF)
    query_grad = jnp.einsum("hqk,khe->qhe", score_low, keys_row, preferred_element_type=F32)
    key_grad = jnp.einsum("hqk,qhe->khe", score_low, queries, preferred_element_type=F32)
    value_grad = jnp.einsum(
        "hqk,qhe->khe", attention.astype(BF), context_grad, preferred_element_type=F32
    )
    return (query_grad, key_grad, value_grad)


def mm(left, right):
    return jnp.dot(left, right, preferred_element_type=F32)


def mm_t(left, right):
    return lax.dot_general(left, right, (((1,), (1,)), ((), ())), preferred_element_type=F32)


def t_mm(left, right):
    return lax.dot_general(left, right, (((0,), (0,)), ((), ())), preferred_element_type=F32)


class Gather:
    def __init__(self, blocks):
        self.blocks = blocks
        self.n_fsdp = lax.axis_size("fsdp")
        self.core = lax.axis_index("dp") % 2
        self.mine = lax.axis_index("fsdp")
        self.half = blocks.shape[1] // 2
        self.recent = []

    def chunk(self, low, high):
        count = high - low
        piece = self.blocks[low:high].reshape(count, 2, self.half, D).astype(BF)
        own = pick(piece, 1, self.core)
        if len(self.recent) >= 2:
            own = after(own, self.recent[-2])
        masks = bits_of(self.n_fsdp)
        if len(self.recent) % 2:
            masks = masks[::-1]
        pieces = {0: own}
        for mask in masks:
            for known, held in list(pieces.items()):
                pieces[known | mask] = swap(held, 0, mask)
            if mask == masks[0]:
                self.recent.append(pieces[mask])
        other = {0: pick(piece, 1, 1 - self.core)}
        for known, held in pieces.items():
            if known:
                other[known] = swap(held, 1, 0)
        full = jnp.zeros((count, self.n_fsdp, 2, self.half, D), BF)
        for known in pieces:
            at = self.mine ^ known
            for held, side in ((pieces[known], self.core), (other[known], 1 - self.core)):
                full = lax.dynamic_update_slice(full, held[:, None, None], (0, at, side, 0, 0))
        return full.reshape(count, D, D)


class Reduce:
    def __init__(self, rows_own):
        self.n_fsdp = lax.axis_size("fsdp")
        self.n_dp = lax.axis_size("dp")
        self.core = lax.axis_index("dp") % 2
        self.dp = lax.axis_index("dp")
        self.mine = lax.axis_index("fsdp")
        self.half = rows_own // 2
        self.count = 0

    def group(self, left, right):
        tokens = left.shape[0]
        wide = left.shape[1] // D
        tall = right.shape[1] // D
        split = left.reshape(tokens, wide, self.n_fsdp, 2, self.half)
        sides = []
        for side in (1 - self.core, self.core):
            sides.append(pick(split, 3, side).reshape(tokens, -1))
        away = t_mm(sides[0], right).astype(BF)
        arrived = swap(away, 1, 0)
        held = (t_mm(sides[1], right) + arrived.astype(F32)).astype(BF)
        held = held.reshape(wide, self.n_fsdp, self.half, tall, D)
        masks = bits_of(self.n_fsdp)
        order = masks[::-1] if self.count % 2 else masks
        self.count += 1
        left_masks = list(masks)
        for mask in order:
            place_at = left_masks.index(mask)
            below = 1 << place_at
            shape = held.shape
            parted = held.reshape(shape[0], shape[1] // (2 * below), 2, below, *shape[2:])
            bit = (self.mine // mask) % 2
            arrived = swap(pick(parted, 2, 1 - bit), 0, mask)
            kept = pick(parted, 2, bit)
            held = (kept.astype(F32) + arrived.astype(F32)).astype(BF)
            held = held.reshape(shape[0], shape[1] // 2, *shape[2:])
            left_masks.remove(mask)
        held = held.reshape(wide, self.half, tall, D)
        for mask in bits_of(self.n_dp)[1:]:
            shape = held.shape
            parted = held.reshape(shape[0], 2, shape[1] // 2, *shape[2:])
            bit = (self.dp // mask) % 2
            arrived = swap(pick(parted, 1, 1 - bit), mask, 0)
            held = (pick(parted, 1, bit).astype(F32) + arrived.astype(F32)).astype(BF)
        if tall > 1:
            return jnp.moveaxis(held[0], 1, 0)
        return held[:, :, 0]


def feed_forward(hidden, scale_row, shift_row, weights_in, weights_out):
    normed, norm_pullback = jax.vjp(norm_apply, hidden, scale_row, shift_row)
    normed_low = normed.astype(BF)
    lifted, acted = [], []
    for part in weights_in:
        up = jnp.einsum("td,jdh->tjh", normed_low, part, preferred_element_type=F32)
        up = up.reshape(up.shape[0], -1)
        lifted.append(up.astype(BF))
        acted.append(swish(up).astype(BF))
    result = sum(mm(s, part.reshape(-1, D)) for s, part in zip(acted, weights_out))
    return hidden + 0.5 * result, (norm_pullback, normed_low, lifted, acted)


def feed_backward(gradient, saved, weights_in, weights_out, reduce):
    norm_pullback, normed_low, lifted, acted = saved
    result_low = (0.5 * gradient).astype(BF)
    out_grads, in_grads, normed_grad = [], [], 0.0
    for up, s, part_in, part_out in zip(lifted, acted, weights_in, weights_out):
        out_grads.append(reduce.group(s, result_low))
        acted_grad = mm_t(result_low, part_out.reshape(-1, D))
        up = up.astype(F32)
        gate = jax.nn.sigmoid(up)
        low = (acted_grad * (gate * (1.0 + up * (1.0 - gate)))).astype(BF)
        in_grads.append(reduce.group(normed_low, low))
        low = low.reshape(low.shape[0], -1, D)
        normed_grad = normed_grad + jnp.einsum(
            "tjh,jdh->td", low, part_in, preferred_element_type=F32
        )
    hidden_grad, scale_grad, shift_grad = norm_pullback(normed_grad)
    return gradient + hidden_grad, scale_grad, shift_grad, in_grads, out_grads


def per_device(
    frames,
    segment_ids,
    out_grad,
    blocks,
    small_params,
    owners,
    left_bases,
    right_bases,
    block_first,
    block_second,
    small_first,
    small_second,
):
    rows_here = frames.shape[0]
    tokens = rows_here * LENGTH
    n_blocks = blocks.shape[0]
    rows_own = blocks.shape[1]
    scale_head = HEAD ** (-0.5)
    n_dp = lax.axis_size("dp")
    n_fsdp = lax.axis_size("fsdp")
    mine = lax.axis_index("fsdp")
    count_all = tokens * n_dp * n_fsdp
    gather = Gather(blocks)
    reduce = Reduce(rows_own)
    w_in1 = [gather.chunk(0, 2), gather.chunk(2, 4)]
    w_out1 = [gather.chunk(4, 6), gather.chunk(6, 8)]
    w_qk = gather.chunk(8, 10)
    w_vo = gather.chunk(10, 12)
    w_point = gather.chunk(12, 14)
    w_back = gather.chunk(14, 15)[0]
    w_in2 = [gather.chunk(15, 17), gather.chunk(17, 19)]
    w_out2 = [gather.chunk(19, 21), gather.chunk(21, 23)]
    gains = small_params[0:5]
    shifts = small_params[5:10]
    bn_gain = small_params[10]
    bn_shift = small_params[11]
    kernel_taps = small_params[12 : 12 + KERNEL]

    start_x = frames.astype(F32).reshape(tokens, D)
    first_x, first_saved = feed_forward(start_x, gains[0], shifts[0], w_in1, w_out1)
    normed, attn_pullback = jax.vjp(norm_apply, first_x, gains[1], shifts[1])
    attn_low = normed.astype(BF)
    split_shape = (rows_here, LENGTH, HEADS, HEAD)
    queries = (mm(attn_low, w_qk[0]) * scale_head).astype(BF).reshape(split_shape)
    keys_all = mm(attn_low, w_qk[1]).astype(BF).reshape(split_shape)
    values_all = mm(attn_low, w_vo[0]).astype(BF).reshape(split_shape)
    context, log_total = lax.map(attend_forward, (queries, keys_all, values_all, segment_ids))
    context_low = context.reshape(tokens, D).astype(BF)
    second_x = first_x + mm(context_low, w_vo[1])
    normed, conv_pullback = jax.vjp(norm_apply, second_x, gains[2], shifts[2])
    conv_low = normed.astype(BF)
    convolved, gated_pullback = jax.vjp(
        lambda pre_a, pre_g, taps_in: gated_conv(pre_a, pre_g, taps_in, segment_ids),
        mm(conv_low, w_point[0]),
        mm(conv_low, w_point[1]),
        kernel_taps,
    )
    stats = total(
        jnp.stack([jnp.sum(convolved, axis=0), jnp.sum(convolved * convolved, axis=0)])
    )
    average = stats[0] / count_all
    inverse_dev = lax.rsqrt(stats[1] / count_all - average * average + EPS_NORM)
    standard = (convolved - average) * inverse_dev
    activated, bn_swish_pullback = jax.vjp(swish, standard * bn_gain + bn_shift)
    activated_low = activated.astype(BF)
    third_x = second_x + mm(activated_low, w_back)
    fourth_x, last_saved = feed_forward(third_x, gains[3], shifts[3], w_in2, w_out2)
    layer_value, final_pullback = jax.vjp(norm_apply, fourth_x, gains[4], shifts[4])
    layer_out = layer_value.astype(BF).reshape(rows_here, LENGTH, D)

    grad_x, final_gain, final_shift = final_pullback(out_grad.astype(F32).reshape(tokens, D))
    grad_x, ffn2_gain, ffn2_shift, grad_in2, grad_out2 = feed_backward(
        grad_x, last_saved, w_in2, w_out2, reduce
    )
    branch_low = grad_x.astype(BF)
    grad_back = reduce.group(activated_low, branch_low)
    (bn_grad,) = bn_swish_pullback(mm_t(branch_low, w_back))
    sums = total(jnp.stack([jnp.sum(bn_grad, axis=0), jnp.sum(bn_grad * standard, axis=0)]))
    shift_sum, gain_sum = sums[0], sums[1]
    conv_grad = (
        bn_gain
        * inverse_dev
        * (bn_grad - shift_sum / count_all - standard * (gain_sum / count_all))
    )
    grad_a, grad_g, taps_grad = gated_pullback(conv_grad)
    grad_a, grad_g = grad_a.astype(BF), grad_g.astype(BF)
    grad_point = reduce.group(conv_low, jnp.concatenate([grad_a, grad_g], axis=1))
    part_x, conv_gain, conv_shift = conv_pullback(
        mm_t(grad_a, w_point[0]) + mm_t(grad_g, w_point[1])
    )
    grad_x = grad_x + part_x
    branch_low = grad_x.astype(BF)
    grad_proj = reduce.group(context_low, branch_low)
    context_grad = mm_t(branch_low, w_vo[1]).astype(BF).reshape(split_shape)
    query_grad, key_grad, value_grad = lax.map(
        attend_backward, (queries, keys_all, values_all, segment_ids, log_total, context_grad)
    )
    query_low = (query_grad.reshape(tokens, D) * scale_head).astype(BF)
    key_low = key_grad.reshape(tokens, D).astype(BF)
    value_low = value_grad.reshape(tokens, D).astype(BF)
    grad_attn = reduce.group(attn_low, jnp.concatenate([query_low, key_low, value_low], axis=1))
    part_x, attn_gain, attn_shift = attn_pullback(
        mm_t(query_low, w_qk[0]) + mm_t(key_low, w_qk[1]) + mm_t(value_low, w_vo[0])
    )
    grad_x = grad_x + part_x
    grad_x, ffn1_gain, ffn1_shift, grad_in1, grad_out1 = feed_backward(
        grad_x, first_saved, w_in1, w_out1, reduce
    )
    frames_grad = grad_x.reshape(rows_here, LENGTH, D)
    local_small = jnp.concatenate(
        [
            jnp.stack([ffn1_gain, attn_gain, conv_gain, ffn2_gain, final_gain]),
            jnp.stack([ffn1_shift, attn_shift, conv_shift, ffn2_shift, final_shift]),
            taps_grad,
        ],
        axis=0,
    )
    summed_small = total(local_small)
    small_grads = jnp.concatenate(
        [summed_small[0:10], gain_sum[None], shift_sum[None], summed_small[10:]], axis=0
    )

    parts = jnp.concatenate(
        [
            *grad_in1,
            *grad_out1,
            grad_attn,
            grad_proj,
            grad_point,
            grad_back,
            *grad_in2,
            *grad_out2,
        ],
        axis=0,
    )
    capacity = (n_blocks + n_dp - 1) // n_dp
    matches = slot_tables(owners, n_dp, n_blocks)
    piece = parts.shape[1]
    sent = mm(matches.astype(BF), parts.reshape(n_blocks, -1)).astype(BF)
    sent = sent.reshape(n_dp, capacity * piece, D)
    came = lax.all_to_all(sent, "dp", 0, 0, tiled=False)
    n_bits = n_dp.bit_length() - 1
    came = came.reshape(*([2] * n_bits), capacity, piece, D)
    came = came.transpose(n_bits, *range(n_bits - 1, -1, -1), n_bits + 1, n_bits + 2)
    owned_low = came.reshape(capacity, rows_own, D)
    owned = owned_low.astype(F32)

    dp_here = lax.axis_index("dp")
    my_match = lax.dynamic_slice_in_dim(
        matches.astype(jnp.int32), dp_here * capacity, capacity, axis=0
    )
    my_blocks = jnp.sum(my_match * jnp.arange(n_blocks, dtype=jnp.int32)[None], axis=1)
    my_used = jnp.sum(my_match, axis=1).astype(F32)
    first_list, second_list, weight_list = [], [], []
    masks = bits_of(n_fsdp)
    for slot in range(capacity):
        left_rows = left_bases[slot].astype(BF)
        right_basis = right_bases[slot].astype(BF)
        product = mm(owned_low[slot], right_basis).astype(BF)
        spread = t_mm(left_rows, product).astype(BF).reshape(n_fsdp, rows_own, D)
        halves = []
        for side, order in ((0, masks), (1, masks[::-1])):
            held = spread[:, :, side * (D // 2) : (side + 1) * (D // 2)]
            left_masks = list(masks)
            for mask in order:
                below = 1 << left_masks.index(mask)
                shape = held.shape
                parted = held.reshape(shape[0] // (2 * below), 2, below, *shape[1:])
                bit = (mine // mask) % 2
                arrived = swap(pick(parted, 1, 1 - bit), 0, mask)
                held = pick(parted, 1, bit).astype(F32) + arrived.astype(F32)
                held = held.reshape(shape[0] // 2, *shape[1:])
                left_masks.remove(mask)
                if left_masks:
                    held = held.astype(BF)
            halves.append(held[0])
        rotated = jnp.concatenate(halves, axis=1)
        first_step = BETA_DECAY * block_first[slot] + (1.0 - BETA_DECAY) * rotated
        second_step = BETA_DECAY * block_second[slot] + (1.0 - BETA_DECAY) * rotated * rotated
        direction = (first_step / (jnp.sqrt(second_step) + EPS_ADAM)).astype(BF)
        mixed = []
        left_split = left_rows.reshape(rows_own, n_fsdp, rows_own)
        for side, order in ((0, masks), (1, masks[::-1])):
            pieces = {0: direction[:, side * (D // 2) : (side + 1) * (D // 2)]}
            for mask in order:
                for known, held in list(pieces.items()):
                    pieces[known | mask] = swap(held, 0, mask)
            mixed.append(
                sum(mm(pick(left_split, 1, mine ^ known), held) for known, held in pieces.items())
            )
        mixed = jnp.concatenate(mixed, axis=1).astype(BF)
        update = mm_t(mixed, right_basis)
        master = pick(blocks, 0, my_blocks[slot])
        used = my_used[slot]
        first_list.append(first_step * used)
        second_list.append(second_step * used)
        weight_list.append((master - LEARN_RATE * (update + DECAY_WEIGHT * master)) * used)
    small_first_new = BETA_DECAY * small_first + (1.0 - BETA_DECAY) * small_grads
    small_second_new = BETA_DECAY * small_second + (1.0 - BETA_DECAY) * small_grads * small_grads
    small_weights = small_params - SMALL_RATE * small_first_new / (
        jnp.sqrt(small_second_new) + EPS_ADAM
    )
    return (
        layer_out,
        frames_grad,
        owned,
        jnp.stack(first_list),
        jnp.stack(second_list),
        jnp.stack(weight_list),
        small_grads,
        small_weights,
        small_first_new,
        small_second_new,
    )


def solution(mesh):
    placed = (
        P(("dp", "fsdp"), None, None),
        P(("dp", "fsdp"), None),
        P(("dp", "fsdp"), None, None),
        P(None, "fsdp", None),
        P(),
        P(),
        P("dp", "fsdp", None),
        P("dp", None, None),
        P("dp", "fsdp", None),
        P("dp", "fsdp", None),
        P(),
        P(),
    )
    return jax.shard_map(
        per_device,
        mesh=mesh,
        in_specs=placed,
        out_specs=(
            P(("dp", "fsdp"), None, None),
            P(("dp", "fsdp"), None, None),
            P("dp", "fsdp", None),
            P("dp", "fsdp", None),
            P("dp", "fsdp", None),
            P("dp", "fsdp", None),
            P(),
            P(),
            P(),
            P(),
        ),
        check_vma=False,
    )
```

time: 3270 us -> 1320 us (0.40)
  waiting for transfers between devices: 2510 us -> 335 us
  local copies, waits for them, and re-layouts: 205 us -> 479 us
  starting transfers between devices: 0.82 us -> 143 us
  blocking collectives: 121 us -> 0 us
  other arithmetic: 142 us -> 96 us
    reduce_scatter x6 -> x0, waiting for transfers between devices: 2060 us -> none  [the longest x3 2010 us: per_device(): lax.psum_scatter(picked.reshape(n_dp * n_fsdp, rows_own, D), ('dp', 'fsdp...]
    all_gather x4 -> x0, waiting for transfers between devices: 452 us -> none  [the longest x1 416 us: per_device(): lax.all_gather(blocks.astype(jnp.bfloat16), 'fsdp', axis=1, tiled=True)]
    ppermute x0 -> x177, waiting for transfers between devices: none -> 335 us  [swap(): return lax.ppermute(value, AXES, pairs)]
    ppermute x0 -> x177, starting transfers between devices: none -> 138 us  [swap(): return lax.ppermute(value, AXES, pairs)]
    dynamic_update_slice x0 -> x95, local copies, waits for them, and re-layouts: none -> 133 us  [chunk(): lax.dynamic_update_slice(full, held[:, None, None], (0, at, side, 0, 0))]
    psum x3 -> x0, blocking collectives: 121 us -> none  [the longest x1 41.3 us: per_device(): lax.psum((jnp.sum(bn_grad, axis=0), jnp.sum(bn_grad * standard, axis=0)),...]
    gather x7 -> x0, local copies, waits for them, and re-layouts: 85.2 us -> none  [the longest x3 70.9 us: per_device(): picked = split_blocks[rank_block, shard_index] * rank_used]
    dynamic_slice x0 -> x36, local copies, waits for them, and re-layouts: none -> 78.6 us  [pick(): return lax.dynamic_index_in_dim(value, index, axis, keepdims=False)]
  transfers between devices with their start and end apart: 10 -> 178, of which waited for: 9 -> 60; matrix products, arithmetic and copies ran while one was open for 7% -> 54% of each run, Pallas kernels for 0% -> 0%
where the time goes in v1:
time: 1320 us; the launch traced here: 1310 us
  local copies, waits for them, and re-layouts  479 us (36%)
  waiting for transfers between devices  335 us (25%)
  matrix products  244 us (18%)
  starting transfers between devices  143 us (11%)
  other arithmetic  96 us (7%)
    ppermute x177, waiting for transfers between devices, swap(): return lax.ppermute(value, AXES, pairs)  335 us
    ppermute x177, starting transfers between devices, swap(): return lax.ppermute(value, AXES, pairs)  138 us
    dynamic_update_slice x95, local copies, waits for them, and re-layouts, chunk(): lax.dynamic_update_slice(full, held[:, None, None], (0, at, side, 0, 0))  133 us
    dot_general x27, matrix products, t_mm(): lax.dot_general(left, right, (((0,), (0,)), ((), ())), preferred_element_...  93.6 us
    unnamed x496, local copies, waits for them, and re-layouts  93.4 us
    dynamic_slice x36, local copies, waits for them, and re-layouts, pick(): return lax.dynamic_index_in_dim(value, index, axis, keepdims=False)  78.6 us
    dot_general x14, matrix products, mm_t(): lax.dot_general(left, right, (((1,), (1,)), ((), ())), preferred_element_...  43.6 us
    dot_general x36, matrix products, mm(): return jnp.dot(left, right, preferred_element_type=F32)  42.3 us
  transfers between devices with their start and end apart: 178, of which 60 were waited for; matrix products, arithmetic and copies ran while one was open for 54% of the time, Pallas kernels for 0%

profile of v1, /device:TPU:0, one launch (start us, length us, event | category | flops | bytes accessed | tf_op | source)
XLA Modules:
  0.0 1308.0 jit_solution(8683339995294121103)
XLA Ops:
  0.7 9.4 convert.75
  73.3 12.9 collective-permute-done.18
  109.3 7.9 collective-permute-done.16
  123.1 6.2 copy.1171
  131.4 6.2 copy.1029
  137.6 7.0 multiply_convert_fusion.4
  144.6 4.9 multiply_convert_fusion.3
  183.2 6.4 constant_dynamic-slice_fusion.48
  192.6 6.3 constant_dynamic-slice_fusion.53
  199.7 5.8 copy.1178
  209.7 6.0 copy.1175
  243.0 4.7 fusion.377
  372.2 9.3 collective-permute-done.69
  451.9 6.3 copy.1084
  458.2 6.9 multiply_convert_fusion.1
  465.1 4.6 reshape.1986
  469.7 8.6 constant_dynamic-slice_fusion.10
  482.5 5.8 copy.1194
  488.3 5.8 copy.1193
  501.3 6.2 copy.1069
  507.5 6.9 multiply_convert_fusion.2
  518.8 8.7 constant_dynamic-slice_fusion.15
  535.9 6.2 copy.1190
  548.0 4.7 fusion.378
  553.6 4.8 fusion.376
  564.8 5.3 fusion.8
  570.1 5.3 fusion.59
  575.4 5.5 fusion.15
  580.9 6.5 multiply_reduce_fusion.2
  636.1 5.1 multiply_reduce_fusion
  665.2 6.3 fusion.29
  683.9 7.3 convolution_convert_fusion.1
  691.2 5.9 fusion.53
  704.7 9.4 collective-permute-done.118
  714.4 9.3 collective-permute-done.108
  725.0 5.4 collective-permute-done.119
  731.4 5.3 collective-permute-done.109
  737.3 5.0 collective-permute-done.120
  742.8 5.1 collective-permute-done.110
  806.1 5.0 add_convert_fusion.8
  860.4 12.6 collective-permute-done.123
  877.9 8.9 add_convert_fusion
  886.8 8.6 collective-permute-done.113
  911.6 6.3 collective-permute-done.88
  920.6 19.8 %collective-permute-done.83 = bf16[1,1,2,128,2,1024]{5,3,4,2,1,0:T(8,128)(2,1)} collective-permute-done((bf16[1,1,2,128,2,1024]{5,3,4,2,1,0:T(8,128)(2,1)}, bf16[1,1,2,128,2,1024]{5,3,4,2,1,0:T(8,128)(2,1)}, u32[]{:S(2)}, u32[]{:S(2)}) %collective-permute-start.83) | collective-permute-done | bytes 1048608 | tf_op jit(solution)/shard_map/ppermute | solution.py:36
  955.4 7.5 collective-permute-done.134
  972.5 35.2 %collective-permute-done.99 = bf16[2,1,1,128,1,1024]{5,3,0,4,2,1:T(8,128)(2,1)S(1)} collective-permute-done((bf16[2,1,1,128,1,1024]{5,3,0,4,2,1:T(8,128)(2,1)}, bf16[2,1,1,128,1,1024]{5,3,0,4,2,1:T(8,128)(2,1)S(1)}, u32[]{:S(2)}, u32[]{:S(2)}) %collective-permute-start.99) | collective-permute-done | bytes 524320 | tf_op jit(solution)/shard_map/ppermute | solution.py:36
  1008.0 9.4 collective-permute-done.94
  1026.8 5.5 collective-permute-done.130
  1032.4 5.5 collective-permute-done.125
  1038.1 5.5 collective-permute-done.115
  1043.6 6.9 collective-permute-done.100
  1051.3 7.6 collective-permute-done.95
  1059.8 6.1 collective-permute-done.90
  1072.7 9.8 collective-permute-done.136
  1092.5 5.4 collective-permute-done.116
  1107.9 8.2 collective-permute-done.105
  1116.6 9.6 collective-permute-done.106
  1133.0 4.6 all-to-all-start
  1137.8 6.1 fusion.346
  1182.7 4.8 convolution_convert_fusion.8
  1193.0 4.8 convolution_convert_fusion.7
  1204.3 4.8 convolution_convert_fusion.9
  1221.2 6.4 collective-permute-done.142
  (1280 shorter events, 827.3 us)
Async XLA Ops:
  18.9 41.8 %collective-permute-start = (bf16[2,128,1024]{2,1,0:T(8,128)(2,1)}, bf16[2,128,1024]{2,1,0:T(8,128)(2,1)}, u32[]{:S(2)}, u32[]{:S(2)}) collective-permute-start(bf16[2,128,1024]{2,1,0:T(8,128)(2,1)} %dynamic-slice_bitcast_fusion.18), channel_id=1, source_target_pairs={{0,1},{1,0},{2,3},{3,2},{4,5},{5,4},{6,7},{7,6},{8,9},{9,8},{10,11... | collective-permute-start | bytes 1572872 | tf_op jit(solution)/shard_map/ppermute | solution.py:36
  21.9 75.7 %collective-permute-start.2 = (bf16[2,128,1024]{2,1,0:T(8,128)(2,1)}, bf16[2,128,1024]{2,1,0:T(8,128)(2,1)}, u32[]{:S(2)}, u32[]{:S(2)}) collective-permute-start(bf16[2,128,1024]{2,1,0:T(8,128)(2,1)} %dynamic-slice_bitcast_fusion.18), channel_id=1, source_target_pairs={{0,2},{1,3},{2,0},{3,1},{4,6},{5,7},{6,4},{7,5},{8,10},{9,11},{10,... | collective-permute-start | bytes 1572872 | tf_op jit(solution)/shard_map/ppermute | solution.py:36
  24.2 39.9 %collective-permute-start.12 = (bf16[2,128,1024]{2,1,0:T(8,128)(2,1)}, bf16[2,128,1024]{2,1,0:T(8,128)(2,1)}, u32[]{:S(2)}, u32[]{:S(2)}) collective-permute-start(bf16[2,128,1024]{2,1,0:T(8,128)(2,1)} %dynamic-slice_bitcast_fusion.17), channel_id=1, source_target_pairs={{0,2},{1,3},{2,0},{3,1},{4,6},{5,7},{6,4},{7,5},{8,10},{9,11},{10,... | collective-permute-start | bytes 1572872 | tf_op jit(solution)/shard_map/ppermute | solution.py:36
  24.7 77.4 %collective-permute-start.14 = (bf16[2,128,1024]{2,1,0:T(8,128)(2,1)}, bf16[2,128,1024]{2,1,0:T(8,128)(2,1)}, u32[]{:S(2)}, u32[]{:S(2)}) collective-permute-start(bf16[2,128,1024]{2,1,0:T(8,128)(2,1)} %dynamic-slice_bitcast_fusion.17), channel_id=1, source_target_pairs={{0,1},{1,0},{2,3},{3,2},{4,5},{5,4},{6,7},{7,6},{8,9},{9,8},{10,11... | collective-permute-start | bytes 1572872 | tf_op jit(solution)/shard_map/ppermute | solution.py:36
  60.7 29.9 %collective-permute-start.6 = (bf16[2,128,1024]{2,1,0:T(8,128)(2,1)S(1)}, bf16[2,128,1024]{2,1,0:T(8,128)(2,1)}, u32[]{:S(2)}, u32[]{:S(2)}) collective-permute-start(bf16[2,128,1024]{2,1,0:T(8,128)(2,1)S(1)} %copy-done.94), channel_id=1, source_target_pairs={{0,1},{1,0},{2,3},{3,2},{4,5},{5,4},{6,7},{7,6},{8,9},{9,8},{10,11... | collective-permute-start | bytes 1572872 | tf_op jit(solution)/shard_map/ppermute | solution.py:36
  62.6 93.9 %collective-permute-start.8 = (bf16[2,128,1024]{2,1,0:T(8,128)(2,1)S(1)}, bf16[2,128,1024]{2,1,0:T(8,128)(2,1)}, u32[]{:S(2)}, u32[]{:S(2)}) collective-permute-start(bf16[2,128,1024]{2,1,0:T(8,128)(2,1)S(1)} %copy-done.94), channel_id=1, source_target_pairs={{0,2},{1,3},{2,0},{3,1},{4,6},{5,7},{6,4},{7,5},{8,10},{9,11},{10,... | collective-permute-start | bytes 1572872 | tf_op jit(solution)/shard_map/ppermute | solution.py:36
  105.6 55.3 %collective-permute-start.20 = (bf16[2,128,1024]{2,1,0:T(8,128)(2,1)S(1)}, bf16[2,128,1024]{2,1,0:T(8,128)(2,1)S(1)}, u32[]{:S(2)}, u32[]{:S(2)}) collective-permute-start(bf16[2,128,1024]{2,1,0:T(8,128)(2,1)S(1)} %copy-done.93), channel_id=1, source_target_pairs={{0,1},{1,0},{2,3},{3,2},{4,5},{5,4},{6,7},{7,6},{8,9},{9,8},{10,11... | collective-permute-start | bytes 1572872 | tf_op jit(solution)/shard_map/ppermute | solution.py:36
  107.8 41.7 %collective-permute-start.30 = (bf16[2,128,1024]{2,1,0:T(8,128)(2,1)}, bf16[2,128,1024]{2,1,0:T(8,128)(2,1)}, u32[]{:S(2)}, u32[]{:S(2)}) collective-permute-start(bf16[2,128,1024]{2,1,0:T(8,128)(2,1)} %dynamic-slice_bitcast_fusion.13), channel_id=1, source_target_pairs={{0,1},{1,0},{2,3},{3,2},{4,5},{5,4},{6,7},{7,6},{8,9},{9,8},{10,11... | collective-permute-start | bytes 1572872 | tf_op jit(solution)/shard_map/ppermute | solution.py:36
  121.7 40.9 %collective-permute-start.24 = (bf16[2,128,1024]{2,1,0:T(8,128)(2,1)}, bf16[2,128,1024]{2,1,0:T(8,128)(2,1)}, u32[]{:S(2)}, u32[]{:S(2)}) collective-permute-start(bf16[2,128,1024]{2,1,0:T(8,128)(2,1)} %dynamic-slice_bitcast_fusion.14), channel_id=1, source_target_pairs={{0,2},{1,3},{2,0},{3,1},{4,6},{5,7},{6,4},{7,5},{8,10},{9,11},{10,... | collective-permute-start | bytes 1572872 | tf_op jit(solution)/shard_map/ppermute | solution.py:36
  154.1 103.9 %collective-permute-start.26 = (bf16[2,128,1024]{2,1,0:T(8,128)(2,1)}, bf16[2,128,1024]{2,1,0:T(8,128)(2,1)}, u32[]{:S(2)}, u32[]{:S(2)}) collective-permute-start(bf16[2,128,1024]{2,1,0:T(8,128)(2,1)} %dynamic-slice_bitcast_fusion.14), channel_id=1, source_target_pairs={{0,1},{1,0},{2,3},{3,2},{4,5},{5,4},{6,7},{7,6},{8,9},{9,8},{10,11... | collective-permute-start | bytes 1572872 | tf_op jit(solution)/shard_map/ppermute | solution.py:36
  156.5 105.1 %collective-permute-start.32 = (bf16[2,128,1024]{2,1,0:T(8,128)(2,1)}, bf16[2,128,1024]{2,1,0:T(8,128)(2,1)}, u32[]{:S(2)}, u32[]{:S(2)}) collective-permute-start(bf16[2,128,1024]{2,1,0:T(8,128)(2,1)} %dynamic-slice_bitcast_fusion.13), channel_id=1, source_target_pairs={{0,2},{1,3},{2,0},{3,1},{4,6},{5,7},{6,4},{7,5},{8,10},{9,11},{10,... | collective-permute-start | bytes 1572872 | tf_op jit(solution)/shard_map/ppermute | solution.py:36
  160.9 59.1 %collective-permute-start.10 = (bf16[2,128,1024]{2,1,0:T(8,128)(2,1)}, bf16[2,128,1024]{2,1,0:T(8,128)(2,1)}, u32[]{:S(2)}, u32[]{:S(2)}) collective-permute-start(bf16[2,128,1024]{2,1,0:T(8,128)(2,1)} %collective-permute-done.6), channel_id=1, source_target_pairs={{0,2},{1,3},{2,0},{3,1},{4,6},{5,7},{6,4},{7,5},{8,10},{9,11},{10,... | collective-permute-start | bytes 1572872 | tf_op jit(solution)/shard_map/ppermute | solution.py:36
  179.6 42.4 %collective-permute-start.47 = (bf16[1,128,1024]{2,1,0:T(8,128)(2,1)}, bf16[1,128,1024]{2,1,0:T(8,128)(2,1)}, u32[]{:S(2)}, u32[]{:S(2)}) collective-permute-start(bf16[1,128,1024]{2,1,0:T(8,128)(2,1)} %dynamic-slice_bitcast_fusion.29), channel_id=1, source_target_pairs={{0,2},{1,3},{2,0},{3,1},{4,6},{5,7},{6,4},{7,5},{8,10},{9,11},{10,... | collective-permute-start | bytes 786440 | tf_op jit(solution)/shard_map/ppermute | solution.py:36
  190.3 39.3 %collective-permute-start.49 = (bf16[1,128,1024]{2,1,0:T(8,128)(2,1)}, bf16[1,128,1024]{2,1,0:T(8,128)(2,1)}, u32[]{:S(2)}, u32[]{:S(2)}) collective-permute-start(bf16[1,128,1024]{2,1,0:T(8,128)(2,1)} %dynamic-slice_bitcast_fusion.29), channel_id=1, source_target_pairs={{0,1},{1,0},{2,3},{3,2},{4,5},{5,4},{6,7},{7,6},{8,9},{9,8},{10,11... | collective-permute-start | bytes 786440 | tf_op jit(solution)/shard_map/ppermute | solution.py:36
  239.1 96.8 %collective-permute-start.38 = (bf16[2,128,1024]{2,1,0:T(8,128)(2,1)}, bf16[2,128,1024]{2,1,0:T(8,128)(2,1)}, u32[]{:S(2)}, u32[]{:S(2)}) collective-permute-start(bf16[2,128,1024]{2,1,0:T(8,128)(2,1)} %dynamic-slice_bitcast_fusion.12), channel_id=1, source_target_pairs={{0,2},{1,3},{2,0},{3,1},{4,6},{5,7},{6,4},{7,5},{8,10},{9,11},{10,... | collective-permute-start | bytes 1572872 | tf_op jit(solution)/shard_map/ppermute | solution.py:36
  265.0 28.1 %collective-permute-start.65 = (bf16[2,128,1024]{2,1,0:T(8,128)(2,1)}, bf16[2,128,1024]{2,1,0:T(8,128)(2,1)}, u32[]{:S(2)}, u32[]{:S(2)}) collective-permute-start(bf16[2,128,1024]{2,1,0:T(8,128)(2,1)} %dynamic-slice_bitcast_fusion.9), channel_id=1, source_target_pairs={{0,2},{1,3},{2,0},{3,1},{4,6},{5,7},{6,4},{7,5},{8,10},{9,11},{10,... | collective-permute-start | bytes 1572872 | tf_op jit(solution)/shard_map/ppermute | solution.py:36
  272.7 90.5 %collective-permute-start.67 = (bf16[2,128,1024]{2,1,0:T(8,128)(2,1)}, bf16[2,128,1024]{2,1,0:T(8,128)(2,1)}, u32[]{:S(2)}, u32[]{:S(2)}) collective-permute-start(bf16[2,128,1024]{2,1,0:T(8,128)(2,1)} %dynamic-slice_bitcast_fusion.9), channel_id=1, source_target_pairs={{0,1},{1,0},{2,3},{3,2},{4,5},{5,4},{6,7},{7,6},{8,9},{9,8},{10,11... | collective-permute-start | bytes 1572872 | tf_op jit(solution)/shard_map/ppermute | solution.py:36
  287.4 49.9 %collective-permute-start.53 = (bf16[2,128,1024]{2,1,0:T(8,128)(2,1)}, bf16[2,128,1024]{2,1,0:T(8,128)(2,1)}, u32[]{:S(2)}, u32[]{:S(2)}) collective-permute-start(bf16[2,128,1024]{2,1,0:T(8,128)(2,1)} %dynamic-slice_bitcast_fusion.11), channel_id=1, source_target_pairs={{0,1},{1,0},{2,3},{3,2},{4,5},{5,4},{6,7},{7,6},{8,9},{9,8},{10,11... | collective-permute-start | bytes 1572872 | tf_op jit(solution)/shard_map/ppermute | solution.py:36
  290.7 93.9 %collective-permute-start.55 = (bf16[2,128,1024]{2,1,0:T(8,128)(2,1)}, bf16[2,128,1024]{2,1,0:T(8,128)(2,1)}, u32[]{:S(2)}, u32[]{:S(2)}) collective-permute-start(bf16[2,128,1024]{2,1,0:T(8,128)(2,1)} %dynamic-slice_bitcast_fusion.11), channel_id=1, source_target_pairs={{0,2},{1,3},{2,0},{3,1},{4,6},{5,7},{6,4},{7,5},{8,10},{9,11},{10,... | collective-permute-start | bytes 1572872 | tf_op jit(solution)/shard_map/ppermute | solution.py:36
  307.9 37.0 %collective-permute-start.37 = (bf16[2,128,1024]{2,1,0:T(8,128)(2,1)}, bf16[2,128,1024]{2,1,0:T(8,128)(2,1)}, u32[]{:S(2)}, u32[]{:S(2)}) collective-permute-start(bf16[2,128,1024]{2,1,0:T(8,128)(2,1)} %collective-permute-done.36), channel_id=1, source_target_pairs={{0,4},{1,5},{2,6},{3,7},{4,0},{5,1},{6,2},{7,3},{8,12},{9,13},{10,... | collective-permute-start | bytes 1572872 | tf_op jit(solution)/shard_map/ppermute | solution.py:36
  355.3 72.5 %collective-permute-start.73 = (bf16[2,128,1024]{2,1,0:T(8,128)(2,1)}, bf16[2,128,1024]{2,1,0:T(8,128)(2,1)}, u32[]{:S(2)}, u32[]{:S(2)}) collective-permute-start(bf16[2,128,1024]{2,1,0:T(8,128)(2,1)} %dynamic-slice_bitcast_fusion.8), channel_id=1, source_target_pairs={{0,1},{1,0},{2,3},{3,2},{4,5},{5,4},{6,7},{7,6},{8,9},{9,8},{10,11... | collective-permute-start | bytes 1572872 | tf_op jit(solution)/shard_map/ppermute | solution.py:36
  370.7 33.3 %collective-permute-start.59 = (bf16[2,128,1024]{2,1,0:T(8,128)(2,1)}, bf16[2,128,1024]{2,1,0:T(8,128)(2,1)}, u32[]{:S(2)}, u32[]{:S(2)}) collective-permute-start(bf16[2,128,1024]{2,1,0:T(8,128)(2,1)} %dynamic-slice_bitcast_fusion.10), channel_id=1, source_target_pairs={{0,1},{1,0},{2,3},{3,2},{4,5},{5,4},{6,7},{7,6},{8,9},{9,8},{10,11... | collective-permute-start | bytes 1572872 | tf_op jit(solution)/shard_map/ppermute | solution.py:36
  381.5 112.5 %collective-permute-start.61 = (bf16[2,128,1024]{2,1,0:T(8,128)(2,1)}, bf16[2,128,1024]{2,1,0:T(8,128)(2,1)}, u32[]{:S(2)}, u32[]{:S(2)}) collective-permute-start(bf16[2,128,1024]{2,1,0:T(8,128)(2,1)} %dynamic-slice_bitcast_fusion.10), channel_id=1, source_target_pairs={{0,2},{1,3},{2,0},{3,1},{4,6},{5,7},{6,4},{7,5},{8,10},{9,11},{10,... | collective-permute-start | bytes 1572872 | tf_op jit(solution)/shard_map/ppermute | solution.py:36
  405.9 72.4 %collective-permute-start.72 = (bf16[2,128,1024]{2,1,0:T(8,128)(2,1)}, bf16[2,128,1024]{2,1,0:T(8,128)(2,1)}, u32[]{:S(2)}, u32[]{:S(2)}) collective-permute-start(bf16[2,128,1024]{2,1,0:T(8,128)(2,1)} %collective-permute-done.71), channel_id=1, source_target_pairs={{0,4},{1,5},{2,6},{3,7},{4,0},{5,1},{6,2},{7,3},{8,12},{9,13},{10,... | collective-permute-start | bytes 1572872 | tf_op jit(solution)/shard_map/ppermute | solution.py:36
  410.1 85.0 %collective-permute-start.75 = (bf16[2,128,1024]{2,1,0:T(8,128)(2,1)}, bf16[2,128,1024]{2,1,0:T(8,128)(2,1)}, u32[]{:S(2)}, u32[]{:S(2)}) collective-permute-start(bf16[2,128,1024]{2,1,0:T(8,128)(2,1)} %collective-permute-done.71), channel_id=1, source_target_pairs={{0,1},{1,0},{2,3},{3,2},{4,5},{5,4},{6,7},{7,6},{8,9},{9,8},{10,11... | collective-permute-start | bytes 1572872 | tf_op jit(solution)/shard_map/ppermute | solution.py:36
  427.9 67.2 %collective-permute-start.74 = (bf16[2,128,1024]{2,1,0:T(8,128)(2,1)}, bf16[2,128,1024]{2,1,0:T(8,128)(2,1)}, u32[]{:S(2)}, u32[]{:S(2)}) collective-permute-start(bf16[2,128,1024]{2,1,0:T(8,128)(2,1)} %collective-permute-done.73), channel_id=1, source_target_pairs={{0,4},{1,5},{2,6},{3,7},{4,0},{5,1},{6,2},{7,3},{8,12},{9,13},{10,... | collective-permute-start | bytes 1572872 | tf_op jit(solution)/shard_map/ppermute | solution.py:36
  450.0 77.6 %collective-permute-start.60 = (bf16[2,128,1024]{2,1,0:T(8,128)(2,1)}, bf16[2,128,1024]{2,1,0:T(8,128)(2,1)}, u32[]{:S(2)}, u32[]{:S(2)}) collective-permute-start(bf16[2,128,1024]{2,1,0:T(8,128)(2,1)} %collective-permute-done.59), channel_id=1, source_target_pairs={{0,4},{1,5},{2,6},{3,7},{4,0},{5,1},{6,2},{7,3},{8,12},{9,13},{10,... | collective-permute-start | bytes 1572872 | tf_op jit(solution)/shard_map/ppermute | solution.py:36
  494.1 48.1 %collective-permute-start.63 = (bf16[2,128,1024]{2,1,0:T(8,128)(2,1)}, bf16[2,128,1024]{2,1,0:T(8,128)(2,1)}, u32[]{:S(2)}, u32[]{:S(2)}) collective-permute-start(bf16[2,128,1024]{2,1,0:T(8,128)(2,1)} %collective-permute-done.59), channel_id=1, source_target_pairs={{0,2},{1,3},{2,0},{3,1},{4,6},{5,7},{6,4},{7,5},{8,10},{9,11},{10,... | collective-permute-start | bytes 1572872 | tf_op jit(solution)/shard_map/ppermute | solution.py:36
  495.1 47.1 %collective-permute-start.62 = (bf16[2,128,1024]{2,1,0:T(8,128)(2,1)}, bf16[2,128,1024]{2,1,0:T(8,128)(2,1)}, u32[]{:S(2)}, u32[]{:S(2)}) collective-permute-start(bf16[2,128,1024]{2,1,0:T(8,128)(2,1)} %collective-permute-done.61), channel_id=1, source_target_pairs={{0,4},{1,5},{2,6},{3,7},{4,0},{5,1},{6,2},{7,3},{8,12},{9,13},{10,... | collective-permute-start | bytes 1572872 | tf_op jit(solution)/shard_map/ppermute | solution.py:36
  495.1 51.0 %collective-permute-start.76 = (bf16[2,128,1024]{2,1,0:T(8,128)(2,1)}, bf16[2,128,1024]{2,1,0:T(8,128)(2,1)}, u32[]{:S(2)}, u32[]{:S(2)}) collective-permute-start(bf16[2,128,1024]{2,1,0:T(8,128)(2,1)} %collective-permute-done.75), channel_id=1, source_target_pairs={{0,4},{1,5},{2,6},{3,7},{4,0},{5,1},{6,2},{7,3},{8,12},{9,13},{10,... | collective-permute-start | bytes 1572872 | tf_op jit(solution)/shard_map/ppermute | solution.py:36
  604.3 160.4 %collective-permute-start.137 = (bf16[1024,1024]{1,0:T(8,128)(2,1)}, bf16[1024,1024]{1,0:T(8,128)(2,1)}, u32[]{:S(2)}, u32[]{:S(2)}) collective-permute-start(bf16[1024,1024]{1,0:T(8,128)(2,1)} %convolution_convert_fusion.10), channel_id=1, source_target_pairs={{0,4},{1,5},{2,6},{3,7},{4,0},{5,1},{6,2},{7,3},{8,12},{9,13},{10,... | collective-permute-start | bytes 6291464 | tf_op jit(solution)/shard_map/ppermute | solution.py:36
  609.0 160.0 %collective-permute-start.132 = (bf16[1024,1024]{1,0:T(8,128)(2,1)}, bf16[1024,1024]{1,0:T(8,128)(2,1)}, u32[]{:S(2)}, u32[]{:S(2)}) collective-permute-start(bf16[1024,1024]{1,0:T(8,128)(2,1)} %convolution_convert_fusion.11), channel_id=1, source_target_pairs={{0,4},{1,5},{2,6},{3,7},{4,0},{5,1},{6,2},{7,3},{8,12},{9,13},{10,... | collective-permute-start | bytes 6291464 | tf_op jit(solution)/shard_map/ppermute | solution.py:36
  609.0 150.8 %collective-permute-start.127 = (bf16[512,2048]{1,0:T(8,128)(2,1)}, bf16[512,2048]{1,0:T(8,128)(2,1)}, u32[]{:S(2)}, u32[]{:S(2)}) collective-permute-start(bf16[512,2048]{1,0:T(8,128)(2,1)} %convolution_convert_fusion.2), channel_id=1, source_target_pairs={{0,4},{1,5},{2,6},{3,7},{4,0},{5,1},{6,2},{7,3},{8,12},{9,13},{10,... | collective-permute-start | bytes 6291464 | tf_op jit(solution)/shard_map/ppermute | solution.py:36
  611.7 85.4 %collective-permute-start.117 = (bf16[512,1024]{1,0:T(8,128)(2,1)}, bf16[512,1024]{1,0:T(8,128)(2,1)}, u32[]{:S(2)}, u32[]{:S(2)}) collective-permute-start(bf16[512,1024]{1,0:T(8,128)(2,1)} %convolution_convert_fusion.18), channel_id=1, source_target_pairs={{0,4},{1,5},{2,6},{3,7},{4,0},{5,1},{6,2},{7,3},{8,12},{9,13},{10,... | collective-permute-start | bytes 3145736 | tf_op jit(solution)/shard_map/ppermute | solution.py:36
  672.2 28.0 %collective-permute-start.107 = (bf16[512,1024]{1,0:T(8,128)(2,1)S(1)}, bf16[512,1024]{1,0:T(8,128)(2,1)S(1)}, u32[]{:S(2)}, u32[]{:S(2)}) collective-permute-start(bf16[512,1024]{1,0:T(8,128)(2,1)S(1)} %convolution_convert_fusion.19), channel_id=1, source_target_pairs={{0,4},{1,5},{2,6},{3,7},{4,0},{5,1},{6,2},{7,3},{8,12},{9,13},{10,... | collective-permute-start | bytes 3145736 | tf_op jit(solution)/shard_map/ppermute | solution.py:36
  714.1 66.1 %collective-permute-start.122 = (bf16[512,2048]{1,0:T(8,128)(2,1)}, bf16[512,2048]{1,0:T(8,128)(2,1)}, u32[]{:S(2)}, u32[]{:S(2)}) collective-permute-start(bf16[512,2048]{1,0:T(8,128)(2,1)} %convolution_convert_fusion.3), channel_id=1, source_target_pairs={{0,4},{1,5},{2,6},{3,7},{4,0},{5,1},{6,2},{7,3},{8,12},{9,13},{10,... | collective-permute-start | bytes 6291464 | tf_op jit(solution)/shard_map/ppermute | solution.py:36
  759.7 39.2 %collective-permute-start.112 = (bf16[512,2048]{1,0:T(8,128)(2,1)}, bf16[512,2048]{1,0:T(8,128)(2,1)}, u32[]{:S(2)}, u32[]{:S(2)}) collective-permute-start(bf16[512,2048]{1,0:T(8,128)(2,1)} %convolution_convert_fusion.4), channel_id=1, source_target_pairs={{0,4},{1,5},{2,6},{3,7},{4,0},{5,1},{6,2},{7,3},{8,12},{9,13},{10,... | collective-permute-start | bytes 6291464 | tf_op jit(solution)/shard_map/ppermute | solution.py:36
  759.8 64.3 %collective-permute-start.97 = (bf16[1024,1024]{1,0:T(8,128)(2,1)}, bf16[1024,1024]{1,0:T(8,128)(2,1)}, u32[]{:S(2)}, u32[]{:S(2)}) collective-permute-start(bf16[1024,1024]{1,0:T(8,128)(2,1)} %convolution_convert_fusion.12), channel_id=1, source_target_pairs={{0,4},{1,5},{2,6},{3,7},{4,0},{5,1},{6,2},{7,3},{8,12},{9,13},{10,... | collective-permute-start | bytes 6291464 | tf_op jit(solution)/shard_map/ppermute | solution.py:36
  764.8 40.4 %collective-permute-start.87 = (bf16[512,2048]{1,0:T(8,128)(2,1)}, bf16[512,2048]{1,0:T(8,128)(2,1)}, u32[]{:S(2)}, u32[]{:S(2)}) collective-permute-start(bf16[512,2048]{1,0:T(8,128)(2,1)} %convolution_convert_fusion.5), channel_id=1, source_target_pairs={{0,4},{1,5},{2,6},{3,7},{4,0},{5,1},{6,2},{7,3},{8,12},{9,13},{10,... | collective-permute-start | bytes 6291464 | tf_op jit(solution)/shard_map/ppermute | solution.py:36
  769.1 49.7 %collective-permute-start.82 = (bf16[512,2048]{1,0:T(8,128)(2,1)}, bf16[512,2048]{1,0:T(8,128)(2,1)}, u32[]{:S(2)}, u32[]{:S(2)}) collective-permute-start(bf16[512,2048]{1,0:T(8,128)(2,1)} %convolution_convert_fusion.6), channel_id=1, source_target_pairs={{0,4},{1,5},{2,6},{3,7},{4,0},{5,1},{6,2},{7,3},{8,12},{9,13},{10,... | collective-permute-start | bytes 6291464 | tf_op jit(solution)/shard_map/ppermute | solution.py:36
  780.2 47.9 %collective-permute-start.92 = (bf16[1024,1024]{1,0:T(8,128)(2,1)}, bf16[1024,1024]{1,0:T(8,128)(2,1)}, u32[]{:S(2)}, u32[]{:S(2)}) collective-permute-start(bf16[1024,1024]{1,0:T(8,128)(2,1)} %convolution_convert_fusion.13), channel_id=1, source_target_pairs={{0,4},{1,5},{2,6},{3,7},{4,0},{5,1},{6,2},{7,3},{8,12},{9,13},{10,... | collective-permute-start | bytes 6291464 | tf_op jit(solution)/shard_map/ppermute | solution.py:36
  798.9 78.0 %collective-permute-start.102 = (bf16[512,3072]{1,0:T(8,128)(2,1)}, bf16[512,3072]{1,0:T(8,128)(2,1)}, u32[]{:S(2)}, u32[]{:S(2)}) collective-permute-start(bf16[512,3072]{1,0:T(8,128)(2,1)} %convolution_convert_fusion.1), channel_id=1, source_target_pairs={{0,4},{1,5},{2,6},{3,7},{4,0},{5,1},{6,2},{7,3},{8,12},{9,13},{10,... | collective-permute-start | bytes 9437192 | tf_op jit(solution)/shard_map/ppermute | solution.py:36
  805.2 43.3 %collective-permute-start.138 = (bf16[2,2,1,128,1,1024]{5,3,0,4,2,1:T(8,128)(2,1)}, bf16[2,2,1,128,1,1024]{5,3,0,4,2,1:T(8,128)(2,1)}, u32[]{:S(2)}, u32[]{:S(2)}) collective-permute-start(bf16[2,2,1,128,1,1024]{5,3,0,4,2,1:T(8,128)(2,1)} %bitcast.1449), channel_id=1, source_target_pairs={{0,1},{1,0},{2,3},{3,2},{4,5},{5,4},{6,7},{7,6},{8,9},{9,8},{10,11... | collective-permute-start | bytes 3145736 | tf_op jit(solution)/shard_map/ppermute | solution.py:36
  818.8 34.3 %collective-permute-start.133 = (bf16[2,2,1,128,1,1024]{5,3,0,4,2,1:T(8,128)(2,1)}, bf16[2,2,1,128,1,1024]{5,3,0,4,2,1:T(8,128)(2,1)}, u32[]{:S(2)}, u32[]{:S(2)}) collective-permute-start(bf16[2,2,1,128,1,1024]{5,3,0,4,2,1:T(8,128)(2,1)} %bitcast.1297), channel_id=1, source_target_pairs={{0,1},{1,0},{2,3},{3,2},{4,5},{5,4},{6,7},{7,6},{8,9},{9,8},{10,11... | collective-permute-start | bytes 3145736 | tf_op jit(solution)/shard_map/ppermute | solution.py:36
  824.1 32.5 %collective-permute-start.128 = (bf16[1,1,2,128,2,1024]{5,3,4,2,1,0:T(8,128)(2,1)}, bf16[1,1,2,128,2,1024]{5,3,4,2,1,0:T(8,128)(2,1)}, u32[]{:S(2)}, u32[]{:S(2)}) collective-permute-start(bf16[1,1,2,128,2,1024]{5,3,4,2,1,0:T(8,128)(2,1)} %bitcast.1298), channel_id=1, source_target_pairs={{0,2},{1,3},{2,0},{3,1},{4,6},{5,7},{6,4},{7,5},{8,10},{9,11},{10,... | collective-permute-start | bytes 3145736 | tf_op jit(solution)/shard_map/ppermute | solution.py:36
  828.1 44.9 %collective-permute-start.123 = (bf16[1,1,2,128,2,1024]{5,3,4,2,1,0:T(8,128)(2,1)}, bf16[1,1,2,128,2,1024]{5,3,4,2,1,0:T(8,128)(2,1)}, u32[]{:S(2)}, u32[]{:S(2)}) collective-permute-start(bf16[1,1,2,128,2,1024]{5,3,4,2,1,0:T(8,128)(2,1)} %bitcast.1299), channel_id=1, source_target_pairs={{0,2},{1,3},{2,0},{3,1},{4,6},{5,7},{6,4},{7,5},{8,10},{9,11},{10,... | collective-permute-start | bytes 3145736 | tf_op jit(solution)/shard_map/ppermute | solution.py:36
  848.5 46.9 %collective-permute-start.113 = (bf16[1,1,2,128,2,1024]{5,3,4,2,1,0:T(8,128)(2,1)S(1)}, bf16[1,1,2,128,2,1024]{5,3,4,2,1,0:T(8,128)(2,1)S(1)}, u32[]{:S(2)}, u32[]{:S(2)}) collective-permute-start(bf16[1,1,2,128,2,1024]{5,3,4,2,1,0:T(8,128)(2,1)S(1)} %bitcast.1450), channel_id=1, source_target_pairs={{0,2},{1,3},{2,0},{3,1},{4,6},{5,7},{6,4},{7,5},{8,10},{9,11},{10,... | collective-permute-start | bytes 3145736 | tf_op jit(solution)/shard_map/ppermute | solution.py:36
  853.1 52.9 %collective-permute-start.98 = (bf16[2,2,1,128,1,1024]{5,3,0,4,2,1:T(8,128)(2,1)}, bf16[2,2,1,128,1,1024]{5,3,0,4,2,1:T(8,128)(2,1)}, u32[]{:S(2)}, u32[]{:S(2)}) collective-permute-start(bf16[2,2,1,128,1,1024]{5,3,0,4,2,1:T(8,128)(2,1)} %bitcast.1301), channel_id=1, source_target_pairs={{0,1},{1,0},{2,3},{3,2},{4,5},{5,4},{6,7},{7,6},{8,9},{9,8},{10,11... | collective-permute-start | bytes 3145736 | tf_op jit(solution)/shard_map/ppermute | solution.py:36
  856.6 52.3 %collective-permute-start.93 = (bf16[2,2,1,128,1,1024]{5,3,0,4,2,1:T(8,128)(2,1)}, bf16[2,2,1,128,1,1024]{5,3,0,4,2,1:T(8,128)(2,1)}, u32[]{:S(2)}, u32[]{:S(2)}) collective-permute-start(bf16[2,2,1,128,1,1024]{5,3,0,4,2,1:T(8,128)(2,1)} %bitcast.1302), channel_id=1, source_target_pairs={{0,1},{1,0},{2,3},{3,2},{4,5},{5,4},{6,7},{7,6},{8,9},{9,8},{10,11... | collective-permute-start | bytes 3145736 | tf_op jit(solution)/shard_map/ppermute | solution.py:36
  873.0 44.9 %collective-permute-start.88 = (bf16[1,1,2,128,2,1024]{5,3,4,2,1,0:T(8,128)(2,1)}, bf16[1,1,2,128,2,1024]{5,3,4,2,1,0:T(8,128)(2,1)}, u32[]{:S(2)}, u32[]{:S(2)}) collective-permute-start(bf16[1,1,2,128,2,1024]{5,3,4,2,1,0:T(8,128)(2,1)} %bitcast.1303), channel_id=1, source_target_pairs={{0,2},{1,3},{2,0},{3,1},{4,6},{5,7},{6,4},{7,5},{8,10},{9,11},{10,... | collective-permute-start | bytes 3145736 | tf_op jit(solution)/shard_map/ppermute | solution.py:36
  876.8 63.6 %collective-permute-start.83 = (bf16[1,1,2,128,2,1024]{5,3,4,2,1,0:T(8,128)(2,1)}, bf16[1,1,2,128,2,1024]{5,3,4,2,1,0:T(8,128)(2,1)}, u32[]{:S(2)}, u32[]{:S(2)}) collective-permute-start(bf16[1,1,2,128,2,1024]{5,3,4,2,1,0:T(8,128)(2,1)} %bitcast.1304), channel_id=1, source_target_pairs={{0,2},{1,3},{2,0},{3,1},{4,6},{5,7},{6,4},{7,5},{8,10},{9,11},{10,... | collective-permute-start | bytes 3145736 | tf_op jit(solution)/shard_map/ppermute | solution.py:36
  895.4 57.5 %collective-permute-start.139 = (bf16[2,1,1,128,1,1024]{5,3,0,4,2,1:T(8,128)(2,1)}, bf16[2,1,1,128,1,1024]{5,3,0,4,2,1:T(8,128)(2,1)}, u32[]{:S(2)}, u32[]{:S(2)}) collective-permute-start(bf16[2,1,1,128,1,1024]{5,3,0,4,2,1:T(8,128)(2,1)} %constant_dynamic-slice_fusion.7), channel_id=1, source_target_pairs={{0,2},{1,3},{2,0},{3,1},{4,6},{5,7},{6,4},{7,5},{8,10},{9,11},{10,... | collective-permute-start | bytes 1572872 | tf_op jit(solution)/shard_map/ppermute | solution.py:36
  906.0 56.9 %collective-permute-start.134 = (bf16[2,1,1,128,1,1024]{5,3,0,4,2,1:T(8,128)(2,1)}, bf16[2,1,1,128,1,1024]{5,3,0,4,2,1:T(8,128)(2,1)}, u32[]{:S(2)}, u32[]{:S(2)}) collective-permute-start(bf16[2,1,1,128,1,1024]{5,3,0,4,2,1:T(8,128)(2,1)} %constant_dynamic-slice_fusion.12), channel_id=1, source_target_pairs={{0,2},{1,3},{2,0},{3,1},{4,6},{5,7},{6,4},{7,5},{8,10},{9,11},{10,... | collective-permute-start | bytes 1572872 | tf_op jit(solution)/shard_map/ppermute | solution.py:36
  909.0 56.4 %collective-permute-start.129 = (bf16[1,1,1,128,2,1024]{5,3,4,2,1,0:T(8,128)(2,1)}, bf16[1,1,1,128,2,1024]{5,3,4,2,1,0:T(8,128)(2,1)}, u32[]{:S(2)}, u32[]{:S(2)}) collective-permute-start(bf16[1,1,1,128,2,1024]{5,3,4,2,1,0:T(8,128)(2,1)} %constant_dynamic-slice_fusion.17), channel_id=1, source_target_pairs={{0,1},{1,0},{2,3},{3,2},{4,5},{5,4},{6,7},{7,6},{8,9},{9,8},{10,11... | collective-permute-start | bytes 1572872 | tf_op jit(solution)/shard_map/ppermute | solution.py:36
  918.0 49.7 %collective-permute-start.124 = (bf16[1,1,1,128,2,1024]{5,3,4,2,1,0:T(8,128)(2,1)}, bf16[1,1,1,128,2,1024]{5,3,4,2,1,0:T(8,128)(2,1)}, u32[]{:S(2)}, u32[]{:S(2)}) collective-permute-start(bf16[1,1,1,128,2,1024]{5,3,4,2,1,0:T(8,128)(2,1)} %constant_dynamic-slice_fusion.20), channel_id=1, source_target_pairs={{0,1},{1,0},{2,3},{3,2},{4,5},{5,4},{6,7},{7,6},{8,9},{9,8},{10,11... | collective-permute-start | bytes 1572872 | tf_op jit(solution)/shard_map/ppermute | solution.py:36
  940.4 29.7 %collective-permute-start.114 = (bf16[1,1,1,128,2,1024]{5,3,4,2,1,0:T(8,128)(2,1)}, bf16[1,1,1,128,2,1024]{5,3,4,2,1,0:T(8,128)(2,1)}, u32[]{:S(2)}, u32[]{:S(2)}) collective-permute-start(bf16[1,1,1,128,2,1024]{5,3,4,2,1,0:T(8,128)(2,1)} %constant_dynamic-slice_fusion.30), channel_id=1, source_target_pairs={{0,1},{1,0},{2,3},{3,2},{4,5},{5,4},{6,7},{7,6},{8,9},{9,8},{10,11... | collective-permute-start | bytes 1572872 | tf_op jit(solution)/shard_map/ppermute | solution.py:36
  952.9 129.6 %collective-permute-start.103 = (bf16[1,1,2,128,3,1024]{5,3,4,2,1,0:T(8,128)(2,1)}, bf16[1,1,2,128,3,1024]{5,3,4,2,1,0:T(8,128)(2,1)S(1)}, u32[]{:S(2)}, u32[]{:S(2)}) collective-permute-start(bf16[1,1,2,128,3,1024]{5,3,4,2,1,0:T(8,128)(2,1)} %bitcast.1434), channel_id=1, source_target_pairs={{0,2},{1,3},{2,0},{3,1},{4,6},{5,7},{6,4},{7,5},{8,10},{9,11},{10,... | collective-permute-start | bytes 4718600 | tf_op jit(solution)/shard_map/ppermute | solution.py:36
  962.9 44.8 %collective-permute-start.99 = (bf16[2,1,1,128,1,1024]{5,3,0,4,2,1:T(8,128)(2,1)}, bf16[2,1,1,128,1,1024]{5,3,0,4,2,1:T(8,128)(2,1)S(1)}, u32[]{:S(2)}, u32[]{:S(2)}) collective-permute-start(bf16[2,1,1,128,1,1024]{5,3,0,4,2,1:T(8,128)(2,1)} %constant_dynamic-slice_fusion.45), channel_id=1, source_target_pairs={{0,2},{1,3},{2,0},{3,1},{4,6},{5,7},{6,4},{7,5},{8,10},{9,11},{10,... | collective-permute-start | bytes 1572872 | tf_op jit(solution)/shard_map/ppermute | solution.py:36
  965.3 52.1 %collective-permute-start.94 = (bf16[2,1,1,128,1,1024]{5,3,0,4,2,1:T(8,128)(2,1)S(1)}, bf16[2,1,1,128,1,1024]{5,3,0,4,2,1:T(8,128)(2,1)S(1)}, u32[]{:S(2)}, u32[]{:S(2)}) collective-permute-start(bf16[2,1,1,128,1,1024]{5,3,0,4,2,1:T(8,128)(2,1)S(1)} %copy-done.157), channel_id=1, source_target_pairs={{0,2},{1,3},{2,0},{3,1},{4,6},{5,7},{6,4},{7,5},{8,10},{9,11},{10,... | collective-permute-start | bytes 1572872 | tf_op jit(solution)/shard_map/ppermute | solution.py:36
  967.7 49.9 %collective-permute-start.89 = (bf16[1,1,1,128,2,1024]{5,3,4,2,1,0:T(8,128)(2,1)S(1)}, bf16[1,1,1,128,2,1024]{5,3,4,2,1,0:T(8,128)(2,1)S(1)}, u32[]{:S(2)}, u32[]{:S(2)}) collective-permute-start(bf16[1,1,1,128,2,1024]{5,3,4,2,1,0:T(8,128)(2,1)S(1)} %copy-done.156), channel_id=1, source_target_pairs={{0,1},{1,0},{2,3},{3,2},{4,5},{5,4},{6,7},{7,6},{8,9},{9,8},{10,11... | collective-permute-start | bytes 1572872 | tf_op jit(solution)/shard_map/ppermute | solution.py:36
  970.1 49.8 %collective-permute-start.84 = (bf16[1,1,1,128,2,1024]{5,3,4,2,1,0:T(8,128)(2,1)S(1)}, bf16[1,1,1,128,2,1024]{5,3,4,2,1,0:T(8,128)(2,1)S(1)}, u32[]{:S(2)}, u32[]{:S(2)}) collective-permute-start(bf16[1,1,1,128,2,1024]{5,3,4,2,1,0:T(8,128)(2,1)S(1)} %copy-done.155), channel_id=1, source_target_pairs={{0,1},{1,0},{2,3},{3,2},{4,5},{5,4},{6,7},{7,6},{8,9},{9,8},{10,11... | collective-permute-start | bytes 1572872 | tf_op jit(solution)/shard_map/ppermute | solution.py:36
  1037.9 28.0 %collective-permute-start.90 = (bf16[1,64,2,1024]{3,1,2,0:T(8,128)(2,1)S(1)}, bf16[1,64,2,1024]{3,1,2,0:T(8,128)(2,1)S(1)}, u32[]{:S(2)}, u32[]{:S(2)}) collective-permute-start(bf16[1,64,2,1024]{3,1,2,0:T(8,128)(2,1)S(1)} %dynamic-slice_bitcast_fusion.27), channel_id=1, source_target_pairs={{0,8},{1,9},{2,10},{3,11},{4,12},{5,13},{6,14},{7,15},{8,0},{9,1},... | collective-permute-start | bytes 786440 | tf_op jit(solution)/shard_map/ppermute | solution.py:36
  1069.6 28.3 %collective-permute-start.116 = (bf16[1,32,2,1024]{3,1,2,0:T(8,128)(2,1)S(1)}, bf16[1,32,2,1024]{3,1,2,0:T(8,128)(2,1)S(1)}, u32[]{:S(2)}, u32[]{:S(2)}) collective-permute-start(bf16[1,32,2,1024]{3,1,2,0:T(8,128)(2,1)S(1)} %dynamic-slice_bitcast_fusion.36), channel_id=1, source_target_pairs={{0,16},{1,17},{2,18},{3,19},{4,20},{5,21},{6,22},{7,23},{8,24},{9,... | collective-permute-start | bytes 393224 | tf_op jit(solution)/shard_map/ppermute | solution.py:36
  1133.0 45.8 %all-to-all-start = ((bf16[8,96,1024]{2,1,0:T(8,128)(2,1)}), bf16[8,96,1024]{2,1,0:T(8,128)(2,1)}, u32[]{:S(2)}, u32[]{:S(2)}) async-start(bf16[8,96,1024]{2,1,0:T(8,128)(2,1)} %reshape.1990), calls=%async_computation | async-start | bytes 3145728 | tf_op jit(solution)/shard_map/all_to_all | solution.py:406
  (347 other events, 4108.2 us)

commit v2 on v1

v2 whole, which is shorter than its diff:
```python
import jax
import jax.numpy as jnp
from jax import lax
from jax.experimental import pallas as pl
from jax.experimental.pallas import tpu as pltpu
from jax.sharding import Mesh
from jax.sharding import PartitionSpec as P

D = 1024
HEADS = 8
FF = 4096
KERNEL = 5
LENGTH = 512
HEAD = 128

EPS_NORM = 1e-05
EPS_ADAM = 1e-08
LEARN_RATE = 0.02
SMALL_RATE = 0.3
DECAY_WEIGHT = 0.01
BETA_DECAY = 0.5
MASKED = -1000000000.0
DP = ("dpz", "core")
AXES = (*DP, "fsdp")
BF = jnp.bfloat16
F32 = jnp.float32


def bits_of(size):
    return [1 << k for k in range(size.bit_length() - 1)]


def swap(value, dp_mask, fsdp_mask):
    n_dp, n_fsdp = lax.axis_size(DP), lax.axis_size("fsdp")
    pairs = [
        (d * n_fsdp + f, (d ^ dp_mask) * n_fsdp + (f ^ fsdp_mask))
        for d in range(n_dp)
        for f in range(n_fsdp)
    ]
    return lax.ppermute(value, AXES, pairs)


def swap_core(value):
    return swap(value, 1, 0)


def total(value):
    for mask in bits_of(lax.axis_size("fsdp")):
        value = value + swap(value, 0, mask)
    for mask in bits_of(lax.axis_size(DP)):
        value = value + swap(value, mask, 0)
    return value


class Route:
    def __init__(self, axis, flip):
        self.axis = axis
        if axis == "fsdp":
            self.size = lax.axis_size("fsdp")
            self.here = lax.axis_index("fsdp").astype(jnp.int32)
        else:
            self.size = lax.axis_size(DP) // 2
            self.here = lax.axis_index(DP).astype(jnp.int32) // 2
        self.bits = bits_of(self.size)
        if flip:
            self.bits = self.bits[::-1]
        self.differ = [0]
        for bit in self.bits[::-1]:
            self.differ = self.differ + [held | bit for held in self.differ]

    def trade(self, value, step):
        bit = self.bits[step]
        return swap(value, 0, bit) if self.axis == "fsdp" else swap(value, 2 * bit, 0)

    def indices(self):
        return self.here ^ jnp.array(self.differ, jnp.int32)


def after(value, *earlier):
    return lax.optimization_barrier((value, *earlier))[0]


def pick(value, axis, index):
    return lax.dynamic_index_in_dim(value, index, axis, keepdims=False)


def norm_apply(values, scale_row, shift_row):
    average = jnp.mean(values, axis=-1, keepdims=True)
    centered = values - average
    variance = jnp.mean(centered * centered, axis=-1, keepdims=True)
    return centered * lax.rsqrt(variance + EPS_NORM) * scale_row + shift_row


def swish(values):
    return values * jax.nn.sigmoid(values)


def depthwise(gated_rows, kernel_taps, segment_ids):
    length = gated_rows.shape[1]
    margin = KERNEL // 2
    padded = jnp.pad(gated_rows, ((0, 0), (margin, margin), (0, 0)))
    segment_pad = jnp.pad(segment_ids, ((0, 0), (margin, margin)), constant_values=-1)
    summed = jnp.zeros_like(gated_rows)
    for offset in range(KERNEL):
        matched = (segment_pad[:, offset : offset + length] == segment_ids)[:, :, None]
        summed = summed + kernel_taps[offset] * jnp.where(
            matched, padded[:, offset : offset + length], 0.0
        )
    return summed


def slot_tables(owners, groups, count_blocks):
    capacity = (count_blocks + groups - 1) // groups
    block_index = jnp.arange(count_blocks, dtype=jnp.int32)
    earlier = (owners[None, :] == owners[:, None]) & (block_index[None, :] < block_index[:, None])
    ranking = jnp.sum(earlier.astype(jnp.int32), axis=1)
    slot_of = owners * capacity + ranking
    return slot_of[None, :] == jnp.arange(capacity * groups, dtype=jnp.int32)[:, None]


def gated_conv(pre_a, pre_g, kernel_taps, segment_ids):
    rows_here = segment_ids.shape[0]
    gated_rows = pre_a * jax.nn.sigmoid(pre_g)
    shaped = gated_rows.reshape(rows_here, -1, gated_rows.shape[-1])
    return depthwise(shaped, kernel_taps, segment_ids).reshape(gated_rows.shape)


def masked_scores(queries, keys_row, segment_row):
    scores = jnp.einsum("qhe,khe->hqk", queries, keys_row, preferred_element_type=F32)
    matched = (segment_row[:, None] == segment_row[None, :])[None]
    return jnp.where(matched, scores, MASKED)


def attend_forward(arrays):
    queries, keys_row, values_row, segment_row = arrays
    scores = masked_scores(queries, keys_row, segment_row)
    highest = jnp.max(scores, axis=-1, keepdims=True)
    exponent = jnp.exp(scores - highest)
    summed = jnp.sum(exponent, axis=-1, keepdims=True)
    attention = (exponent / summed).astype(BF)
    context = jnp.einsum("hqk,khe->qhe", attention, values_row, preferred_element_type=F32)
    return (context, (highest + jnp.log(summed))[..., 0])


def attend_backward(arrays):
    queries, keys_row, values_row, segment_row, log_total, context_grad = arrays
    scores = masked_scores(queries, keys_row, segment_row)
    attention = jnp.exp(scores - log_total[..., None])
    attention_grad = jnp.einsum(
        "qhe,khe->hqk", context_grad, values_row, preferred_element_type=F32
    )
    score_grad = attention * (
        attention_grad - jnp.sum(attention_grad * attention, axis=-1, keepdims=True)
    )
    score_low = score_grad.astype(BF)
    query_grad = jnp.einsum("hqk,khe->qhe", score_low, keys_row, preferred_element_type=F32)
    key_grad = jnp.einsum("hqk,qhe->khe", score_low, queries, preferred_element_type=F32)
    value_grad = jnp.einsum(
        "hqk,qhe->khe", attention.astype(BF), context_grad, preferred_element_type=F32
    )
    return (query_grad, key_grad, value_grad)


def mm(left, right):
    return jnp.dot(left, right, preferred_element_type=F32)


def mm_t(left, right):
    return lax.dot_general(left, right, (((1,), (1,)), ((), ())), preferred_element_type=F32)


def t_mm(left, right):
    return lax.dot_general(left, right, (((0,), (0,)), ((), ())), preferred_element_type=F32)


def interleave(side, shard, fetched, arrived, local):
    count, n_shards, size, _ = fetched.shape

    def kernel(at_ref, fetched_ref, arrived_ref, local_ref, out_ref):
        near, here = at_ref[0], at_ref[1]
        for i in range(n_shards):
            at = pl.multiple_of((2 * i + near) * size, size)
            out_ref[0, pl.ds(at, size), :] = fetched_ref[0, i]
            at = pl.multiple_of((2 * (here ^ i) + 1 - near) * size, size)
            out_ref[0, pl.ds(at, size), :] = arrived_ref[0, i - 1] if i else local_ref[0]

    return pl.pallas_call(
        kernel,
        grid_spec=pltpu.PrefetchScalarGridSpec(
            num_scalar_prefetch=1,
            grid=(count,),
            in_specs=[
                pl.BlockSpec((1, n_shards, size, D), lambda b, s: (b, 0, 0, 0)),
                pl.BlockSpec((1, n_shards - 1, size, D), lambda b, s: (b, 0, 0, 0)),
                pl.BlockSpec((1, size, D), lambda b, s: (b, 0, 0)),
            ],
            out_specs=pl.BlockSpec((1, D, D), lambda b, s: (b, 0, 0)),
        ),
        out_shape=jax.ShapeDtypeStruct((count, D, D), BF),
        cost_estimate=pl.CostEstimate(
            flops=0, bytes_accessed=count * 4 * D * D, transcendentals=0
        ),
        name="interleave",
    )(jnp.stack([side, shard]), fetched, arrived, local)


def deal(chosen, used, parts):
    n_slots = chosen.shape[0]
    sizes = [part.shape[0] for part in parts]

    def kernel(chosen_ref, used_ref, *refs):
        *part_refs, out_ref, all_ref = refs
        at = 0
        for ref, size in zip(part_refs, sizes):
            all_ref[at : at + size] = ref[...]
            at += size
        for slot in range(n_slots):
            held = all_ref[chosen_ref[slot]].astype(F32)
            out_ref[slot] = (held * used_ref[slot].astype(F32)).astype(BF)

    return pl.pallas_call(
        kernel,
        in_specs=[pl.BlockSpec(memory_space=pltpu.SMEM)] * 2
        + [pl.BlockSpec(memory_space=pltpu.VMEM)] * len(parts),
        out_specs=pl.BlockSpec(memory_space=pltpu.VMEM),
        out_shape=jax.ShapeDtypeStruct((n_slots, *parts[0].shape[1:]), BF),
        scratch_shapes=[pltpu.VMEM((sum(sizes), *parts[0].shape[1:]), BF)],
        name="deal",
    )(chosen, used, *parts)


def regroup(starts, value, act=False, blocks=None):
    tokens = value.shape[0]
    blocks = list(range(value.shape[1] // D)) if blocks is None else blocks
    base, stride = blocks[0], (blocks[1] - blocks[0] if len(blocks) > 1 else 1)
    n_blocks = len(blocks)
    n_chunks = starts.shape[0]
    size = D // n_chunks
    if size % 128:
        value = jnp.concatenate([value[:, j * D : (j + 1) * D] for j in blocks], axis=1)
        value = swish(value.astype(F32)).astype(BF) if act else value
        split = value.reshape(tokens, n_blocks, n_chunks, size)
        return jnp.concatenate(
            [
                lax.dynamic_index_in_dim(split, starts[q], 2, keepdims=False).reshape(tokens, -1)
                for q in range(n_chunks)
            ],
            axis=1,
        )

    def kernel(starts_ref, value_ref, out_ref):
        block = pl.program_id(0)
        for place in range(n_chunks):
            at = pl.multiple_of(starts_ref[place] * size, size)
            held = value_ref[:, pl.ds(at, size)]
            if act:
                held = swish(held.astype(F32)).astype(BF)
            to = pl.multiple_of((place * n_blocks + block) * size, size)
            out_ref[:, pl.ds(to, size)] = held

    return pl.pallas_call(
        kernel,
        grid_spec=pltpu.PrefetchScalarGridSpec(
            num_scalar_prefetch=1,
            grid=(n_blocks,),
            in_specs=[pl.BlockSpec((tokens, D), lambda b, s: (0, base + stride * b))],
            out_specs=pl.BlockSpec((tokens, n_blocks * D), lambda b, s: (0, 0)),
        ),
        out_shape=jax.ShapeDtypeStruct((tokens, n_blocks * D), BF),
        cost_estimate=pl.CostEstimate(
            flops=0, bytes_accessed=4 * tokens * n_blocks * D, transcendentals=0
        ),
        name="regroup",
    )(starts, value)


def run(*tasks):
    got = [None] * len(tasks)
    left = list(tasks)
    while left:
        going, wants = [], []
        for task, arrived in zip(left, got):
            try:
                wants.append(task.send(arrived))
                going.append(task)
            except StopIteration:
                pass
        left, got = going, wants


def fetch(route, own, sink):
    sink[0] = own
    for step in range(len(route.bits)):
        known = list(sink)
        got = yield [route.trade(sink[place], step) for place in known]
        for place, piece in zip(known, got):
            sink[place + (route.size >> (step + 1))] = piece


def low_add(left, right):
    return (left.astype(F32) + right.astype(F32)).astype(BF)


def halve(route, kept, sent, sink, name):
    for step in range(len(route.bits)):
        arrived = yield route.trade(sent, step)
        if step + 1 == len(route.bits):
            sink[name] = kept + arrived.astype(F32) if kept.dtype == F32 else low_add(kept, arrived)
            return
        part = kept.shape[0] // 2
        sent = low_add(kept[part:], arrived[part:])
        kept = kept[:part].astype(F32) + arrived[:part].astype(F32) if kept.dtype == F32 else low_add(
            kept[:part], arrived[:part]
        )


def halve_dp(route, held, sink, name):
    count, sides, rows, _ = held.shape
    piece = rows // route.size
    core = lax.axis_index(DP) % 2
    indices = route.indices()
    parts = [
        lax.dynamic_slice(held, (0, 0, indices[place] * piece, 0), (count, sides, piece, D))
        for place in range(route.size)
    ]
    middle = route.size // 2
    yield from halve(route, jnp.stack(parts[:middle]), jnp.stack(parts[middle:]), sink, name)
    held = sink[name][0]
    if sides == 1:
        sink[name] = held[:, 0]
        return
    arrived = yield swap_core(pick(held, 1, 1 - core))
    sink[name] = [pick(held, 1, core), arrived]


def both(value):
    return jnp.concatenate([value, swap_core(value)], axis=0)


def across(partial):
    tokens = partial.shape[0] // 2
    return partial[:tokens] + swap_core(partial[tokens:])


def per_device(
    frames,
    segment_ids,
    out_grad,
    blocks,
    small_params,
    owners,
    left_bases,
    right_bases,
    block_first,
    block_second,
    small_first,
    small_second,
):
    rows_here = frames.shape[0]
    tokens = rows_here * LENGTH
    n_blocks = blocks.shape[0]
    rows_own = blocks.shape[1]
    scale_head = HEAD ** (-0.5)
    n_dp = lax.axis_size(DP)
    n_fsdp = lax.axis_size("fsdp")
    mine = lax.axis_index("fsdp")
    count_all = tokens * n_dp * n_fsdp
    core = lax.axis_index("core").astype(jnp.int32)
    dpz = lax.axis_index("dpz").astype(jnp.int32)
    fsdp = lax.axis_index("fsdp").astype(jnp.int32)
    half = rows_own // 2
    per_in = FF // D
    per_core = per_in // 2
    base_attn = 2 * per_in
    base_last = base_attn + 7
    routes = [Route("fsdp", False), Route("fsdp", True)]
    routes_dp = [Route("dp", False), Route("dp", True)]
    shards = [route.indices() for route in routes]

    def rows_of(low, count, side, size):
        return lax.dynamic_slice(blocks, (low, side * size, 0), (count, size, D)).astype(BF)

    def fetch_own(base):
        own = [rows_of(base + k * per_in + core * per_core, per_core, 0, rows_own) for k in (0, 1)]
        fetched = lax.all_gather(jnp.concatenate(own, axis=0), "fsdp", axis=1, tiled=True)
        return [fetched[j] for j in range(2 * per_core)]

    def fetch_shared(base):
        side = dpz % 2
        listed = []
        for k in (0, 1):
            at = base + k * per_in + core * per_core
            listed.append([rows_of(at, per_core, held, half) for held in (side, 1 - side)])
        own = jnp.concatenate([held for held, _ in listed], axis=0)
        fetched = lax.all_gather(own, "fsdp", axis=1, tiled=True)
        fetched = fetched.reshape(2, per_core, n_fsdp, half, D)
        result = []
        for k in (0, 1):
            away = jnp.stack(
                [pick(fetched[k], 1, shard) for shard in [fsdp ^ i for i in range(1, n_fsdp)]], axis=1
            )
            arrived = swap(away, 2, 0)
            result.append(interleave(side, fsdp, fetched[k], arrived, listed[k][1]))
        return [held[j] for held in result for j in range(per_core)]

    def fetch_half(low, high):
        own = rows_of(low, high - low, core, half)
        return lax.all_gather(own, ("fsdp", "core"), axis=1, tiled=True)

    gains = small_params[0:5]
    shifts = small_params[5:10]
    bn_gain = small_params[10]
    bn_shift = small_params[11]
    kernel_taps = small_params[12 : 12 + KERNEL]

    def feed_up(hidden, index, weights):
        normed, pullback = jax.vjp(norm_apply, hidden, gains[index], shifts[index])
        pair = both(normed.astype(BF))
        return [mm(pair, weights[j]).astype(BF) for j in range(per_core)], pullback, pair

    def feed_down(hidden, lifted, weights):
        acted = [swish(up.astype(F32)).astype(BF) for up in lifted]
        result = across(sum(mm(acted[j], weights[per_core + j]) for j in range(per_core)))
        return hidden + 0.5 * result, acted

    def feed_back(gradient, lifted, acted, normed_pair, weights):
        pair = both((0.5 * gradient).astype(BF))
        lows, grads_in, grads_out = [], [], []
        for j in range(per_core):
            acted_grad = mm_t(pair, weights[per_core + j])
            up = lifted[j].astype(F32)
            gate = jax.nn.sigmoid(up)
            lows.append((acted_grad * (gate * (1.0 + up * (1.0 - gate)))).astype(BF))
        normed_grad = across(sum(mm_t(lows[j], weights[j]) for j in range(per_core)))
        for j in range(per_core):
            grads_out.append(t_mm(acted[j], pair).astype(BF))
            grads_in.append(t_mm(normed_pair, lows[j]).astype(BF))
        listed = [held.reshape(n_fsdp, rows_own, D) for held in grads_in + grads_out]
        return normed_grad, jnp.stack(listed, axis=1)

    last = []

    def scatter(stacked):
        if last:
            stacked = after(stacked, last[-1])
        summed = lax.psum_scatter(stacked, "fsdp", scatter_dimension=0, tiled=True)
        last.append(lax.optimization_barrier(summed))
        return last[-1][0]

    def share(products, along_z):
        pieces = n_dp // 2
        shape = (n_fsdp, 2, pieces // 2, 2, half // pieces, D)
        split = [held.astype(BF).reshape(shape) for held in products]
        away = jnp.stack([pick(held, 1, 1 - core) for held in split], axis=1)
        arrived = swap_core(away)
        if not along_z:
            kept = jnp.stack([pick(held, 1, core) for held in split], axis=1)
            return low_add(kept, arrived).reshape(n_fsdp, len(split), half, D)
        side = dpz % 2

        def summed(which):
            kept = jnp.stack([pick(pick(held, 1, core), 2, which) for held in split], axis=1)
            return low_add(kept, pick(arrived, 3, which))

        sent, kept = summed(1 - side), summed(side)
        return low_add(kept, swap(sent, 2, 0))

    def spread_shared(held, name):
        for bit in bits_of(n_dp // 2)[1:]:
            count, left, rows, _ = held.shape
            parted = held.reshape(count, left // 2, 2, rows, D)
            which = (dpz // bit) % 2
            arrived = swap(pick(parted, 2, 1 - which), 2 * bit, 0)
            held = low_add(pick(parted, 2, which), arrived)
        sums[name] = held[:, 0]

    def spread_dp(held, sides, name):
        middle = (held.shape[0] + 1) // 2
        tasks = []
        for route, part, place in zip(routes_dp, (held[:middle], held[middle:]), "xy"):
            shaped = part.reshape(part.shape[0], sides, half, D)
            tasks.append(halve_dp(route, shaped, sums, name + place))
        run(*tasks)

    sums = {}
    weights1 = fetch_shared(0)
    weights_middle = fetch_half(base_attn, base_last)
    weights2 = fetch_own(base_last)
    w_attn, w_conv = weights_middle[:4], weights_middle[4:]
    start_x = frames.astype(F32).reshape(tokens, D)
    lifted1, ffn1_pullback, normed_pair1 = feed_up(start_x, 0, weights1)
    first_x, acted1 = feed_down(start_x, lifted1, weights1)
    normed, attn_pullback = jax.vjp(norm_apply, first_x, gains[1], shifts[1])
    attn_low = normed.astype(BF)
    split_shape = (rows_here, LENGTH, HEADS, HEAD)
    queries = (mm(attn_low, w_attn[0]) * scale_head).astype(BF).reshape(split_shape)
    keys_all = mm(attn_low, w_attn[1]).astype(BF).reshape(split_shape)
    values_all = mm(attn_low, w_attn[2]).astype(BF).reshape(split_shape)
    context, log_total = lax.map(attend_forward, (queries, keys_all, values_all, segment_ids))
    context_low = context.reshape(tokens, D).astype(BF)
    second_x = first_x + mm(context_low, w_attn[3])
    normed, conv_pullback = jax.vjp(norm_apply, second_x, gains[2], shifts[2])
    conv_low = normed.astype(BF)
    convolved, gated_pullback = jax.vjp(
        lambda pre_a, pre_g, taps_in: gated_conv(pre_a, pre_g, taps_in, segment_ids),
        mm(conv_low, w_conv[0]),
        mm(conv_low, w_conv[1]),
        kernel_taps,
    )
    stats = jnp.stack([jnp.sum(convolved, axis=0), jnp.sum(convolved * convolved, axis=0)])
    stats = total(stats)
    average = stats[0] / count_all
    inverse_dev = lax.rsqrt(stats[1] / count_all - average * average + EPS_NORM)
    standard = (convolved - average) * inverse_dev
    activated, bn_swish_pullback = jax.vjp(swish, standard * bn_gain + bn_shift)
    activated_low = activated.astype(BF)
    third_x = second_x + mm(activated_low, w_conv[2])
    lifted2, ffn2_pullback, normed_pair2 = feed_up(third_x, 3, weights2)
    fourth_x, acted2 = feed_down(third_x, lifted2, weights2)
    layer_value, final_pullback = jax.vjp(norm_apply, fourth_x, gains[4], shifts[4])
    layer_out = layer_value.astype(BF).reshape(rows_here, LENGTH, D)

    grad_x, final_gain, final_shift = final_pullback(out_grad.astype(F32).reshape(tokens, D))
    normed_grad, stacked = feed_back(grad_x, lifted2, acted2, normed_pair2, weights2)
    hidden_grad, ffn2_gain, ffn2_shift = ffn2_pullback(normed_grad)
    grad_x = grad_x + hidden_grad
    branch_low = grad_x.astype(BF)
    (bn_grad,) = bn_swish_pullback(mm_t(branch_low, w_conv[2]))
    bn_sums = jnp.stack([jnp.sum(bn_grad, axis=0), jnp.sum(bn_grad * standard, axis=0)])
    bn_sums = total(bn_sums)
    summed2 = scatter(stacked)
    grad_back = t_mm(activated_low, branch_low)
    shift_sum, gain_sum = bn_sums[0], bn_sums[1]
    conv_grad = (
        bn_gain
        * inverse_dev
        * (bn_grad - shift_sum / count_all - standard * (gain_sum / count_all))
    )
    grad_a, grad_g, taps_grad = gated_pullback(conv_grad)
    grad_a, grad_g = grad_a.astype(BF), grad_g.astype(BF)
    shared_conv = share([t_mm(conv_low, grad_a), t_mm(conv_low, grad_g), grad_back], False)
    summed_conv = scatter(shared_conv)
    part_x, conv_gain, conv_shift = conv_pullback(
        mm_t(grad_a, w_conv[0]) + mm_t(grad_g, w_conv[1])
    )
    grad_x = grad_x + part_x
    branch_low = grad_x.astype(BF)
    context_grad = mm_t(branch_low, w_attn[3]).astype(BF).reshape(split_shape)
    query_grad, key_grad, value_grad = lax.map(
        attend_backward, (queries, keys_all, values_all, segment_ids, log_total, context_grad)
    )
    query_low = (query_grad.reshape(tokens, D) * scale_head).astype(BF)
    key_low = key_grad.reshape(tokens, D).astype(BF)
    value_low = value_grad.reshape(tokens, D).astype(BF)
    grad_heads = [t_mm(attn_low, held) for held in (query_low, key_low, value_low)]
    shared_attn = share([*grad_heads, t_mm(context_low, branch_low)], True)
    part_x, attn_gain, attn_shift = attn_pullback(
        mm_t(query_low, w_attn[0]) + mm_t(key_low, w_attn[1]) + mm_t(value_low, w_attn[2])
    )
    grad_x = grad_x + part_x
    normed_grad, stacked = feed_back(grad_x, lifted1, acted1, normed_pair1, weights1)
    summed1 = scatter(stacked)
    summed_attn = scatter(shared_attn)
    hidden_grad, ffn1_gain, ffn1_shift = ffn1_pullback(normed_grad)
    grad_x = grad_x + hidden_grad
    frames_grad = grad_x.reshape(rows_here, LENGTH, D)
    local_small = jnp.concatenate(
        [
            jnp.stack([ffn1_gain, attn_gain, conv_gain, ffn2_gain, final_gain]),
            jnp.stack([ffn1_shift, attn_shift, conv_shift, ffn2_shift, final_shift]),
            taps_grad,
        ],
        axis=0,
    )
    spread_dp(summed2, 2, "ffn2")
    spread_dp(summed_conv, 1, "conv")
    summed1 = after(summed1, *[sums[name + place] for name in ("ffn2", "conv") for place in "xy"])
    spread_dp(summed1, 2, "ffn1")
    summed_attn = after(summed_attn, *[sums["ffn1" + place] for place in "xy"])
    spread_shared(summed_attn, "attn")
    summed_small = total(local_small)
    small_grads = jnp.concatenate(
        [summed_small[0:10], gain_sum[None], shift_sum[None], summed_small[10:]], axis=0
    )

    parts, places = [], []
    for name in ("ffn1", "middle", "ffn2"):
        base = sum(part.shape[0] for part in parts)
        if name == "middle":
            parts += [sums["attn"], sums["convx"], sums["convy"]]
            places.append(base + jnp.arange(base_last - base_attn, dtype=jnp.int32))
            continue
        (in_mine, in_other), (out_mine, out_other) = sums[name + "x"], sums[name + "y"]
        parts += [in_mine, out_mine, in_other, out_other]
        index = jnp.arange(2 * per_in, dtype=jnp.int32)
        is_out, index = index // per_in, index % per_in
        away = (index // per_core != core).astype(jnp.int32)
        places.append(base + (2 * away + is_out) * per_core + index % per_core)
    places = jnp.concatenate(places)
    capacity = (n_blocks + n_dp - 1) // n_dp
    matches = slot_tables(owners, n_dp, n_blocks).astype(jnp.int32)
    slot_block = jnp.sum(matches * jnp.arange(n_blocks, dtype=jnp.int32)[None], axis=1)
    slot_used = jnp.sum(matches, axis=1)
    piece = half // (n_dp // 2)
    slot_place = jnp.sum(matches * places[None], axis=1)
    sent = deal(slot_place, slot_used, parts).reshape(n_dp, capacity, piece, D)
    came = lax.all_to_all(sent, DP, 0, 0, tiled=False)
    came = came.reshape(n_dp // 2, 2, capacity, piece, D).transpose(2, 1, 0, 3, 4)
    owned_list = came.reshape(capacity, rows_own, D)

    dp_here = lax.axis_index(DP)
    my_blocks = lax.dynamic_slice_in_dim(slot_block, dp_here * capacity, capacity)
    my_used = lax.dynamic_slice_in_dim(slot_used, dp_here * capacity, capacity).astype(F32)
    rotated_list, weight_list = [], []
    sides = [slice(0, D // 2), slice(D // 2, D)]
    for slot in range(capacity):
        right_basis = right_bases[slot].astype(BF)
        left_low = left_bases[slot].astype(BF)
        lefts = [regroup(held, left_low) for held in shards]
        product = mm(owned_list[slot], right_basis).astype(BF)
        sink = {}
        run(
            *[
                halve(
                    routes[i],
                    t_mm(lefts[i][:, : D // 2], product[:, sides[i]]),
                    t_mm(lefts[i][:, D // 2 :], product[:, sides[i]]).astype(BF),
                    sink,
                    i,
                )
                for i in (0, 1)
            ]
        )
        sinks = [{}, {}]
        tasks = []
        for i in (0, 1):
            first_step = 0.5 * block_first[slot][:, sides[i]] + 0.5 * sink[i]
            second_step = 0.5 * block_second[slot][:, sides[i]] + 0.5 * sink[i] * sink[i]
            direction = (first_step / (jnp.sqrt(second_step) + EPS_ADAM)).astype(BF)
            tasks.append(fetch(routes[i], direction, sinks[i]))
        run(*tasks)
        rotated_list.append(jnp.concatenate([sink[0], sink[1]], axis=1))
        mixed = [
            mm(
                lefts[i], jnp.concatenate([sinks[i][place] for place in range(n_fsdp)], axis=0)
            ).astype(BF)
            for i in (0, 1)
        ]
        update = mm_t(jnp.concatenate(mixed, axis=1), right_basis)
        master = pick(blocks, 0, my_blocks[slot])
        weight_list.append(master - LEARN_RATE * (update + DECAY_WEIGHT * master))
    used = my_used[:, None, None]
    rotated = jnp.stack(rotated_list)
    first_step = BETA_DECAY * block_first + (1.0 - BETA_DECAY) * rotated
    second_step = BETA_DECAY * block_second + (1.0 - BETA_DECAY) * rotated * rotated
    small_first_new = BETA_DECAY * small_first + (1.0 - BETA_DECAY) * small_grads
    small_second_new = BETA_DECAY * small_second + (1.0 - BETA_DECAY) * small_grads * small_grads
    small_weights = small_params - SMALL_RATE * small_first_new / (
        jnp.sqrt(small_second_new) + EPS_ADAM
    )
    return (
        layer_out,
        frames_grad,
        owned_list.astype(F32),
        first_step * used,
        second_step * used,
        jnp.stack(weight_list) * used,
        small_grads,
        small_weights,
        small_first_new,
        small_second_new,
    )


def solution(mesh):
    n_dp, n_fsdp = mesh.shape["dp"], mesh.shape["fsdp"]
    finer = Mesh(mesh.devices.reshape(n_dp // 2, 2, n_fsdp), AXES)
    placed = (
        P(AXES, None, None),
        P(AXES, None),
        P(AXES, None, None),
        P(None, "fsdp", None),
        P(),
        P(),
        P(DP, "fsdp", None),
        P(DP, None, None),
        P(DP, "fsdp", None),
        P(DP, "fsdp", None),
        P(),
        P(),
    )
    return jax.shard_map(
        per_device,
        mesh=finer,
        in_specs=placed,
        out_specs=(
            P(AXES, None, None),
            P(AXES, None, None),
            P(DP, "fsdp", None),
            P(DP, "fsdp", None),
            P(DP, "fsdp", None),
            P(DP, "fsdp", None),
            P(),
            P(),
            P(),
            P(),
        ),
        check_vma=False,
    )
```

time: 1320 us -> 849 us (0.64)
  local copies, waits for them, and re-layouts: 479 us -> 91.8 us
  matrix products: 244 us -> 175 us
  starting transfers between devices: 143 us -> 91.1 us
  Pallas kernels: 0 us -> 27.4 us
  between operations: 11 us -> 28.5 us
    dynamic_update_slice x95 -> x0, local copies, waits for them, and re-layouts: 133 us -> none  [chunk(): lax.dynamic_update_slice(full, held[:, None, None], (0, at, side, 0, 0))]
    ppermute x177 -> x75, waiting for transfers between devices: 335 us -> 243 us  [swap(): return lax.ppermute(value, AXES, pairs)]
    all_gather x0 -> x3, waiting for transfers between devices: none -> 77.7 us  [the longest x1 50.6 us: fetch_shared(): fetched = lax.all_gather(own, 'fsdp', axis=1, tiled=True)]
    dynamic_slice x36 -> x8, local copies, waits for them, and re-layouts: 78.6 us -> 2.74 us  [pick(): return lax.dynamic_index_in_dim(value, index, axis, keepdims=False)]
    reshape x17 -> x1, local copies, waits for them, and re-layouts: 61.4 us -> 1.55 us  [per_device(): came.reshape(n_dp // 2, 2, capacity, piece, D).transpose(2, 1, 0, 3, 4)]
    ppermute x177 -> x75, starting transfers between devices: 138 us -> 86.2 us  [swap(): return lax.ppermute(value, AXES, pairs)]
    unnamed x496 -> x350, local copies, waits for them, and re-layouts: 93.4 us -> 43.4 us
    dot_general x8 -> x0, matrix products: 49.4 us -> none  [the longest x4 25.6 us: feed_forward(): up = jnp.einsum('td,jdh->tjh', normed_low, part, preferred_element_type=F32)]
  transfers between devices with their start and end apart: 178 -> 83, of which waited for: 60 -> 47; matrix products, arithmetic and copies ran while one was open for 54% -> 32% of each run, Pallas kernels for 0% -> 3%
where the time goes in v2:
time: 849 us; the launch traced here: 843 us
  waiting for transfers between devices  332 us (39%)
  matrix products  175 us (21%)
  other arithmetic  97.3 us (11%)
  local copies, waits for them, and re-layouts  91.8 us (11%)
  starting transfers between devices  91.1 us (11%)
  between operations  28.5 us (3%)
  Pallas kernels  27.4 us (3%)
    ppermute x75, waiting for transfers between devices, swap(): return lax.ppermute(value, AXES, pairs)  243 us
    ppermute x75, starting transfers between devices, swap(): return lax.ppermute(value, AXES, pairs)  86.2 us
    dot_general x18, matrix products, mm_t(): lax.dot_general(left, right, (((1,), (1,)), ((), ())), preferred_element_...  60.8 us
    dot_general x24, matrix products, mm(): return jnp.dot(left, right, preferred_element_type=F32)  57.6 us
    all_gather x1, waiting for transfers between devices, fetch_shared(): fetched = lax.all_gather(own, 'fsdp', axis=1, tiled=True)  50.6 us
    dot_general x27, matrix products, t_mm(): lax.dot_general(left, right, (((0,), (0,)), ((), ())), preferred_element_...  45.5 us
    unnamed x350, local copies, waits for them, and re-layouts  43.4 us
    all_gather x1, waiting for transfers between devices, fetch_own(): lax.all_gather(jnp.concatenate(own, axis=0), 'fsdp', axis=1, tiled=True)  27.1 us
  transfers between devices with their start and end apart: 83, of which 47 were waited for; matrix products, arithmetic and copies ran while one was open for 32% of the time, Pallas kernels for 3%

profile of v2, /device:TPU:0, one launch (start us, length us, event | category | flops | bytes accessed | tf_op | source)
XLA Modules:
  0.0 842.9 jit_solution(10130147510640690117)
XLA Ops:
  7.3 3.5 dynamic-slice_convert_fusion.4
  11.9 3.7 dynamic-slice_convert_fusion
  16.8 50.6 %all-gather.4.cloned.1.call-done = bf16[4,512,1024]{2,1,0:T(8,128)(2,1)} async-done(((bf16[4,128,1024]{2,1,0:T(8,128)(2,1)}), bf16[4,512,1024]{2,1,0:T(8,128)(2,1)}) %all-gather.4.cloned.1.call-update) | async-done | bytes 4194320 | tf_op jit(solution)/shard_map/all_gather | solution.py:395
  78.3 31.3 %collective-permute-done.1.arrived_ref = bf16[2,3,128,1024]{3,2,1,0:T(8,128)(2,1)S(1)} collective-permute-done((bf16[2,3,128,1024]{3,2,1,0:T(8,128)(2,1)S(1)}, bf16[2,3,128,1024]{3,2,1,0:T(8,128)(2,1)S(1)}, u32[]{:S(2)}, u32[]{:S(2)}) %collective-permute-start.1) | collective-permute-done | bytes 1572896 | tf_op jit(solution)/shard_map/ppermute | solution.py:40
  110.7 4.4 interleave.2
  115.1 27.1 %collective-permute-done.2.arrived_ref = bf16[2,3,128,1024]{3,2,1,0:T(8,128)(2,1)} collective-permute-done((bf16[2,3,128,1024]{3,2,1,0:T(8,128)(2,1)}, bf16[2,3,128,1024]{3,2,1,0:T(8,128)(2,1)}, u32[]{:S(2)}, u32[]{:S(2)}) %collective-permute-start.2) | collective-permute-done | bytes 1572896 | tf_op jit(solution)/shard_map/ppermute | solution.py:40
  142.2 4.5 interleave.3
  146.7 4.8 convolution_convert_fusion.18
  151.5 4.8 convolution_convert_fusion.17
  174.5 4.5 fusion.105
  181.8 3.8 multiply_convert_fusion.7
  187.2 3.6 fusion.111
  230.1 27.1 %all-gather.8.cloned.1.call-done = bf16[4,1024,1024]{2,1,0:T(8,128)(2,1)} async-done(((bf16[4,256,1024]{2,1,0:T(8,128)(2,1)}), bf16[4,1024,1024]{2,1,0:T(8,128)(2,1)}) %all-gather.8.cloned.1.call-update) | async-done | bytes 8388624 | tf_op jit(solution)/shard_map/all_gather | solution.py:385
  257.2 4.4 convolution_convert_fusion.15
  261.7 4.4 convolution_convert_fusion.16
  288.7 3.4 fusion.35
  292.1 3.8 fusion.27
  308.5 3.6 convolution_convert_fusion.7
  312.1 3.6 convolution_convert_fusion.6
  315.7 4.1 pad_maximum_fusion.1
  319.8 3.4 fusion.322
  327.3 5.9 fusion.325
  343.7 3.4 convolution_convert_fusion.8
  359.9 3.5 fusion.93
  363.5 4.3 multiply_reduce_fusion.3
  371.0 3.9 fusion.104
  389.8 3.1 multiply_convert_fusion
  393.6 3.2 fusion.87
  404.8 3.3 fusion.323
  412.3 3.9 add_convert_fusion
  416.6 5.9 fusion.11
  422.5 4.7 convolution_convert_fusion.14
  427.2 4.8 fusion.19
  432.0 4.7 convolution_convert_fusion.13
  436.7 4.1 convolution_convert_fusion.12
  440.8 3.7 convolution_convert_fusion.11
  444.5 4.0 pad_maximum_fusion
  448.5 11.1 %reduce-scatter.15.cloned.1.call-done = bf16[1,3,128,1024]{3,2,1,0:T(8,128)(2,1)} async-done(((bf16[4,3,128,1024]{3,2,1,0:T(8,128)(2,1)}), bf16[1,3,128,1024]{3,2,1,0:T(8,128)(2,1)}) %reduce-scatter.15.cloned.1.call-update) | async-done | bytes 786448
  481.1 4.2 fusion.36
  502.2 41.9 %collective-permute-done.24 = bf16[2,2,2,32,1024]{4,3,2,1,0:T(8,128)(2,1)S(1)} collective-permute-done((bf16[2,2,2,32,1024]{4,3,2,1,0:T(8,128)(2,1)S(1)}, bf16[2,2,2,32,1024]{4,3,2,1,0:T(8,128)(2,1)S(1)}, u32[]{:S(2)}, u32[]{:S(2)}) %collective-permute-start.24) | collective-permute-done | bytes 524320 | tf_op jit(solution)/shard_map/ppermute | solution.py:40
  544.2 3.5 collective-permute-start.25
  547.7 3.1 add_convert_fusion.1
  550.8 5.6 collective-permute-done.21
  558.9 6.8 collective-permute-done.25
  570.6 3.8 collective-permute-start.27
  594.0 8.1 collective-permute-start.31
  602.1 9.0 %collective-permute-done.33 = bf16[2,2,2,32,1024]{4,3,2,1,0:T(8,128)(2,1)S(1)} collective-permute-done((bf16[2,2,2,32,1024]{4,3,2,1,0:T(8,128)(2,1)S(1)}, bf16[2,2,2,32,1024]{4,3,2,1,0:T(8,128)(2,1)S(1)}, u32[]{:S(2)}, u32[]{:S(2)}) %collective-permute-start.33) | collective-permute-done | bytes 524320 | tf_op jit(solution)/shard_map/ppermute | solution.py:40
  616.5 3.2 collective-permute-start.32
  620.4 11.3 %collective-permute-done.32 = bf16[1,2,2,32,1024]{4,3,2,1,0:T(8,128)(2,1)S(1)} collective-permute-done((bf16[1,2,2,32,1024]{4,3,2,1,0:T(8,128)(2,1)S(1)}, bf16[1,2,2,32,1024]{4,3,2,1,0:T(8,128)(2,1)S(1)}, u32[]{:S(2)}, u32[]{:S(2)}) %collective-permute-start.32) | collective-permute-done | bytes 262176 | tf_op jit(solution)/shard_map/ppermute | solution.py:40
  636.2 13.1 %collective-permute-done.39 = bf16[4,1,32,1024]{3,2,0,1:T(8,128)(2,1)S(1)} collective-permute-done((bf16[4,1,32,1024]{3,2,0,1:T(8,128)(2,1)S(1)}, bf16[4,1,32,1024]{3,2,0,1:T(8,128)(2,1)S(1)}, u32[]{:S(2)}, u32[]{:S(2)}) %collective-permute-start.39) | collective-permute-done | bytes 262176 | tf_op jit(solution)/shard_map/ppermute | solution.py:40
  653.0 4.4 all-to-all-start
  657.5 3.0 fusion.75
  701.7 3.6 add_bitcast_fusion
  705.3 3.1 copy.173
  711.0 3.1 convolution_convert_fusion.28
  715.8 3.3 convolution_convert_fusion.25
  729.5 7.3 collective-permute-done.42
  741.5 6.6 collective-permute-done.46
  752.7 6.6 collective-permute-done.50
  763.9 3.7 collective-permute-done.43
  789.8 3.9 collective-permute-done.54
  796.8 4.6 collective-permute-done.57
  807.9 7.7 collective-permute-done.60
  831.3 4.5 fusion.44
  (729 shorter events, 353.7 us)
Async XLA Ops:
  7.2 60.2 %all-gather.4.cloned.1.call-start = ((), (), s32[]{:S(2)}) async-start(), calls=%async_computation.5 | async-start | bytes 5242880 | tf_op jit(solution)/shard_map/all_gather | solution.py:395
  11.8 162.7 %all-gather.6.cloned.1.call-start = ((), (), s32[]{:S(2)}) async-start(), calls=%async_computation.6 | async-start | bytes 16515072 | tf_op jit(solution)/shard_map/all_gather | solution.py:408
  15.6 241.6 %all-gather.8.cloned.1.call-start = ((), (), s32[]{:S(2)}) async-start(), calls=%async_computation.7 | async-start | bytes 10485760 | tf_op jit(solution)/shard_map/all_gather | solution.py:385
  72.2 37.3 %collective-permute-start.1 = (bf16[2,3,128,1024]{3,2,1,0:T(8,128)(2,1)S(1)}, bf16[2,3,128,1024]{3,2,1,0:T(8,128)(2,1)S(1)}, u32[]{:S(2)}, u32[]{:S(2)}) collective-permute-start(bf16[2,3,128,1024]{3,2,1,0:T(8,128)(2,1)S(1)} %pad_maximum_fusion.10), channel_id=1, source_target_pairs={{0,8},{1,9},{2,10},{3,11},{4,12},{5,13},{6,14},{7,15},{8,0},{9,1},... | collective-permute-start | bytes 4718600 | tf_op jit(solution)/shard_map/ppermute | solution.py:40
  75.1 67.1 %collective-permute-start.2 = (bf16[2,3,128,1024]{3,2,1,0:T(8,128)(2,1)}, bf16[2,3,128,1024]{3,2,1,0:T(8,128)(2,1)}, u32[]{:S(2)}, u32[]{:S(2)}) collective-permute-start(bf16[2,3,128,1024]{3,2,1,0:T(8,128)(2,1)} %pad_maximum_fusion.11), channel_id=1, source_target_pairs={{0,8},{1,9},{2,10},{3,11},{4,12},{5,13},{6,14},{7,15},{8,0},{9,1},... | collective-permute-start | bytes 4718600 | tf_op jit(solution)/shard_map/ppermute | solution.py:40
  77.7 69.1 %collective-permute-start = (bf16[512,1024]{0,1:T(8,128)(2,1)}, bf16[512,1024]{0,1:T(8,128)(2,1)}, u32[]{:S(2)}, u32[]{:S(2)}) collective-permute-start(bf16[512,1024]{0,1:T(8,128)(2,1)} %fusion.58), channel_id=1, source_target_pairs={{0,4},{1,5},{2,6},{3,7},{4,0},{5,1},{6,2},{7,3},{8,12},{9,13},{10,... | collective-permute-start | bytes 3145736 | tf_op jit(solution)/shard_map/ppermute | solution.py:40
  168.9 247.4 %reduce-scatter.13.cloned.1.call-start = ((), (), s32[]{:S(2)}) async-start(), calls=%async_computation.8 | async-start | bytes 10485760
  230.0 27.2 %collective-permute-start.9 = (bf16[512,1024]{0,1:T(8,128)(2,1)S(1)}, bf16[512,1024]{0,1:T(8,128)(2,1)}, u32[]{:S(2)}, u32[]{:S(2)}) collective-permute-start(bf16[512,1024]{0,1:T(8,128)(2,1)S(1)} %add_convert_fusion.3), channel_id=1, source_target_pairs={{0,4},{1,5},{2,6},{3,7},{4,0},{5,1},{6,2},{7,3},{8,12},{9,13},{10,... | collective-permute-start | bytes 3145736 | tf_op jit(solution)/shard_map/ppermute | solution.py:40
  303.4 16.4 %collective-permute-start.12 = (f32[512,1024]{0,1:T(8,128)}, f32[512,1024]{0,1:T(8,128)}, u32[]{:S(2)}, u32[]{:S(2)}) collective-permute-start(f32[512,1024]{0,1:T(8,128)} %slice.771), channel_id=1, source_target_pairs={{0,4},{1,5},{2,6},{3,7},{4,0},{5,1},{6,2},{7,3},{8,12},{9,13},{10,... | collective-permute-start | bytes 6291464 | tf_op jit(solution)/shard_map/ppermute | solution.py:40
  319.8 139.9 %reduce-scatter.15.cloned.1.call-start = ((), (), s32[]{:S(2)}) async-start(), calls=%async_computation.9 | async-start | bytes 3932160
  385.1 27.3 %collective-permute-start.20 = (bf16[4,3,2,2,32,1024]{5,4,3,2,1,0:T(8,128)(2,1)}, bf16[4,3,2,2,32,1024]{5,4,3,2,1,0:T(8,128)(2,1)}, u32[]{:S(2)}, u32[]{:S(2)}) collective-permute-start(bf16[4,3,2,2,32,1024]{5,4,3,2,1,0:T(8,128)(2,1)} %pad_maximum_fusion.3), channel_id=1, source_target_pairs={{0,4},{1,5},{2,6},{3,7},{4,0},{5,1},{6,2},{7,3},{8,12},{9,13},{10,... | collective-permute-start | bytes 9437192 | tf_op jit(solution)/shard_map/ppermute | solution.py:40
  416.3 158.8 %reduce-scatter.17.cloned.1.call-start = ((), (), s32[]{:S(2)}) async-start(), calls=%async_computation.10 | async-start | bytes 10485760
  459.7 173.1 %reduce-scatter.19.cloned.1.call-start = ((), (), s32[]{:S(2)}) async-start(), calls=%async_computation.11 | async-start | bytes 2621440
  473.5 7.5 collective-permute-start.37
  485.2 62.4 %collective-permute-start.38 = (bf16[4,4,2,32,1024]{4,3,2,1,0:T(8,128)(2,1)}, bf16[4,4,2,32,1024]{4,3,2,1,0:T(8,128)(2,1)}, u32[]{:S(2)}, u32[]{:S(2)}) collective-permute-start(bf16[4,4,2,32,1024]{4,3,2,1,0:T(8,128)(2,1)} %fusion.36), channel_id=1, source_target_pairs={{0,8},{1,9},{2,10},{3,11},{4,12},{5,13},{6,14},{7,15},{8,0},{9,1},... | collective-permute-start | bytes 6291464 | tf_op jit(solution)/shard_map/ppermute | solution.py:40
  496.4 47.7 %collective-permute-start.24 = (bf16[2,2,2,32,1024]{4,3,2,1,0:T(8,128)(2,1)S(1)}, bf16[2,2,2,32,1024]{4,3,2,1,0:T(8,128)(2,1)S(1)}, u32[]{:S(2)}, u32[]{:S(2)}) collective-permute-start(bf16[2,2,2,32,1024]{4,3,2,1,0:T(8,128)(2,1)S(1)} %pad_maximum_fusion.14), channel_id=1, source_target_pairs={{0,16},{1,17},{2,18},{3,19},{4,20},{5,21},{6,22},{7,23},{8,24},{9,... | collective-permute-start | bytes 1572872 | tf_op jit(solution)/shard_map/ppermute | solution.py:40
  501.8 54.7 %collective-permute-start.21 = (bf16[2,2,2,32,1024]{4,3,2,1,0:T(8,128)(2,1)S(1)}, bf16[2,2,2,32,1024]{4,3,2,1,0:T(8,128)(2,1)S(1)}, u32[]{:S(2)}, u32[]{:S(2)}) collective-permute-start(bf16[2,2,2,32,1024]{4,3,2,1,0:T(8,128)(2,1)S(1)} %pad_maximum_fusion.13), channel_id=1, source_target_pairs={{0,8},{1,9},{2,10},{3,11},{4,12},{5,13},{6,14},{7,15},{8,0},{9,1},... | collective-permute-start | bytes 1572872 | tf_op jit(solution)/shard_map/ppermute | solution.py:40
  544.2 21.5 %collective-permute-start.25 = (bf16[1,2,2,32,1024]{4,3,2,1,0:T(8,128)(2,1)S(1)}, bf16[1,2,2,32,1024]{4,3,2,1,0:T(8,128)(2,1)S(1)}, u32[]{:S(2)}, u32[]{:S(2)}) collective-permute-start(bf16[1,2,2,32,1024]{4,3,2,1,0:T(8,128)(2,1)S(1)} %fusion.241), channel_id=1, source_target_pairs={{0,8},{1,9},{2,10},{3,11},{4,12},{5,13},{6,14},{7,15},{8,0},{9,1},... | collective-permute-start | bytes 786440 | tf_op jit(solution)/shard_map/ppermute | solution.py:40
  556.5 13.1 %collective-permute-start.22 = (bf16[1,2,2,32,1024]{4,3,2,1,0:T(8,128)(2,1)S(1)}, bf16[1,2,2,32,1024]{4,3,2,1,0:T(8,128)(2,1)S(1)}, u32[]{:S(2)}, u32[]{:S(2)}) collective-permute-start(bf16[1,2,2,32,1024]{4,3,2,1,0:T(8,128)(2,1)S(1)} %fusion.243), channel_id=1, source_target_pairs={{0,16},{1,17},{2,18},{3,19},{4,20},{5,21},{6,22},{7,23},{8,24},{9,... | collective-permute-start | bytes 786440 | tf_op jit(solution)/shard_map/ppermute | solution.py:40
  566.6 21.7 %collective-permute-start.26 = (bf16[2,32,1024]{2,1,0:T(8,128)(2,1)}, bf16[2,32,1024]{2,1,0:T(8,128)(2,1)S(1)}, u32[]{:S(2)}, u32[]{:S(2)}) collective-permute-start(bf16[2,32,1024]{2,1,0:T(8,128)(2,1)} %get-tuple-element.254), channel_id=1, source_target_pairs={{0,4},{1,5},{2,6},{3,7},{4,0},{5,1},{6,2},{7,3},{8,12},{9,13},{10,... | collective-permute-start | bytes 393224 | tf_op jit(solution)/shard_map/ppermute | solution.py:40
  570.5 7.3 collective-permute-start.29
  570.6 9.7 %collective-permute-start.27 = (bf16[2,2,1,32,1024]{4,3,1,2,0:T(8,128)(2,1)S(1)}, bf16[2,2,1,32,1024]{4,3,1,2,0:T(8,128)(2,1)S(1)}, u32[]{:S(2)}, u32[]{:S(2)}) collective-permute-start(bf16[2,2,1,32,1024]{4,3,1,2,0:T(8,128)(2,1)S(1)} %pad_maximum_fusion.17), channel_id=1, source_target_pairs={{0,8},{1,9},{2,10},{3,11},{4,12},{5,13},{6,14},{7,15},{8,0},{9,1},... | collective-permute-start | bytes 786440 | tf_op jit(solution)/shard_map/ppermute | solution.py:40
  575.1 13.2 %collective-permute-start.23 = (bf16[2,32,1024]{2,1,0:T(8,128)(2,1)}, bf16[2,32,1024]{2,1,0:T(8,128)(2,1)}, u32[]{:S(2)}, u32[]{:S(2)}) collective-permute-start(bf16[2,32,1024]{2,1,0:T(8,128)(2,1)} %get-tuple-element.256), channel_id=1, source_target_pairs={{0,4},{1,5},{2,6},{3,7},{4,0},{5,1},{6,2},{7,3},{8,12},{9,13},{10,... | collective-permute-start | bytes 393224 | tf_op jit(solution)/shard_map/ppermute | solution.py:40
  580.3 7.3 collective-permute-start.28
  589.1 22.0 %collective-permute-start.33 = (bf16[2,2,2,32,1024]{4,3,2,1,0:T(8,128)(2,1)S(1)}, bf16[2,2,2,32,1024]{4,3,2,1,0:T(8,128)(2,1)S(1)}, u32[]{:S(2)}, u32[]{:S(2)}) collective-permute-start(bf16[2,2,2,32,1024]{4,3,2,1,0:T(8,128)(2,1)S(1)} %pad_maximum_fusion.16), channel_id=1, source_target_pairs={{0,16},{1,17},{2,18},{3,19},{4,20},{5,21},{6,22},{7,23},{8,24},{9,... | collective-permute-start | bytes 1572872 | tf_op jit(solution)/shard_map/ppermute | solution.py:40
  594.0 22.3 %collective-permute-start.31 = (bf16[2,2,2,32,1024]{4,3,2,1,0:T(8,128)(2,1)S(1)}, bf16[2,2,2,32,1024]{4,3,2,1,0:T(8,128)(2,1)S(1)}, u32[]{:S(2)}, u32[]{:S(2)}) collective-permute-start(bf16[2,2,2,32,1024]{4,3,2,1,0:T(8,128)(2,1)S(1)} %pad_maximum_fusion.15), channel_id=1, source_target_pairs={{0,8},{1,9},{2,10},{3,11},{4,12},{5,13},{6,14},{7,15},{8,0},{9,1},... | collective-permute-start | bytes 1572872 | tf_op jit(solution)/shard_map/ppermute | solution.py:40
  611.2 8.4 %collective-permute-start.34 = (bf16[1,2,2,32,1024]{4,3,2,1,0:T(8,128)(2,1)S(1)}, bf16[1,2,2,32,1024]{4,3,2,1,0:T(8,128)(2,1)S(1)}, u32[]{:S(2)}, u32[]{:S(2)}) collective-permute-start(bf16[1,2,2,32,1024]{4,3,2,1,0:T(8,128)(2,1)S(1)} %fusion.237), channel_id=1, source_target_pairs={{0,8},{1,9},{2,10},{3,11},{4,12},{5,13},{6,14},{7,15},{8,0},{9,1},... | collective-permute-start | bytes 786440 | tf_op jit(solution)/shard_map/ppermute | solution.py:40
  616.4 44.3 %collective-permute-start.19 = (f32[512,1024]{0,1:T(8,128)}, f32[512,1024]{0,1:T(8,128)}, u32[]{:S(2)}, u32[]{:S(2)}) collective-permute-start(f32[512,1024]{0,1:T(8,128)} %slice.775), channel_id=1, source_target_pairs={{0,4},{1,5},{2,6},{3,7},{4,0},{5,1},{6,2},{7,3},{8,12},{9,13},{10,... | collective-permute-start | bytes 6291464 | tf_op jit(solution)/shard_map/ppermute | solution.py:40
  616.5 15.3 %collective-permute-start.32 = (bf16[1,2,2,32,1024]{4,3,2,1,0:T(8,128)(2,1)S(1)}, bf16[1,2,2,32,1024]{4,3,2,1,0:T(8,128)(2,1)S(1)}, u32[]{:S(2)}, u32[]{:S(2)}) collective-permute-start(bf16[1,2,2,32,1024]{4,3,2,1,0:T(8,128)(2,1)S(1)} %fusion.239), channel_id=1, source_target_pairs={{0,16},{1,17},{2,18},{3,19},{4,20},{5,21},{6,22},{7,23},{8,24},{9,... | collective-permute-start | bytes 786440 | tf_op jit(solution)/shard_map/ppermute | solution.py:40
  620.4 12.4 %collective-permute-start.36 = (bf16[2,32,1024]{2,1,0:T(8,128)(2,1)S(1)}, bf16[2,32,1024]{2,1,0:T(8,128)(2,1)S(1)}, u32[]{:S(2)}, u32[]{:S(2)}) collective-permute-start(bf16[2,32,1024]{2,1,0:T(8,128)(2,1)S(1)} %get-tuple-element.248), channel_id=1, source_target_pairs={{0,4},{1,5},{2,6},{3,7},{4,0},{5,1},{6,2},{7,3},{8,12},{9,13},{10,... | collective-permute-start | bytes 393224 | tf_op jit(solution)/shard_map/ppermute | solution.py:40
  634.9 14.3 %collective-permute-start.39 = (bf16[4,1,32,1024]{3,2,0,1:T(8,128)(2,1)S(1)}, bf16[4,1,32,1024]{3,2,0,1:T(8,128)(2,1)S(1)}, u32[]{:S(2)}, u32[]{:S(2)}) collective-permute-start(bf16[4,1,32,1024]{3,2,0,1:T(8,128)(2,1)S(1)} %constant_dynamic-slice_fusion.4), channel_id=1, source_target_pairs={{0,16},{1,17},{2,18},{3,19},{4,20},{5,21},{6,22},{7,23},{8,24},{9,... | collective-permute-start | bytes 786440 | tf_op jit(solution)/shard_map/ppermute | solution.py:40
  653.0 56.3 %all-to-all-start = ((bf16[8,3,32,1024]{3,2,1,0:T(8,128)(2,1)}), bf16[8,3,32,1024]{3,2,1,0:T(8,128)(2,1)}, u32[]{:S(2)}, u32[]{:S(2)}) async-start(bf16[8,3,32,1024]{3,2,1,0:T(8,128)(2,1)} %bitcast.572), calls=%async_computation | async-start | bytes 3145728 | tf_op jit(solution)/shard_map/all_to_all | solution.py:607
  669.4 22.4 %collective-permute-start.71 = (f32[15,1024]{1,0:T(8,128)S(1)}, f32[15,1024]{1,0:T(8,128)S(1)}, u32[]{:S(2)}, u32[]{:S(2)}) collective-permute-start(f32[15,1024]{1,0:T(8,128)S(1)} %add.1033), channel_id=1, source_target_pairs={{0,2},{1,3},{2,0},{3,1},{4,6},{5,7},{6,4},{7,5},{8,10},{9,11},{10,... | collective-permute-start | bytes 184328 | tf_op jit(solution)/shard_map/ppermute | solution.py:40
  698.9 9.4 %collective-permute-start.74 = (f32[15,1024]{1,0:T(8,128)S(1)}, f32[15,1024]{1,0:T(8,128)S(1)}, u32[]{:S(2)}, u32[]{:S(2)}) collective-permute-start(f32[15,1024]{1,0:T(8,128)S(1)} %add.1036), channel_id=1, source_target_pairs={{0,16},{1,17},{2,18},{3,19},{4,20},{5,21},{6,22},{7,23},{8,24},{9,... | collective-permute-start | bytes 184328 | tf_op jit(solution)/shard_map/ppermute | solution.py:40
  722.0 14.9 %collective-permute-start.42 = (bf16[512,512]{1,0:T(8,128)(2,1)S(1)}, bf16[512,512]{1,0:T(8,128)(2,1)S(1)}, u32[]{:S(2)}, u32[]{:S(2)}) collective-permute-start(bf16[512,512]{1,0:T(8,128)(2,1)S(1)} %convolution_convert_fusion.26), channel_id=1, source_target_pairs={{0,2},{1,3},{2,0},{3,1},{4,6},{5,7},{6,4},{7,5},{8,10},{9,11},{10,... | collective-permute-start | bytes 1572872 | tf_op jit(solution)/shard_map/ppermute | solution.py:40
  724.6 14.9 %collective-permute-start.40 = (bf16[512,512]{1,0:T(8,128)(2,1)S(1)}, bf16[512,512]{1,0:T(8,128)(2,1)S(1)}, u32[]{:S(2)}, u32[]{:S(2)}) collective-permute-start(bf16[512,512]{1,0:T(8,128)(2,1)S(1)} %convolution_convert_fusion.27), channel_id=1, source_target_pairs={{0,1},{1,0},{2,3},{3,2},{4,5},{5,4},{6,7},{7,6},{8,9},{9,8},{10,11... | collective-permute-start | bytes 1572872 | tf_op jit(solution)/shard_map/ppermute | solution.py:40
  726.9 21.2 %collective-permute-start.46 = (bf16[512,512]{1,0:T(8,128)(2,1)S(1)}, bf16[512,512]{1,0:T(8,128)(2,1)S(1)}, u32[]{:S(2)}, u32[]{:S(2)}) collective-permute-start(bf16[512,512]{1,0:T(8,128)(2,1)S(1)} %convolution_convert_fusion.23), channel_id=1, source_target_pairs={{0,2},{1,3},{2,0},{3,1},{4,6},{5,7},{6,4},{7,5},{8,10},{9,11},{10,... | collective-permute-start | bytes 1572872 | tf_op jit(solution)/shard_map/ppermute | solution.py:40
  727.9 22.8 %collective-permute-start.44 = (bf16[512,512]{1,0:T(8,128)(2,1)S(1)}, bf16[512,512]{1,0:T(8,128)(2,1)S(1)}, u32[]{:S(2)}, u32[]{:S(2)}) collective-permute-start(bf16[512,512]{1,0:T(8,128)(2,1)S(1)} %convolution_convert_fusion.24), channel_id=1, source_target_pairs={{0,1},{1,0},{2,3},{3,2},{4,5},{5,4},{6,7},{7,6},{8,9},{9,8},{10,11... | collective-permute-start | bytes 1572872 | tf_op jit(solution)/shard_map/ppermute | solution.py:40
  729.4 29.9 %collective-permute-start.50 = (bf16[512,512]{1,0:T(8,128)(2,1)S(1)}, bf16[512,512]{1,0:T(8,128)(2,1)S(1)}, u32[]{:S(2)}, u32[]{:S(2)}) collective-permute-start(bf16[512,512]{1,0:T(8,128)(2,1)S(1)} %convolution_convert_fusion.20), channel_id=1, source_target_pairs={{0,2},{1,3},{2,0},{3,1},{4,6},{5,7},{6,4},{7,5},{8,10},{9,11},{10,... | collective-permute-start | bytes 1572872 | tf_op jit(solution)/shard_map/ppermute | solution.py:40
  736.9 25.1 %collective-permute-start.48 = (bf16[512,512]{1,0:T(8,128)(2,1)S(1)}, bf16[512,512]{1,0:T(8,128)(2,1)S(1)}, u32[]{:S(2)}, u32[]{:S(2)}) collective-permute-start(bf16[512,512]{1,0:T(8,128)(2,1)S(1)} %convolution_convert_fusion.21), channel_id=1, source_target_pairs={{0,1},{1,0},{2,3},{3,2},{4,5},{5,4},{6,7},{7,6},{8,9},{9,8},{10,11... | collective-permute-start | bytes 1572872 | tf_op jit(solution)/shard_map/ppermute | solution.py:40
  739.5 28.1 %collective-permute-start.43 = (bf16[256,512]{1,0:T(8,128)(2,1)S(1)}, bf16[256,512]{1,0:T(8,128)(2,1)S(1)}, u32[]{:S(2)}, u32[]{:S(2)}) collective-permute-start(bf16[256,512]{1,0:T(8,128)(2,1)S(1)} %fusion.224), channel_id=1, source_target_pairs={{0,1},{1,0},{2,3},{3,2},{4,5},{5,4},{6,7},{7,6},{8,9},{9,8},{10,11... | collective-permute-start | bytes 786440 | tf_op jit(solution)/shard_map/ppermute | solution.py:40
  748.1 21.4 %collective-permute-start.41 = (bf16[256,512]{1,0:T(8,128)(2,1)S(1)}, bf16[256,512]{1,0:T(8,128)(2,1)S(1)}, u32[]{:S(2)}, u32[]{:S(2)}) collective-permute-start(bf16[256,512]{1,0:T(8,128)(2,1)S(1)} %fusion.226), channel_id=1, source_target_pairs={{0,2},{1,3},{2,0},{3,1},{4,6},{5,7},{6,4},{7,5},{8,10},{9,11},{10,... | collective-permute-start | bytes 786440 | tf_op jit(solution)/shard_map/ppermute | solution.py:40
  750.8 22.5 %collective-permute-start.47 = (bf16[256,512]{1,0:T(8,128)(2,1)S(1)}, bf16[256,512]{1,0:T(8,128)(2,1)S(1)}, u32[]{:S(2)}, u32[]{:S(2)}) collective-permute-start(bf16[256,512]{1,0:T(8,128)(2,1)S(1)} %fusion.220), channel_id=1, source_target_pairs={{0,1},{1,0},{2,3},{3,2},{4,5},{5,4},{6,7},{7,6},{8,9},{9,8},{10,11... | collective-permute-start | bytes 786440 | tf_op jit(solution)/shard_map/ppermute | solution.py:40
  759.3 15.8 %collective-permute-start.45 = (bf16[256,512]{1,0:T(8,128)(2,1)S(1)}, bf16[256,512]{1,0:T(8,128)(2,1)S(1)}, u32[]{:S(2)}, u32[]{:S(2)}) collective-permute-start(bf16[256,512]{1,0:T(8,128)(2,1)S(1)} %fusion.222), channel_id=1, source_target_pairs={{0,2},{1,3},{2,0},{3,1},{4,6},{5,7},{6,4},{7,5},{8,10},{9,11},{10,... | collective-permute-start | bytes 786440 | tf_op jit(solution)/shard_map/ppermute | solution.py:40
  762.0 16.9 %collective-permute-start.51 = (bf16[256,512]{1,0:T(8,128)(2,1)S(1)}, bf16[256,512]{1,0:T(8,128)(2,1)S(1)}, u32[]{:S(2)}, u32[]{:S(2)}) collective-permute-start(bf16[256,512]{1,0:T(8,128)(2,1)S(1)} %fusion.216), channel_id=1, source_target_pairs={{0,1},{1,0},{2,3},{3,2},{4,5},{5,4},{6,7},{7,6},{8,9},{9,8},{10,11... | collective-permute-start | bytes 786440 | tf_op jit(solution)/shard_map/ppermute | solution.py:40
  767.6 13.1 %collective-permute-start.49 = (bf16[256,512]{1,0:T(8,128)(2,1)S(1)}, bf16[256,512]{1,0:T(8,128)(2,1)S(1)}, u32[]{:S(2)}, u32[]{:S(2)}) collective-permute-start(bf16[256,512]{1,0:T(8,128)(2,1)S(1)} %fusion.218), channel_id=1, source_target_pairs={{0,2},{1,3},{2,0},{3,1},{4,6},{5,7},{6,4},{7,5},{8,10},{9,11},{10,... | collective-permute-start | bytes 786440 | tf_op jit(solution)/shard_map/ppermute | solution.py:40
  770.3 14.2 %collective-permute-start.53 = (bf16[256,512]{1,0:T(8,128)(2,1)S(1)}, bf16[256,512]{1,0:T(8,128)(2,1)S(1)}, u32[]{:S(2)}, u32[]{:S(2)}) collective-permute-start(bf16[256,512]{1,0:T(8,128)(2,1)S(1)} %get-tuple-element.149), channel_id=1, source_target_pairs={{0,1},{1,0},{2,3},{3,2},{4,5},{5,4},{6,7},{7,6},{8,9},{9,8},{10,11... | collective-permute-start | bytes 786440 | tf_op jit(solution)/shard_map/ppermute | solution.py:40
  773.2 15.7 %collective-permute-start.52 = (bf16[256,512]{1,0:T(8,128)(2,1)S(1)}, bf16[256,512]{1,0:T(8,128)(2,1)S(1)}, u32[]{:S(2)}, u32[]{:S(2)}) collective-permute-start(bf16[256,512]{1,0:T(8,128)(2,1)S(1)} %get-tuple-element.149), channel_id=1, source_target_pairs={{0,2},{1,3},{2,0},{3,1},{4,6},{5,7},{6,4},{7,5},{8,10},{9,11},{10,... | collective-permute-start | bytes 786440 | tf_op jit(solution)/shard_map/ppermute | solution.py:40
  775.1 12.8 %collective-permute-start.56 = (bf16[256,512]{1,0:T(8,128)(2,1)S(1)}, bf16[256,512]{1,0:T(8,128)(2,1)S(1)}, u32[]{:S(2)}, u32[]{:S(2)}) collective-permute-start(bf16[256,512]{1,0:T(8,128)(2,1)S(1)} %get-tuple-element.195), channel_id=1, source_target_pairs={{0,2},{1,3},{2,0},{3,1},{4,6},{5,7},{6,4},{7,5},{8,10},{9,11},{10,... | collective-permute-start | bytes 786440 | tf_op jit(solution)/shard_map/ppermute | solution.py:40
  778.9 17.2 %collective-permute-start.55 = (bf16[256,512]{1,0:T(8,128)(2,1)S(1)}, bf16[256,512]{1,0:T(8,128)(2,1)S(1)}, u32[]{:S(2)}, u32[]{:S(2)}) collective-permute-start(bf16[256,512]{1,0:T(8,128)(2,1)S(1)} %get-tuple-element.195), channel_id=1, source_target_pairs={{0,1},{1,0},{2,3},{3,2},{4,5},{5,4},{6,7},{7,6},{8,9},{9,8},{10,11... | collective-permute-start | bytes 786440 | tf_op jit(solution)/shard_map/ppermute | solution.py:40
  780.7 22.9 %collective-permute-start.59 = (bf16[256,512]{1,0:T(8,128)(2,1)S(1)}, bf16[256,512]{1,0:T(8,128)(2,1)S(1)}, u32[]{:S(2)}, u32[]{:S(2)}) collective-permute-start(bf16[256,512]{1,0:T(8,128)(2,1)S(1)} %get-tuple-element.153), channel_id=1, source_target_pairs={{0,1},{1,0},{2,3},{3,2},{4,5},{5,4},{6,7},{7,6},{8,9},{9,8},{10,11... | collective-permute-start | bytes 786440 | tf_op jit(solution)/shard_map/ppermute | solution.py:40
  784.5 9.2 %collective-permute-start.54 = (bf16[256,512]{1,0:T(8,128)(2,1)S(1)}, bf16[256,512]{1,0:T(8,128)(2,1)S(1)}, u32[]{:S(2)}, u32[]{:S(2)}) collective-permute-start(bf16[256,512]{1,0:T(8,128)(2,1)S(1)} %collective-permute-done.53), channel_id=1, source_target_pairs={{0,2},{1,3},{2,0},{3,1},{4,6},{5,7},{6,4},{7,5},{8,10},{9,11},{10,... | collective-permute-start | bytes 786440 | tf_op jit(solution)/shard_map/ppermute | solution.py:40
  787.9 13.4 %collective-permute-start.57 = (bf16[256,512]{1,0:T(8,128)(2,1)S(1)}, bf16[256,512]{1,0:T(8,128)(2,1)S(1)}, u32[]{:S(2)}, u32[]{:S(2)}) collective-permute-start(bf16[256,512]{1,0:T(8,128)(2,1)S(1)} %collective-permute-done.56), channel_id=1, source_target_pairs={{0,1},{1,0},{2,3},{3,2},{4,5},{5,4},{6,7},{7,6},{8,9},{9,8},{10,11... | collective-permute-start | bytes 786440 | tf_op jit(solution)/shard_map/ppermute | solution.py:40
  788.9 15.4 %collective-permute-start.58 = (bf16[256,512]{1,0:T(8,128)(2,1)S(1)}, bf16[256,512]{1,0:T(8,128)(2,1)S(1)}, u32[]{:S(2)}, u32[]{:S(2)}) collective-permute-start(bf16[256,512]{1,0:T(8,128)(2,1)S(1)} %get-tuple-element.153), channel_id=1, source_target_pairs={{0,2},{1,3},{2,0},{3,1},{4,6},{5,7},{6,4},{7,5},{8,10},{9,11},{10,... | collective-permute-start | bytes 786440 | tf_op jit(solution)/shard_map/ppermute | solution.py:40
  793.7 12.0 %collective-permute-start.62 = (bf16[256,512]{1,0:T(8,128)(2,1)S(1)}, bf16[256,512]{1,0:T(8,128)(2,1)S(1)}, u32[]{:S(2)}, u32[]{:S(2)}) collective-permute-start(bf16[256,512]{1,0:T(8,128)(2,1)S(1)} %get-tuple-element.197), channel_id=1, source_target_pairs={{0,2},{1,3},{2,0},{3,1},{4,6},{5,7},{6,4},{7,5},{8,10},{9,11},{10,... | collective-permute-start | bytes 786440 | tf_op jit(solution)/shard_map/ppermute | solution.py:40
  796.0 20.9 %collective-permute-start.61 = (bf16[256,512]{1,0:T(8,128)(2,1)S(1)}, bf16[256,512]{1,0:T(8,128)(2,1)S(1)}, u32[]{:S(2)}, u32[]{:S(2)}) collective-permute-start(bf16[256,512]{1,0:T(8,128)(2,1)S(1)} %get-tuple-element.197), channel_id=1, source_target_pairs={{0,1},{1,0},{2,3},{3,2},{4,5},{5,4},{6,7},{7,6},{8,9},{9,8},{10,11... | collective-permute-start | bytes 786440 | tf_op jit(solution)/shard_map/ppermute | solution.py:40
  801.3 16.3 %collective-permute-start.65 = (bf16[256,512]{1,0:T(8,128)(2,1)S(1)}, bf16[256,512]{1,0:T(8,128)(2,1)S(1)}, u32[]{:S(2)}, u32[]{:S(2)}) collective-permute-start(bf16[256,512]{1,0:T(8,128)(2,1)S(1)} %get-tuple-element.157), channel_id=1, source_target_pairs={{0,1},{1,0},{2,3},{3,2},{4,5},{5,4},{6,7},{7,6},{8,9},{9,8},{10,11... | collective-permute-start | bytes 786440 | tf_op jit(solution)/shard_map/ppermute | solution.py:40
  803.6 14.9 %collective-permute-start.68 = (bf16[256,512]{1,0:T(8,128)(2,1)S(1)}, bf16[256,512]{1,0:T(8,128)(2,1)S(1)}, u32[]{:S(2)}, u32[]{:S(2)}) collective-permute-start(bf16[256,512]{1,0:T(8,128)(2,1)S(1)} %get-tuple-element.199), channel_id=1, source_target_pairs={{0,2},{1,3},{2,0},{3,1},{4,6},{5,7},{6,4},{7,5},{8,10},{9,11},{10,... | collective-permute-start | bytes 786440 | tf_op jit(solution)/shard_map/ppermute | solution.py:40
  804.4 11.2 %collective-permute-start.60 = (bf16[256,512]{1,0:T(8,128)(2,1)S(1)}, bf16[256,512]{1,0:T(8,128)(2,1)S(1)}, u32[]{:S(2)}, u32[]{:S(2)}) collective-permute-start(bf16[256,512]{1,0:T(8,128)(2,1)S(1)} %collective-permute-done.59), channel_id=1, source_target_pairs={{0,2},{1,3},{2,0},{3,1},{4,6},{5,7},{6,4},{7,5},{8,10},{9,11},{10,... | collective-permute-start | bytes 786440 | tf_op jit(solution)/shard_map/ppermute | solution.py:40
  805.7 14.5 %collective-permute-start.63 = (bf16[256,512]{1,0:T(8,128)(2,1)S(1)}, bf16[256,512]{1,0:T(8,128)(2,1)S(1)}, u32[]{:S(2)}, u32[]{:S(2)}) collective-permute-start(bf16[256,512]{1,0:T(8,128)(2,1)S(1)} %collective-permute-done.62), channel_id=1, source_target_pairs={{0,1},{1,0},{2,3},{3,2},{4,5},{5,4},{6,7},{7,6},{8,9},{9,8},{10,11... | collective-permute-start | bytes 786440 | tf_op jit(solution)/shard_map/ppermute | solution.py:40
  815.6 7.3 collective-permute-start.64
  816.9 8.7 %collective-permute-start.67 = (bf16[256,512]{1,0:T(8,128)(2,1)S(1)}, bf16[256,512]{1,0:T(8,128)(2,1)S(1)}, u32[]{:S(2)}, u32[]{:S(2)}) collective-permute-start(bf16[256,512]{1,0:T(8,128)(2,1)S(1)} %get-tuple-element.199), channel_id=1, source_target_pairs={{0,1},{1,0},{2,3},{3,2},{4,5},{5,4},{6,7},{7,6},{8,9},{9,8},{10,11... | collective-permute-start | bytes 786440 | tf_op jit(solution)/shard_map/ppermute | solution.py:40
  817.7 7.5 collective-permute-start.66
  818.5 9.1 %collective-permute-start.69 = (bf16[256,512]{1,0:T(8,128)(2,1)S(1)}, bf16[256,512]{1,0:T(8,128)(2,1)S(1)}, u32[]{:S(2)}, u32[]{:S(2)}) collective-permute-start(bf16[256,512]{1,0:T(8,128)(2,1)S(1)} %collective-permute-done.68), channel_id=1, source_target_pairs={{0,1},{1,0},{2,3},{3,2},{4,5},{5,4},{6,7},{7,6},{8,9},{9,8},{10,11... | collective-permute-start | bytes 786440 | tf_op jit(solution)/shard_map/ppermute | solution.py:40
  (192 other events, 1576.4 us)
Sparse Core Ops, SparseCore 0:
  11.9 55.3 all-gather.3
  69.8 80.9 all-gather.5
  169.0 88.1 all-gather.7
  319.9 86.6 reduce-scatter.12
  416.4 43.1 reduce-scatter.14
  462.8 86.3 reduce-scatter.16
  576.8 32.5 reduce-scatter.18

commit v3 on v2

--- a/solution.py
+++ b/solution.py
@@ -380,9 +380,12 @@
     def rows_of(low, count, side, size):
         return lax.dynamic_slice(blocks, (low, side * size, 0), (count, size, D)).astype(BF)
 
-    def fetch_own(base):
+    def own_share(base):
         own = [rows_of(base + k * per_in + core * per_core, per_core, 0, rows_own) for k in (0, 1)]
-        fetched = lax.all_gather(jnp.concatenate(own, axis=0), "fsdp", axis=1, tiled=True)
+        return jnp.concatenate(own, axis=0)
+
+    def fetch_own(own):
+        fetched = lax.all_gather(own, "fsdp", axis=1, tiled=True)
         return [fetched[j] for j in range(2 * per_core)]
 
     def fetch_shared(base):
@@ -431,12 +434,13 @@
             up = lifted[j].astype(F32)
             gate = jax.nn.sigmoid(up)
             lows.append((acted_grad * (gate * (1.0 + up * (1.0 - gate)))).astype(BF))
-        normed_grad = across(sum(mm_t(lows[j], weights[j]) for j in range(per_core)))
         for j in range(per_core):
             grads_out.append(t_mm(acted[j], pair).astype(BF))
             grads_in.append(t_mm(normed_pair, lows[j]).astype(BF))
         listed = [held.reshape(n_fsdp, rows_own, D) for held in grads_in + grads_out]
-        return normed_grad, jnp.stack(listed, axis=1)
+        stacked = jnp.stack(listed, axis=1)
+        lows, stacked = lax.optimization_barrier((lows, stacked))
+        return across(sum(mm_t(lows[j], weights[j]) for j in range(per_core))), stacked
 
     last = []
 
@@ -447,32 +451,11 @@
         last.append(lax.optimization_barrier(summed))
         return last[-1][0]
 
-    def share(products, along_z):
-        pieces = n_dp // 2
-        shape = (n_fsdp, 2, pieces // 2, 2, half // pieces, D)
-        split = [held.astype(BF).reshape(shape) for held in products]
-        away = jnp.stack([pick(held, 1, 1 - core) for held in split], axis=1)
-        arrived = swap_core(away)
-        if not along_z:
-            kept = jnp.stack([pick(held, 1, core) for held in split], axis=1)
-            return low_add(kept, arrived).reshape(n_fsdp, len(split), half, D)
-        side = dpz % 2
-
-        def summed(which):
-            kept = jnp.stack([pick(pick(held, 1, core), 2, which) for held in split], axis=1)
-            return low_add(kept, pick(arrived, 3, which))
-
-        sent, kept = summed(1 - side), summed(side)
-        return low_add(kept, swap(sent, 2, 0))
-
-    def spread_shared(held, name):
-        for bit in bits_of(n_dp // 2)[1:]:
-            count, left, rows, _ = held.shape
-            parted = held.reshape(count, left // 2, 2, rows, D)
-            which = (dpz // bit) % 2
-            arrived = swap(pick(parted, 2, 1 - which), 2 * bit, 0)
-            held = low_add(pick(parted, 2, which), arrived)
-        sums[name] = held[:, 0]
+    def share(products):
+        split = [held.astype(BF).reshape(n_fsdp, 2, half, D) for held in products]
+        arrived = swap_core(jnp.stack([pick(held, 1, 1 - core) for held in split], axis=1))
+        kept = jnp.stack([pick(held, 1, core) for held in split], axis=1)
+        return low_add(kept, arrived)
 
     def spread_dp(held, sides, name):
         middle = (held.shape[0] + 1) // 2
@@ -485,9 +468,10 @@
     sums = {}
     weights1 = fetch_shared(0)
     weights_middle = fetch_half(base_attn, base_last)
-    weights2 = fetch_own(base_last)
+    start_x = frames.astype(F32).reshape(tokens, D)
+    start_x, own2 = lax.optimization_barrier((start_x, own_share(base_last)))
+    weights2 = fetch_own(own2)
     w_attn, w_conv = weights_middle[:4], weights_middle[4:]
-    start_x = frames.astype(F32).reshape(tokens, D)
     lifted1, ffn1_pullback, normed_pair1 = feed_up(start_x, 0, weights1)
     first_x, acted1 = feed_down(start_x, lifted1, weights1)
     normed, attn_pullback = jax.vjp(norm_apply, first_x, gains[1], shifts[1])
@@ -538,7 +522,7 @@
     )
     grad_a, grad_g, taps_grad = gated_pullback(conv_grad)
     grad_a, grad_g = grad_a.astype(BF), grad_g.astype(BF)
-    shared_conv = share([t_mm(conv_low, grad_a), t_mm(conv_low, grad_g), grad_back], False)
+    shared_conv = share([t_mm(conv_low, grad_a), t_mm(conv_low, grad_g), grad_back])
     summed_conv = scatter(shared_conv)
     part_x, conv_gain, conv_shift = conv_pullback(
         mm_t(grad_a, w_conv[0]) + mm_t(grad_g, w_conv[1])
@@ -552,15 +536,25 @@
     query_low = (query_grad.reshape(tokens, D) * scale_head).astype(BF)
     key_low = key_grad.reshape(tokens, D).astype(BF)
     value_low = value_grad.reshape(tokens, D).astype(BF)
+    query_low, key_low, value_low, summed2 = lax.optimization_barrier(
+        (query_low, key_low, value_low, summed2)
+    )
     grad_heads = [t_mm(attn_low, held) for held in (query_low, key_low, value_low)]
-    shared_attn = share([*grad_heads, t_mm(context_low, branch_low)], True)
+    grad_proj = t_mm(context_low, branch_low)
     part_x, attn_gain, attn_shift = attn_pullback(
         mm_t(query_low, w_attn[0]) + mm_t(key_low, w_attn[1]) + mm_t(value_low, w_attn[2])
     )
     grad_x = grad_x + part_x
     normed_grad, stacked = feed_back(grad_x, lifted1, acted1, normed_pair1, weights1)
     summed1 = scatter(stacked)
-    summed_attn = scatter(shared_attn)
+    spread_dp(summed2, 2, "ffn2")
+    spread_dp(summed_conv, 1, "conv")
+    summed_attn = scatter(
+        after(
+            share([*grad_heads, grad_proj]),
+            *[sums[name + place] for name in ("ffn2", "conv") for place in "xy"],
+        )
+    )
     hidden_grad, ffn1_gain, ffn1_shift = ffn1_pullback(normed_grad)
     grad_x = grad_x + hidden_grad
     frames_grad = grad_x.reshape(rows_here, LENGTH, D)
@@ -572,12 +566,9 @@
         ],
         axis=0,
     )
-    spread_dp(summed2, 2, "ffn2")
-    spread_dp(summed_conv, 1, "conv")
-    summed1 = after(summed1, *[sums[name + place] for name in ("ffn2", "conv") for place in "xy"])
     spread_dp(summed1, 2, "ffn1")
     summed_attn = after(summed_attn, *[sums["ffn1" + place] for place in "xy"])
-    spread_shared(summed_attn, "attn")
+    spread_dp(summed_attn, 1, "attn")
     summed_small = total(local_small)
     small_grads = jnp.concatenate(
         [summed_small[0:10], gain_sum[None], shift_sum[None], summed_small[10:]], axis=0
@@ -587,7 +578,7 @@
     for name in ("ffn1", "middle", "ffn2"):
         base = sum(part.shape[0] for part in parts)
         if name == "middle":
-            parts += [sums["attn"], sums["convx"], sums["convy"]]
+            parts += [sums[name + place] for name in ("attn", "conv") for place in "xy"]
             places.append(base + jnp.arange(base_last - base_attn, dtype=jnp.int32))
             continue
         (in_mine, in_other), (out_mine, out_other) = sums[name + "x"], sums[name + "y"]
@@ -603,6 +594,7 @@
     slot_used = jnp.sum(matches, axis=1)
     piece = half // (n_dp // 2)
     slot_place = jnp.sum(matches * places[None], axis=1)
+    parts, frames_grad = lax.optimization_barrier((parts, frames_grad))
     sent = deal(slot_place, slot_used, parts).reshape(n_dp, capacity, piece, D)
     came = lax.all_to_all(sent, DP, 0, 0, tiled=False)
     came = came.reshape(n_dp // 2, 2, capacity, piece, D).transpose(2, 1, 0, 3, 4)

time: 849 us -> 835 us (0.984)
  starting transfers between devices: 91.1 us -> 77.4 us
  local copies, waits for them, and re-layouts: 91.8 us -> 81.4 us
    ppermute x75 -> x77, starting transfers between devices: 86.2 us -> 72.1 us  [swap(): return lax.ppermute(value, AXES, pairs)]
    ppermute x75 -> x77, waiting for transfers between devices: 243 us -> 251 us  [swap(): return lax.ppermute(value, AXES, pairs)]
    unnamed x350 -> x338, local copies, waits for them, and re-layouts: 43.4 us -> 36.1 us
    convert_element_type x19 -> x20, other arithmetic: 13.4 us -> 17.1 us  [low_add(): return (left.astype(F32) + right.astype(F32)).astype(BF)]
  transfers between devices with their start and end apart: 83 -> 85, of which waited for: 47 -> 54; matrix products, arithmetic and copies ran while one was open for 32% -> 31% of each run, Pallas kernels for 3% -> 3%
where the time goes in v3:
time: 835 us; the launch traced here: 829 us
  waiting for transfers between devices  335 us (40%)
  matrix products  181 us (22%)
  other arithmetic  97.4 us (12%)
  local copies, waits for them, and re-layouts  81.4 us (10%)
  starting transfers between devices  77.4 us (9%)
  between operations  28.5 us (3%)
  Pallas kernels  28 us (3%)
    ppermute x77, waiting for transfers between devices, swap(): return lax.ppermute(value, AXES, pairs)  251 us
    ppermute x77, starting transfers between devices, swap(): return lax.ppermute(value, AXES, pairs)  72.1 us
    dot_general x18, matrix products, mm_t(): lax.dot_general(left, right, (((1,), (1,)), ((), ())), preferred_element_...  66.1 us
    dot_general x24, matrix products, mm(): return jnp.dot(left, right, preferred_element_type=F32)  55.9 us
    all_gather x1, waiting for transfers between devices, fetch_shared(): fetched = lax.all_gather(own, 'fsdp', axis=1, tiled=True)  45.7 us
    dot_general x27, matrix products, t_mm(): lax.dot_general(left, right, (((0,), (0,)), ((), ())), preferred_element_...  44.9 us
    unnamed x338, local copies, waits for them, and re-layouts  36.1 us
    all_gather x1, waiting for transfers between devices, fetch_own(): fetched = lax.all_gather(own, 'fsdp', axis=1, tiled=True)  26.5 us
  transfers between devices with their start and end apart: 85, of which 54 were waited for; matrix products, arithmetic and copies ran while one was open for 31% of the time, Pallas kernels for 3%

profile of v3, /device:TPU:0, one launch (start us, length us, event | category | flops | bytes accessed | tf_op | source)
XLA Modules:
  0.0 829.0 jit_solution(4906818558757166555)
XLA Ops:
  7.2 3.5 dynamic-slice_convert_fusion.4
  11.9 3.7 dynamic-slice_convert_fusion
  21.7 45.7 %all-gather.4.cloned.1.call-done = bf16[4,512,1024]{2,1,0:T(8,128)(2,1)} async-done(((bf16[4,128,1024]{2,1,0:T(8,128)(2,1)}), bf16[4,512,1024]{2,1,0:T(8,128)(2,1)}) %all-gather.4.cloned.1.call-update) | async-done | bytes 4194320 | tf_op jit(solution)/shard_map/all_gather | solution.py:398
  76.9 32.8 %collective-permute-done.1.arrived_ref = bf16[2,3,128,1024]{3,2,1,0:T(8,128)(2,1)} collective-permute-done((bf16[2,3,128,1024]{3,2,1,0:T(8,128)(2,1)S(1)}, bf16[2,3,128,1024]{3,2,1,0:T(8,128)(2,1)}, u32[]{:S(2)}, u32[]{:S(2)}) %collective-permute-start.1) | collective-permute-done | bytes 1572896 | tf_op jit(solution)/shard_map/ppermute | solution.py:40
  109.7 4.3 interleave.2
  114.0 28.2 %collective-permute-done.2.arrived_ref = bf16[2,3,128,1024]{3,2,1,0:T(8,128)(2,1)} collective-permute-done((bf16[2,3,128,1024]{3,2,1,0:T(8,128)(2,1)}, bf16[2,3,128,1024]{3,2,1,0:T(8,128)(2,1)}, u32[]{:S(2)}, u32[]{:S(2)}) %collective-permute-start.2) | collective-permute-done | bytes 1572896 | tf_op jit(solution)/shard_map/ppermute | solution.py:40
  142.2 4.8 interleave.3
  147.0 4.4 convolution_convert_fusion.18
  151.5 4.4 convolution_convert_fusion.17
  174.2 3.4 fusion.91
  178.3 4.2 multiply_convert_fusion.7
  184.1 3.2 fusion.97
  227.0 26.5 %all-gather.8.cloned.1.call-done = bf16[4,1024,1024]{2,1,0:T(8,128)(2,1)} async-done(((bf16[4,256,1024]{2,1,0:T(8,128)(2,1)}), bf16[4,1024,1024]{2,1,0:T(8,128)(2,1)}) %all-gather.8.cloned.1.call-update) | async-done | bytes 8388624 | tf_op jit(solution)/shard_map/all_gather | solution.py:388
  253.5 4.4 convolution_convert_fusion.15
  258.0 4.4 convolution_convert_fusion.16
  266.3 3.0 convolution_add_fusion.2
  285.2 3.4 fusion.27
  288.6 3.6 fusion.35
  297.2 3.6 convolution_convert_fusion.14
  300.8 3.6 convolution_convert_fusion.13
  304.4 4.0 pad_maximum_fusion
  308.7 4.7 fusion.85
  313.4 4.0 convolution_add_fusion.1
  317.8 4.0 collective-permute-done.12
  327.5 5.9 fusion.316
  343.9 3.3 convolution_convert_fusion.4
  359.8 3.3 fusion.79
  363.2 4.2 multiply_reduce_fusion.3
  370.6 3.9 fusion.90
  396.8 3.2 fusion.94
  400.0 3.2 fusion.73
  406.3 3.3 fusion.314
  413.9 3.9 add_convert_fusion.1
  418.1 5.9 fusion.11
  424.1 4.4 convolution_convert_fusion.10
  428.5 4.7 fusion.19
  433.2 4.4 convolution_convert_fusion.9
  437.6 4.2 convolution_convert_fusion.8
  441.8 3.7 convolution_convert_fusion.7
  445.5 4.0 pad_maximum_fusion.1
  449.5 11.8 %reduce-scatter.15.cloned.1.call-done = bf16[1,3,128,1024]{3,2,1,0:T(8,128)(2,1)} async-done(((bf16[4,3,128,1024]{3,2,1,0:T(8,128)(2,1)}), bf16[1,3,128,1024]{3,2,1,0:T(8,128)(2,1)}) %reduce-scatter.15.cloned.1.call-update) | async-done | bytes 786448
  489.4 18.6 %collective-permute-done.30 = bf16[2,2,2,32,1024]{4,3,2,1,0:T(8,128)(2,1)} collective-permute-done((bf16[2,2,2,32,1024]{4,3,2,1,0:T(8,128)(2,1)}, bf16[2,2,2,32,1024]{4,3,2,1,0:T(8,128)(2,1)}, u32[]{:S(2)}, u32[]{:S(2)}) %collective-permute-start.30) | collective-permute-done | bytes 524320 | tf_op jit(solution)/shard_map/ppermute | solution.py:40
  513.4 3.6 collective-permute-start.28
  521.7 7.1 collective-permute-done.28
  535.2 5.1 add_convert_fusion
  548.0 5.9 collective-permute-done.34
  557.2 4.1 fusion.69
  569.4 22.1 %collective-permute-done.22 = bf16[2,2,2,32,1024]{4,3,2,1,0:T(8,128)(2,1)S(1)} collective-permute-done((bf16[2,2,2,32,1024]{4,3,2,1,0:T(8,128)(2,1)S(1)}, bf16[2,2,2,32,1024]{4,3,2,1,0:T(8,128)(2,1)S(1)}, u32[]{:S(2)}, u32[]{:S(2)}) %collective-permute-start.22) | collective-permute-done | bytes 524320 | tf_op jit(solution)/shard_map/ppermute | solution.py:40
  595.0 7.5 collective-permute-done.23
  603.3 5.0 collective-permute-done.21
  616.9 9.7 %collective-permute-done.39 = bf16[2,2,1,32,1024]{4,3,1,2,0:T(8,128)(2,1)S(1)} collective-permute-done((bf16[2,2,1,32,1024]{4,3,1,2,0:T(8,128)(2,1)S(1)}, bf16[2,2,1,32,1024]{4,3,1,2,0:T(8,128)(2,1)S(1)}, u32[]{:S(2)}, u32[]{:S(2)}) %collective-permute-start.39) | collective-permute-done | bytes 262176 | tf_op jit(solution)/shard_map/ppermute | solution.py:40
  629.0 4.8 collective-permute-done.40
  639.7 4.6 all-to-all-start
  649.2 5.4 slice_bitcast_fusion.67
  696.1 3.1 convolution_convert_fusion.28
  701.0 3.3 convolution_convert_fusion.25
  715.1 6.8 collective-permute-done.44
  726.6 6.6 collective-permute-done.48
  737.8 6.6 collective-permute-done.52
  749.0 4.2 collective-permute-done.45
  774.9 4.4 collective-permute-done.56
  781.8 5.1 collective-permute-done.59
  793.5 7.4 collective-permute-done.62
  817.4 4.5 fusion.42
  (723 shorter events, 356.0 us)
Async XLA Ops:
  7.2 60.2 %all-gather.4.cloned.1.call-start = ((), (), s32[]{:S(2)}) async-start(), calls=%async_computation.5 | async-start | bytes 5242880 | tf_op jit(solution)/shard_map/all_gather | solution.py:398
  11.8 162.4 %all-gather.6.cloned.1.call-start = ((), (), s32[]{:S(2)}) async-start(), calls=%async_computation.6 | async-start | bytes 16515072 | tf_op jit(solution)/shard_map/all_gather | solution.py:411
  15.6 237.9 %all-gather.8.cloned.1.call-start = ((), (), s32[]{:S(2)}) async-start(), calls=%async_computation.7 | async-start | bytes 10485760 | tf_op jit(solution)/shard_map/all_gather | solution.py:388
  72.2 37.5 %collective-permute-start.1 = (bf16[2,3,128,1024]{3,2,1,0:T(8,128)(2,1)S(1)}, bf16[2,3,128,1024]{3,2,1,0:T(8,128)(2,1)}, u32[]{:S(2)}, u32[]{:S(2)}) collective-permute-start(bf16[2,3,128,1024]{3,2,1,0:T(8,128)(2,1)S(1)} %pad_maximum_fusion.10), channel_id=1, source_target_pairs={{0,8},{1,9},{2,10},{3,11},{4,12},{5,13},{6,14},{7,15},{8,0},{9,1},... | collective-permute-start | bytes 4718600 | tf_op jit(solution)/shard_map/ppermute | solution.py:40
  75.1 67.1 %collective-permute-start.2 = (bf16[2,3,128,1024]{3,2,1,0:T(8,128)(2,1)}, bf16[2,3,128,1024]{3,2,1,0:T(8,128)(2,1)}, u32[]{:S(2)}, u32[]{:S(2)}) collective-permute-start(bf16[2,3,128,1024]{3,2,1,0:T(8,128)(2,1)} %pad_maximum_fusion.11), channel_id=1, source_target_pairs={{0,8},{1,9},{2,10},{3,11},{4,12},{5,13},{6,14},{7,15},{8,0},{9,1},... | collective-permute-start | bytes 4718600 | tf_op jit(solution)/shard_map/ppermute | solution.py:40
  76.1 71.0 %collective-permute-start = (bf16[512,1024]{0,1:T(8,128)(2,1)S(1)}, bf16[512,1024]{0,1:T(8,128)(2,1)}, u32[]{:S(2)}, u32[]{:S(2)}) collective-permute-start(bf16[512,1024]{0,1:T(8,128)(2,1)S(1)} %add_convert_fusion.6), channel_id=1, source_target_pairs={{0,4},{1,5},{2,6},{3,7},{4,0},{5,1},{6,2},{7,3},{8,12},{9,13},{10,... | collective-permute-start | bytes 3145736 | tf_op jit(solution)/shard_map/ppermute | solution.py:40
  165.2 234.8 %reduce-scatter.13.cloned.1.call-start = ((), (), s32[]{:S(2)}) async-start(), calls=%async_computation.8 | async-start | bytes 10485760
  226.9 26.6 %collective-permute-start.9 = (bf16[512,1024]{0,1:T(8,128)(2,1)S(1)}, bf16[512,1024]{0,1:T(8,128)(2,1)}, u32[]{:S(2)}, u32[]{:S(2)}) collective-permute-start(bf16[512,1024]{0,1:T(8,128)(2,1)S(1)} %add_convert_fusion.3), channel_id=1, source_target_pairs={{0,4},{1,5},{2,6},{3,7},{4,0},{5,1},{6,2},{7,3},{8,12},{9,13},{10,... | collective-permute-start | bytes 3145736 | tf_op jit(solution)/shard_map/ppermute | solution.py:40
  308.4 152.9 %reduce-scatter.15.cloned.1.call-start = ((), (), s32[]{:S(2)}) async-start(), calls=%async_computation.9 | async-start | bytes 3932160
  384.9 29.0 %collective-permute-start.19 = (bf16[4,3,128,1024]{3,2,1,0:T(8,128)(2,1)}, bf16[4,3,128,1024]{3,2,1,0:T(8,128)(2,1)}, u32[]{:S(2)}, u32[]{:S(2)}) collective-permute-start(bf16[4,3,128,1024]{3,2,1,0:T(8,128)(2,1)} %pad_maximum_fusion.3), channel_id=1, source_target_pairs={{0,4},{1,5},{2,6},{3,7},{4,0},{5,1},{6,2},{7,3},{8,12},{9,13},{10,... | collective-permute-start | bytes 9437192 | tf_op jit(solution)/shard_map/ppermute | solution.py:40
  417.9 137.7 %reduce-scatter.17.cloned.1.call-start = ((), (), s32[]{:S(2)}) async-start(), calls=%async_computation.10 | async-start | bytes 10485760
  461.3 147.8 %reduce-scatter.19.cloned.1.call-start = ((), (), s32[]{:S(2)}) async-start(), calls=%async_computation.11 | async-start | bytes 5242880
  473.9 61.3 %collective-permute-start.26 = (bf16[4,4,128,1024]{3,2,1,0:T(8,128)(2,1)}, bf16[4,4,128,1024]{3,2,1,0:T(8,128)(2,1)}, u32[]{:S(2)}, u32[]{:S(2)}) collective-permute-start(bf16[4,4,128,1024]{3,2,1,0:T(8,128)(2,1)} %pad_maximum_fusion.2), channel_id=1, source_target_pairs={{0,4},{1,5},{2,6},{3,7},{4,0},{5,1},{6,2},{7,3},{8,12},{9,13},{10,... | collective-permute-start | bytes 12582920 | tf_op jit(solution)/shard_map/ppermute | solution.py:40
  481.0 26.9 %collective-permute-start.30 = (bf16[2,2,2,32,1024]{4,3,2,1,0:T(8,128)(2,1)}, bf16[2,2,2,32,1024]{4,3,2,1,0:T(8,128)(2,1)}, u32[]{:S(2)}, u32[]{:S(2)}) collective-permute-start(bf16[2,2,2,32,1024]{4,3,2,1,0:T(8,128)(2,1)} %pad_maximum_fusion.16), channel_id=1, source_target_pairs={{0,16},{1,17},{2,18},{3,19},{4,20},{5,21},{6,22},{7,23},{8,24},{9,... | collective-permute-start | bytes 1572872 | tf_op jit(solution)/shard_map/ppermute | solution.py:40
  487.3 24.9 %collective-permute-start.27 = (bf16[2,2,2,32,1024]{4,3,2,1,0:T(8,128)(2,1)}, bf16[2,2,2,32,1024]{4,3,2,1,0:T(8,128)(2,1)}, u32[]{:S(2)}, u32[]{:S(2)}) collective-permute-start(bf16[2,2,2,32,1024]{4,3,2,1,0:T(8,128)(2,1)} %pad_maximum_fusion.15), channel_id=1, source_target_pairs={{0,8},{1,9},{2,10},{3,11},{4,12},{5,13},{6,14},{7,15},{8,0},{9,1},... | collective-permute-start | bytes 1572872 | tf_op jit(solution)/shard_map/ppermute | solution.py:40
  509.8 10.0 %collective-permute-start.31 = (bf16[1,2,2,32,1024]{4,3,2,1,0:T(8,128)(2,1)}, bf16[1,2,2,32,1024]{4,3,2,1,0:T(8,128)(2,1)S(1)}, u32[]{:S(2)}, u32[]{:S(2)}) collective-permute-start(bf16[1,2,2,32,1024]{4,3,2,1,0:T(8,128)(2,1)} %fusion.223), channel_id=1, source_target_pairs={{0,8},{1,9},{2,10},{3,11},{4,12},{5,13},{6,14},{7,15},{8,0},{9,1},... | collective-permute-start | bytes 786440 | tf_op jit(solution)/shard_map/ppermute | solution.py:40
  513.4 15.4 %collective-permute-start.28 = (bf16[1,2,2,32,1024]{4,3,2,1,0:T(8,128)(2,1)S(1)}, bf16[1,2,2,32,1024]{4,3,2,1,0:T(8,128)(2,1)S(1)}, u32[]{:S(2)}, u32[]{:S(2)}) collective-permute-start(bf16[1,2,2,32,1024]{4,3,2,1,0:T(8,128)(2,1)S(1)} %fusion.225), channel_id=1, source_target_pairs={{0,16},{1,17},{2,18},{3,19},{4,20},{5,21},{6,22},{7,23},{8,24},{9,... | collective-permute-start | bytes 786440 | tf_op jit(solution)/shard_map/ppermute | solution.py:40
  521.7 33.9 %collective-permute-start.32 = (bf16[2,32,1024]{2,1,0:T(8,128)(2,1)}, bf16[2,32,1024]{2,1,0:T(8,128)(2,1)S(1)}, u32[]{:S(2)}, u32[]{:S(2)}) collective-permute-start(bf16[2,32,1024]{2,1,0:T(8,128)(2,1)} %get-tuple-element.306), channel_id=1, source_target_pairs={{0,4},{1,5},{2,6},{3,7},{4,0},{5,1},{6,2},{7,3},{8,12},{9,13},{10,... | collective-permute-start | bytes 393224 | tf_op jit(solution)/shard_map/ppermute | solution.py:40
  530.7 24.8 %collective-permute-start.29 = (bf16[2,32,1024]{2,1,0:T(8,128)(2,1)}, bf16[2,32,1024]{2,1,0:T(8,128)(2,1)}, u32[]{:S(2)}, u32[]{:S(2)}) collective-permute-start(bf16[2,32,1024]{2,1,0:T(8,128)(2,1)} %get-tuple-element.308), channel_id=1, source_target_pairs={{0,4},{1,5},{2,6},{3,7},{4,0},{5,1},{6,2},{7,3},{8,12},{9,13},{10,... | collective-permute-start | bytes 393224 | tf_op jit(solution)/shard_map/ppermute | solution.py:40
  531.6 9.7 %collective-permute-start.35 = (bf16[2,1,1,32,1024]{4,3,2,1,0:T(8,128)(2,1)}, bf16[2,1,1,32,1024]{4,3,2,1,0:T(8,128)(2,1)}, u32[]{:S(2)}, u32[]{:S(2)}) collective-permute-start(bf16[2,1,1,32,1024]{4,3,2,1,0:T(8,128)(2,1)} %pad_maximum_fusion.20), channel_id=1, source_target_pairs={{0,16},{1,17},{2,18},{3,19},{4,20},{5,21},{6,22},{7,23},{8,24},{9,... | collective-permute-start | bytes 393224 | tf_op jit(solution)/shard_map/ppermute | solution.py:40
  532.4 12.6 %collective-permute-start.33 = (bf16[2,2,1,32,1024]{4,3,1,2,0:T(8,128)(2,1)}, bf16[2,2,1,32,1024]{4,3,1,2,0:T(8,128)(2,1)}, u32[]{:S(2)}, u32[]{:S(2)}) collective-permute-start(bf16[2,2,1,32,1024]{4,3,1,2,0:T(8,128)(2,1)} %pad_maximum_fusion.17), channel_id=1, source_target_pairs={{0,8},{1,9},{2,10},{3,11},{4,12},{5,13},{6,14},{7,15},{8,0},{9,1},... | collective-permute-start | bytes 786440 | tf_op jit(solution)/shard_map/ppermute | solution.py:40
  546.0 7.9 collective-permute-start.34
  565.6 25.9 %collective-permute-start.22 = (bf16[2,2,2,32,1024]{4,3,2,1,0:T(8,128)(2,1)S(1)}, bf16[2,2,2,32,1024]{4,3,2,1,0:T(8,128)(2,1)S(1)}, u32[]{:S(2)}, u32[]{:S(2)}) collective-permute-start(bf16[2,2,2,32,1024]{4,3,2,1,0:T(8,128)(2,1)S(1)} %pad_maximum_fusion.14), channel_id=1, source_target_pairs={{0,16},{1,17},{2,18},{3,19},{4,20},{5,21},{6,22},{7,23},{8,24},{9,... | collective-permute-start | bytes 1572872 | tf_op jit(solution)/shard_map/ppermute | solution.py:40
  568.9 25.2 %collective-permute-start.20 = (bf16[2,2,2,32,1024]{4,3,2,1,0:T(8,128)(2,1)S(1)}, bf16[2,2,2,32,1024]{4,3,2,1,0:T(8,128)(2,1)S(1)}, u32[]{:S(2)}, u32[]{:S(2)}) collective-permute-start(bf16[2,2,2,32,1024]{4,3,2,1,0:T(8,128)(2,1)S(1)} %pad_maximum_fusion.13), channel_id=1, source_target_pairs={{0,8},{1,9},{2,10},{3,11},{4,12},{5,13},{6,14},{7,15},{8,0},{9,1},... | collective-permute-start | bytes 1572872 | tf_op jit(solution)/shard_map/ppermute | solution.py:40
  591.6 10.9 %collective-permute-start.23 = (bf16[1,2,2,32,1024]{4,3,2,1,0:T(8,128)(2,1)S(1)}, bf16[1,2,2,32,1024]{4,3,2,1,0:T(8,128)(2,1)S(1)}, u32[]{:S(2)}, u32[]{:S(2)}) collective-permute-start(bf16[1,2,2,32,1024]{4,3,2,1,0:T(8,128)(2,1)S(1)} %fusion.227), channel_id=1, source_target_pairs={{0,8},{1,9},{2,10},{3,11},{4,12},{5,13},{6,14},{7,15},{8,0},{9,1},... | collective-permute-start | bytes 786440 | tf_op jit(solution)/shard_map/ppermute | solution.py:40
  594.2 14.1 %collective-permute-start.21 = (bf16[1,2,2,32,1024]{4,3,2,1,0:T(8,128)(2,1)S(1)}, bf16[1,2,2,32,1024]{4,3,2,1,0:T(8,128)(2,1)S(1)}, u32[]{:S(2)}, u32[]{:S(2)}) collective-permute-start(bf16[1,2,2,32,1024]{4,3,2,1,0:T(8,128)(2,1)S(1)} %fusion.229), channel_id=1, source_target_pairs={{0,16},{1,17},{2,18},{3,19},{4,20},{5,21},{6,22},{7,23},{8,24},{9,... | collective-permute-start | bytes 786440 | tf_op jit(solution)/shard_map/ppermute | solution.py:40
  612.0 14.6 %collective-permute-start.39 = (bf16[2,2,1,32,1024]{4,3,1,2,0:T(8,128)(2,1)S(1)}, bf16[2,2,1,32,1024]{4,3,1,2,0:T(8,128)(2,1)S(1)}, u32[]{:S(2)}, u32[]{:S(2)}) collective-permute-start(bf16[2,2,1,32,1024]{4,3,1,2,0:T(8,128)(2,1)S(1)} %pad_maximum_fusion.19), channel_id=1, source_target_pairs={{0,16},{1,17},{2,18},{3,19},{4,20},{5,21},{6,22},{7,23},{8,24},{9,... | collective-permute-start | bytes 786440 | tf_op jit(solution)/shard_map/ppermute | solution.py:40
  612.2 14.8 %collective-permute-start.37 = (bf16[2,2,1,32,1024]{4,3,1,2,0:T(8,128)(2,1)S(1)}, bf16[2,2,1,32,1024]{4,3,1,2,0:T(8,128)(2,1)S(1)}, u32[]{:S(2)}, u32[]{:S(2)}) collective-permute-start(bf16[2,2,1,32,1024]{4,3,1,2,0:T(8,128)(2,1)S(1)} %pad_maximum_fusion.18), channel_id=1, source_target_pairs={{0,8},{1,9},{2,10},{3,11},{4,12},{5,13},{6,14},{7,15},{8,0},{9,1},... | collective-permute-start | bytes 786440 | tf_op jit(solution)/shard_map/ppermute | solution.py:40
  626.7 7.1 collective-permute-start.40
  627.0 9.0 %collective-permute-start.38 = (bf16[1,2,1,32,1024]{4,3,1,2,0:T(8,128)(2,1)S(1)}, bf16[1,2,1,32,1024]{4,3,1,2,0:T(8,128)(2,1)S(1)}, u32[]{:S(2)}, u32[]{:S(2)}) collective-permute-start(bf16[1,2,1,32,1024]{4,3,1,2,0:T(8,128)(2,1)S(1)} %fusion.253), channel_id=1, source_target_pairs={{0,16},{1,17},{2,18},{3,19},{4,20},{5,21},{6,22},{7,23},{8,24},{9,... | collective-permute-start | bytes 393224 | tf_op jit(solution)/shard_map/ppermute | solution.py:40
  639.7 54.7 %all-to-all-start = ((bf16[8,3,32,1024]{3,2,1,0:T(8,128)(2,1)}), bf16[8,3,32,1024]{3,2,1,0:T(8,128)(2,1)}, u32[]{:S(2)}, u32[]{:S(2)}) async-start(bf16[8,3,32,1024]{3,2,1,0:T(8,128)(2,1)} %bitcast.536), calls=%async_computation | async-start | bytes 3145728 | tf_op jit(solution)/shard_map/all_to_all | solution.py:599
  647.8 7.1 collective-permute-start.72
  661.3 23.0 %collective-permute-start.75 = (f32[15,1024]{1,0:T(8,128)S(1)}, f32[15,1024]{1,0:T(8,128)S(1)}, u32[]{:S(2)}, u32[]{:S(2)}) collective-permute-start(f32[15,1024]{1,0:T(8,128)S(1)} %add.992), channel_id=1, source_target_pairs={{0,8},{1,9},{2,10},{3,11},{4,12},{5,13},{6,14},{7,15},{8,0},{9,1},... | collective-permute-start | bytes 184328 | tf_op jit(solution)/shard_map/ppermute | solution.py:40
  684.3 6.3 collective-permute-start.76
  707.1 14.8 %collective-permute-start.44 = (bf16[512,512]{1,0:T(8,128)(2,1)S(1)}, bf16[512,512]{1,0:T(8,128)(2,1)S(1)}, u32[]{:S(2)}, u32[]{:S(2)}) collective-permute-start(bf16[512,512]{1,0:T(8,128)(2,1)S(1)} %convolution_convert_fusion.26), channel_id=1, source_target_pairs={{0,2},{1,3},{2,0},{3,1},{4,6},{5,7},{6,4},{7,5},{8,10},{9,11},{10,... | collective-permute-start | bytes 1572872 | tf_op jit(solution)/shard_map/ppermute | solution.py:40
  710.2 14.9 %collective-permute-start.42 = (bf16[512,512]{1,0:T(8,128)(2,1)S(1)}, bf16[512,512]{1,0:T(8,128)(2,1)S(1)}, u32[]{:S(2)}, u32[]{:S(2)}) collective-permute-start(bf16[512,512]{1,0:T(8,128)(2,1)S(1)} %convolution_convert_fusion.27), channel_id=1, source_target_pairs={{0,1},{1,0},{2,3},{3,2},{4,5},{5,4},{6,7},{7,6},{8,9},{9,8},{10,11... | collective-permute-start | bytes 1572872 | tf_op jit(solution)/shard_map/ppermute | solution.py:40
  712.0 21.2 %collective-permute-start.48 = (bf16[512,512]{1,0:T(8,128)(2,1)S(1)}, bf16[512,512]{1,0:T(8,128)(2,1)S(1)}, u32[]{:S(2)}, u32[]{:S(2)}) collective-permute-start(bf16[512,512]{1,0:T(8,128)(2,1)S(1)} %convolution_convert_fusion.23), channel_id=1, source_target_pairs={{0,2},{1,3},{2,0},{3,1},{4,6},{5,7},{6,4},{7,5},{8,10},{9,11},{10,... | collective-permute-start | bytes 1572872 | tf_op jit(solution)/shard_map/ppermute | solution.py:40
  713.0 23.3 %collective-permute-start.46 = (bf16[512,512]{1,0:T(8,128)(2,1)S(1)}, bf16[512,512]{1,0:T(8,128)(2,1)S(1)}, u32[]{:S(2)}, u32[]{:S(2)}) collective-permute-start(bf16[512,512]{1,0:T(8,128)(2,1)S(1)} %convolution_convert_fusion.24), channel_id=1, source_target_pairs={{0,1},{1,0},{2,3},{3,2},{4,5},{5,4},{6,7},{7,6},{8,9},{9,8},{10,11... | collective-permute-start | bytes 1572872 | tf_op jit(solution)/shard_map/ppermute | solution.py:40
  714.5 29.9 %collective-permute-start.52 = (bf16[512,512]{1,0:T(8,128)(2,1)S(1)}, bf16[512,512]{1,0:T(8,128)(2,1)S(1)}, u32[]{:S(2)}, u32[]{:S(2)}) collective-permute-start(bf16[512,512]{1,0:T(8,128)(2,1)S(1)} %convolution_convert_fusion.20), channel_id=1, source_target_pairs={{0,2},{1,3},{2,0},{3,1},{4,6},{5,7},{6,4},{7,5},{8,10},{9,11},{10,... | collective-permute-start | bytes 1572872 | tf_op jit(solution)/shard_map/ppermute | solution.py:40
  721.9 25.7 %collective-permute-start.50 = (bf16[512,512]{1,0:T(8,128)(2,1)S(1)}, bf16[512,512]{1,0:T(8,128)(2,1)S(1)}, u32[]{:S(2)}, u32[]{:S(2)}) collective-permute-start(bf16[512,512]{1,0:T(8,128)(2,1)S(1)} %convolution_convert_fusion.21), channel_id=1, source_target_pairs={{0,1},{1,0},{2,3},{3,2},{4,5},{5,4},{6,7},{7,6},{8,9},{9,8},{10,11... | collective-permute-start | bytes 1572872 | tf_op jit(solution)/shard_map/ppermute | solution.py:40
  725.1 28.1 %collective-permute-start.45 = (bf16[256,512]{1,0:T(8,128)(2,1)S(1)}, bf16[256,512]{1,0:T(8,128)(2,1)S(1)}, u32[]{:S(2)}, u32[]{:S(2)}) collective-permute-start(bf16[256,512]{1,0:T(8,128)(2,1)S(1)} %fusion.210), channel_id=1, source_target_pairs={{0,1},{1,0},{2,3},{3,2},{4,5},{5,4},{6,7},{7,6},{8,9},{9,8},{10,11... | collective-permute-start | bytes 786440 | tf_op jit(solution)/shard_map/ppermute | solution.py:40
  733.1 21.4 %collective-permute-start.43 = (bf16[256,512]{1,0:T(8,128)(2,1)S(1)}, bf16[256,512]{1,0:T(8,128)(2,1)S(1)}, u32[]{:S(2)}, u32[]{:S(2)}) collective-permute-start(bf16[256,512]{1,0:T(8,128)(2,1)S(1)} %fusion.212), channel_id=1, source_target_pairs={{0,2},{1,3},{2,0},{3,1},{4,6},{5,7},{6,4},{7,5},{8,10},{9,11},{10,... | collective-permute-start | bytes 786440 | tf_op jit(solution)/shard_map/ppermute | solution.py:40
  736.3 22.5 %collective-permute-start.49 = (bf16[256,512]{1,0:T(8,128)(2,1)S(1)}, bf16[256,512]{1,0:T(8,128)(2,1)S(1)}, u32[]{:S(2)}, u32[]{:S(2)}) collective-permute-start(bf16[256,512]{1,0:T(8,128)(2,1)S(1)} %fusion.206), channel_id=1, source_target_pairs={{0,1},{1,0},{2,3},{3,2},{4,5},{5,4},{6,7},{7,6},{8,9},{9,8},{10,11... | collective-permute-start | bytes 786440 | tf_op jit(solution)/shard_map/ppermute | solution.py:40
  744.4 15.8 %collective-permute-start.47 = (bf16[256,512]{1,0:T(8,128)(2,1)S(1)}, bf16[256,512]{1,0:T(8,128)(2,1)S(1)}, u32[]{:S(2)}, u32[]{:S(2)}) collective-permute-start(bf16[256,512]{1,0:T(8,128)(2,1)S(1)} %fusion.208), channel_id=1, source_target_pairs={{0,2},{1,3},{2,0},{3,1},{4,6},{5,7},{6,4},{7,5},{8,10},{9,11},{10,... | collective-permute-start | bytes 786440 | tf_op jit(solution)/shard_map/ppermute | solution.py:40
  747.6 16.9 %collective-permute-start.53 = (bf16[256,512]{1,0:T(8,128)(2,1)S(1)}, bf16[256,512]{1,0:T(8,128)(2,1)S(1)}, u32[]{:S(2)}, u32[]{:S(2)}) collective-permute-start(bf16[256,512]{1,0:T(8,128)(2,1)S(1)} %fusion.202), channel_id=1, source_target_pairs={{0,1},{1,0},{2,3},{3,2},{4,5},{5,4},{6,7},{7,6},{8,9},{9,8},{10,11... | collective-permute-start | bytes 786440 | tf_op jit(solution)/shard_map/ppermute | solution.py:40
  753.2 12.6 %collective-permute-start.51 = (bf16[256,512]{1,0:T(8,128)(2,1)S(1)}, bf16[256,512]{1,0:T(8,128)(2,1)S(1)}, u32[]{:S(2)}, u32[]{:S(2)}) collective-permute-start(bf16[256,512]{1,0:T(8,128)(2,1)S(1)} %fusion.204), channel_id=1, source_target_pairs={{0,2},{1,3},{2,0},{3,1},{4,6},{5,7},{6,4},{7,5},{8,10},{9,11},{10,... | collective-permute-start | bytes 786440 | tf_op jit(solution)/shard_map/ppermute | solution.py:40
  755.3 14.7 %collective-permute-start.55 = (bf16[256,512]{1,0:T(8,128)(2,1)S(1)}, bf16[256,512]{1,0:T(8,128)(2,1)S(1)}, u32[]{:S(2)}, u32[]{:S(2)}) collective-permute-start(bf16[256,512]{1,0:T(8,128)(2,1)S(1)} %get-tuple-element.199), channel_id=1, source_target_pairs={{0,1},{1,0},{2,3},{3,2},{4,5},{5,4},{6,7},{7,6},{8,9},{9,8},{10,11... | collective-permute-start | bytes 786440 | tf_op jit(solution)/shard_map/ppermute | solution.py:40
  758.8 14.0 %collective-permute-start.54 = (bf16[256,512]{1,0:T(8,128)(2,1)S(1)}, bf16[256,512]{1,0:T(8,128)(2,1)S(1)}, u32[]{:S(2)}, u32[]{:S(2)}) collective-permute-start(bf16[256,512]{1,0:T(8,128)(2,1)S(1)} %get-tuple-element.199), channel_id=1, source_target_pairs={{0,2},{1,3},{2,0},{3,1},{4,6},{5,7},{6,4},{7,5},{8,10},{9,11},{10,... | collective-permute-start | bytes 786440 | tf_op jit(solution)/shard_map/ppermute | solution.py:40
  760.2 12.5 %collective-permute-start.58 = (bf16[256,512]{1,0:T(8,128)(2,1)S(1)}, bf16[256,512]{1,0:T(8,128)(2,1)S(1)}, u32[]{:S(2)}, u32[]{:S(2)}) collective-permute-start(bf16[256,512]{1,0:T(8,128)(2,1)S(1)} %get-tuple-element.245), channel_id=1, source_target_pairs={{0,2},{1,3},{2,0},{3,1},{4,6},{5,7},{6,4},{7,5},{8,10},{9,11},{10,... | collective-permute-start | bytes 786440 | tf_op jit(solution)/shard_map/ppermute | solution.py:40
  764.4 16.7 %collective-permute-start.57 = (bf16[256,512]{1,0:T(8,128)(2,1)S(1)}, bf16[256,512]{1,0:T(8,128)(2,1)S(1)}, u32[]{:S(2)}, u32[]{:S(2)}) collective-permute-start(bf16[256,512]{1,0:T(8,128)(2,1)S(1)} %get-tuple-element.245), channel_id=1, source_target_pairs={{0,1},{1,0},{2,3},{3,2},{4,5},{5,4},{6,7},{7,6},{8,9},{9,8},{10,11... | collective-permute-start | bytes 786440 | tf_op jit(solution)/shard_map/ppermute | solution.py:40
  765.8 22.9 %collective-permute-start.61 = (bf16[256,512]{1,0:T(8,128)(2,1)S(1)}, bf16[256,512]{1,0:T(8,128)(2,1)S(1)}, u32[]{:S(2)}, u32[]{:S(2)}) collective-permute-start(bf16[256,512]{1,0:T(8,128)(2,1)S(1)} %get-tuple-element.203), channel_id=1, source_target_pairs={{0,1},{1,0},{2,3},{3,2},{4,5},{5,4},{6,7},{7,6},{8,9},{9,8},{10,11... | collective-permute-start | bytes 786440 | tf_op jit(solution)/shard_map/ppermute | solution.py:40
  770.0 9.2 %collective-permute-start.56 = (bf16[256,512]{1,0:T(8,128)(2,1)S(1)}, bf16[256,512]{1,0:T(8,128)(2,1)S(1)}, u32[]{:S(2)}, u32[]{:S(2)}) collective-permute-start(bf16[256,512]{1,0:T(8,128)(2,1)S(1)} %collective-permute-done.55), channel_id=1, source_target_pairs={{0,2},{1,3},{2,0},{3,1},{4,6},{5,7},{6,4},{7,5},{8,10},{9,11},{10,... | collective-permute-start | bytes 786440 | tf_op jit(solution)/shard_map/ppermute | solution.py:40
  772.7 14.2 %collective-permute-start.59 = (bf16[256,512]{1,0:T(8,128)(2,1)S(1)}, bf16[256,512]{1,0:T(8,128)(2,1)S(1)}, u32[]{:S(2)}, u32[]{:S(2)}) collective-permute-start(bf16[256,512]{1,0:T(8,128)(2,1)S(1)} %collective-permute-done.58), channel_id=1, source_target_pairs={{0,1},{1,0},{2,3},{3,2},{4,5},{5,4},{6,7},{7,6},{8,9},{9,8},{10,11... | collective-permute-start | bytes 786440 | tf_op jit(solution)/shard_map/ppermute | solution.py:40
  772.8 16.6 %collective-permute-start.60 = (bf16[256,512]{1,0:T(8,128)(2,1)S(1)}, bf16[256,512]{1,0:T(8,128)(2,1)S(1)}, u32[]{:S(2)}, u32[]{:S(2)}) collective-permute-start(bf16[256,512]{1,0:T(8,128)(2,1)S(1)} %get-tuple-element.203), channel_id=1, source_target_pairs={{0,2},{1,3},{2,0},{3,1},{4,6},{5,7},{6,4},{7,5},{8,10},{9,11},{10,... | collective-permute-start | bytes 786440 | tf_op jit(solution)/shard_map/ppermute | solution.py:40
  779.3 11.5 %collective-permute-start.64 = (bf16[256,512]{1,0:T(8,128)(2,1)S(1)}, bf16[256,512]{1,0:T(8,128)(2,1)S(1)}, u32[]{:S(2)}, u32[]{:S(2)}) collective-permute-start(bf16[256,512]{1,0:T(8,128)(2,1)S(1)} %get-tuple-element.247), channel_id=1, source_target_pairs={{0,2},{1,3},{2,0},{3,1},{4,6},{5,7},{6,4},{7,5},{8,10},{9,11},{10,... | collective-permute-start | bytes 786440 | tf_op jit(solution)/shard_map/ppermute | solution.py:40
  781.1 20.8 %collective-permute-start.63 = (bf16[256,512]{1,0:T(8,128)(2,1)S(1)}, bf16[256,512]{1,0:T(8,128)(2,1)S(1)}, u32[]{:S(2)}, u32[]{:S(2)}) collective-permute-start(bf16[256,512]{1,0:T(8,128)(2,1)S(1)} %get-tuple-element.247), channel_id=1, source_target_pairs={{0,1},{1,0},{2,3},{3,2},{4,5},{5,4},{6,7},{7,6},{8,9},{9,8},{10,11... | collective-permute-start | bytes 786440 | tf_op jit(solution)/shard_map/ppermute | solution.py:40
  786.9 16.5 %collective-permute-start.67 = (bf16[256,512]{1,0:T(8,128)(2,1)S(1)}, bf16[256,512]{1,0:T(8,128)(2,1)S(1)}, u32[]{:S(2)}, u32[]{:S(2)}) collective-permute-start(bf16[256,512]{1,0:T(8,128)(2,1)S(1)} %get-tuple-element.207), channel_id=1, source_target_pairs={{0,1},{1,0},{2,3},{3,2},{4,5},{5,4},{6,7},{7,6},{8,9},{9,8},{10,11... | collective-permute-start | bytes 786440 | tf_op jit(solution)/shard_map/ppermute | solution.py:40
  788.7 15.4 %collective-permute-start.70 = (bf16[256,512]{1,0:T(8,128)(2,1)S(1)}, bf16[256,512]{1,0:T(8,128)(2,1)S(1)}, u32[]{:S(2)}, u32[]{:S(2)}) collective-permute-start(bf16[256,512]{1,0:T(8,128)(2,1)S(1)} %get-tuple-element.249), channel_id=1, source_target_pairs={{0,2},{1,3},{2,0},{3,1},{4,6},{5,7},{6,4},{7,5},{8,10},{9,11},{10,... | collective-permute-start | bytes 786440 | tf_op jit(solution)/shard_map/ppermute | solution.py:40
  789.4 11.4 %collective-permute-start.62 = (bf16[256,512]{1,0:T(8,128)(2,1)S(1)}, bf16[256,512]{1,0:T(8,128)(2,1)S(1)}, u32[]{:S(2)}, u32[]{:S(2)}) collective-permute-start(bf16[256,512]{1,0:T(8,128)(2,1)S(1)} %collective-permute-done.61), channel_id=1, source_target_pairs={{0,2},{1,3},{2,0},{3,1},{4,6},{5,7},{6,4},{7,5},{8,10},{9,11},{10,... | collective-permute-start | bytes 786440 | tf_op jit(solution)/shard_map/ppermute | solution.py:40
  790.8 14.6 %collective-permute-start.65 = (bf16[256,512]{1,0:T(8,128)(2,1)S(1)}, bf16[256,512]{1,0:T(8,128)(2,1)S(1)}, u32[]{:S(2)}, u32[]{:S(2)}) collective-permute-start(bf16[256,512]{1,0:T(8,128)(2,1)S(1)} %collective-permute-done.64), channel_id=1, source_target_pairs={{0,1},{1,0},{2,3},{3,2},{4,5},{5,4},{6,7},{7,6},{8,9},{9,8},{10,11... | collective-permute-start | bytes 786440 | tf_op jit(solution)/shard_map/ppermute | solution.py:40
  800.9 7.5 collective-permute-start.66
  802.0 9.7 %collective-permute-start.69 = (bf16[256,512]{1,0:T(8,128)(2,1)S(1)}, bf16[256,512]{1,0:T(8,128)(2,1)S(1)}, u32[]{:S(2)}, u32[]{:S(2)}) collective-permute-start(bf16[256,512]{1,0:T(8,128)(2,1)S(1)} %get-tuple-element.249), channel_id=1, source_target_pairs={{0,1},{1,0},{2,3},{3,2},{4,5},{5,4},{6,7},{7,6},{8,9},{9,8},{10,11... | collective-permute-start | bytes 786440 | tf_op jit(solution)/shard_map/ppermute | solution.py:40
  803.4 7.8 collective-permute-start.68
  804.1 9.7 %collective-permute-start.71 = (bf16[256,512]{1,0:T(8,128)(2,1)S(1)}, bf16[256,512]{1,0:T(8,128)(2,1)S(1)}, u32[]{:S(2)}, u32[]{:S(2)}) collective-permute-start(bf16[256,512]{1,0:T(8,128)(2,1)S(1)} %collective-permute-done.70), channel_id=1, source_target_pairs={{0,1},{1,0},{2,3},{3,2},{4,5},{5,4},{6,7},{7,6},{8,9},{9,8},{10,11... | collective-permute-start | bytes 786440 | tf_op jit(solution)/shard_map/ppermute | solution.py:40
  (188 other events, 2278.1 us)
Sparse Core Ops, SparseCore 0:
  11.9 55.3 all-gather.3
  69.8 80.9 all-gather.5
  165.3 88.1 all-gather.7
  308.5 86.5 reduce-scatter.12
  418.0 43.2 reduce-scatter.14
  464.5 86.4 reduce-scatter.16
  555.8 51.6 reduce-scatter.18

commit v4 on v3

--- a/solution.py
+++ b/solution.py
@@ -204,6 +204,32 @@
     )(jnp.stack([side, shard]), fetched, arrived, local)
 
 
+def turn(starts, square):
+    count = square.shape[0]
+    n_shards = starts.shape[0]
+    size = D // n_shards
+
+    def kernel(starts_ref, square_ref, out_ref):
+        for place in range(n_shards):
+            at = pl.multiple_of(starts_ref[place] * size, size)
+            out_ref[0, :, place * size : (place + 1) * size] = square_ref[0, :, pl.ds(at, size)]
+
+    return pl.pallas_call(
+        kernel,
+        grid_spec=pltpu.PrefetchScalarGridSpec(
+            num_scalar_prefetch=1,
+            grid=(count, n_shards),
+            in_specs=[pl.BlockSpec((1, size, D), lambda b, i, s: (b, s[i], 0))],
+            out_specs=pl.BlockSpec((1, size, D), lambda b, i, s: (b, i, 0)),
+        ),
+        out_shape=jax.ShapeDtypeStruct(square.shape, square.dtype),
+        cost_estimate=pl.CostEstimate(
+            flops=0, bytes_accessed=count * 4 * D * D, transcendentals=0
+        ),
+        name="turn",
+    )(starts, square)
+
+
 def deal(chosen, used, parts):
     n_slots = chosen.shape[0]
     sizes = [part.shape[0] for part in parts]
@@ -266,7 +292,7 @@
             in_specs=[pl.BlockSpec((tokens, D), lambda b, s: (0, base + stride * b))],
             out_specs=pl.BlockSpec((tokens, n_blocks * D), lambda b, s: (0, 0)),
         ),
-        out_shape=jax.ShapeDtypeStruct((tokens, n_blocks * D), BF),
+        out_shape=jax.ShapeDtypeStruct((tokens, n_blocks * D), value.dtype),
         cost_estimate=pl.CostEstimate(
             flops=0, bytes_accessed=4 * tokens * n_blocks * D, transcendentals=0
         ),
@@ -469,7 +495,15 @@
     weights1 = fetch_shared(0)
     weights_middle = fetch_half(base_attn, base_last)
     start_x = frames.astype(F32).reshape(tokens, D)
-    start_x, own2 = lax.optimization_barrier((start_x, own_share(base_last)))
+    capacity = left_bases.shape[0]
+    slots = range(capacity)
+    near = fsdp ^ jnp.arange(n_fsdp, dtype=jnp.int32)
+    rights = [regroup(near, right_bases[slot].astype(BF)) for slot in slots]
+    firsts = [regroup(near, block_first[slot]) for slot in slots]
+    seconds = [regroup(near, block_second[slot]) for slot in slots]
+    start_x, own2, rights, firsts, seconds = lax.optimization_barrier(
+        (start_x, own_share(base_last), rights, firsts, seconds)
+    )
     weights2 = fetch_own(own2)
     w_attn, w_conv = weights_middle[:4], weights_middle[4:]
     lifted1, ffn1_pullback, normed_pair1 = feed_up(start_x, 0, weights1)
@@ -523,7 +557,6 @@
     grad_a, grad_g, taps_grad = gated_pullback(conv_grad)
     grad_a, grad_g = grad_a.astype(BF), grad_g.astype(BF)
     shared_conv = share([t_mm(conv_low, grad_a), t_mm(conv_low, grad_g), grad_back])
-    summed_conv = scatter(shared_conv)
     part_x, conv_gain, conv_shift = conv_pullback(
         mm_t(grad_a, w_conv[0]) + mm_t(grad_g, w_conv[1])
     )
@@ -536,9 +569,10 @@
     query_low = (query_grad.reshape(tokens, D) * scale_head).astype(BF)
     key_low = key_grad.reshape(tokens, D).astype(BF)
     value_low = value_grad.reshape(tokens, D).astype(BF)
-    query_low, key_low, value_low, summed2 = lax.optimization_barrier(
-        (query_low, key_low, value_low, summed2)
-    )
+    query_low, key_low, value_low, summed2, shared_conv = lax.optimization_barrier(
+        (query_low, key_low, value_low, summed2, shared_conv)
+    )
+    summed_conv = scatter(shared_conv)
     grad_heads = [t_mm(attn_low, held) for held in (query_low, key_low, value_low)]
     grad_proj = t_mm(context_low, branch_low)
     part_x, attn_gain, attn_shift = attn_pullback(
@@ -568,6 +602,8 @@
     )
     spread_dp(summed1, 2, "ffn1")
     summed_attn = after(summed_attn, *[sums["ffn1" + place] for place in "xy"])
+    left_own = after(left_bases.astype(BF), summed_attn)
+    left_all = lax.all_gather(left_own, "fsdp", axis=1, tiled=True)
     spread_dp(summed_attn, 1, "attn")
     summed_small = total(local_small)
     small_grads = jnp.concatenate(
@@ -588,7 +624,6 @@
         away = (index // per_core != core).astype(jnp.int32)
         places.append(base + (2 * away + is_out) * per_core + index % per_core)
     places = jnp.concatenate(places)
-    capacity = (n_blocks + n_dp - 1) // n_dp
     matches = slot_tables(owners, n_dp, n_blocks).astype(jnp.int32)
     slot_block = jnp.sum(matches * jnp.arange(n_blocks, dtype=jnp.int32)[None], axis=1)
     slot_used = jnp.sum(matches, axis=1)
@@ -603,46 +638,29 @@
     dp_here = lax.axis_index(DP)
     my_blocks = lax.dynamic_slice_in_dim(slot_block, dp_here * capacity, capacity)
     my_used = lax.dynamic_slice_in_dim(slot_used, dp_here * capacity, capacity).astype(F32)
-    rotated_list, weight_list = [], []
-    sides = [slice(0, D // 2), slice(D // 2, D)]
-    for slot in range(capacity):
-        right_basis = right_bases[slot].astype(BF)
-        left_low = left_bases[slot].astype(BF)
-        lefts = [regroup(held, left_low) for held in shards]
-        product = mm(owned_list[slot], right_basis).astype(BF)
-        sink = {}
-        run(
-            *[
-                halve(
-                    routes[i],
-                    t_mm(lefts[i][:, : D // 2], product[:, sides[i]]),
-                    t_mm(lefts[i][:, D // 2 :], product[:, sides[i]]).astype(BF),
-                    sink,
-                    i,
-                )
-                for i in (0, 1)
-            ]
-        )
-        sinks = [{}, {}]
-        tasks = []
-        for i in (0, 1):
-            first_step = 0.5 * block_first[slot][:, sides[i]] + 0.5 * sink[i]
-            second_step = 0.5 * block_second[slot][:, sides[i]] + 0.5 * sink[i] * sink[i]
-            direction = (first_step / (jnp.sqrt(second_step) + EPS_ADAM)).astype(BF)
-            tasks.append(fetch(routes[i], direction, sinks[i]))
-        run(*tasks)
-        rotated_list.append(jnp.concatenate([sink[0], sink[1]], axis=1))
-        mixed = [
-            mm(
-                lefts[i], jnp.concatenate([sinks[i][place] for place in range(n_fsdp)], axis=0)
-            ).astype(BF)
-            for i in (0, 1)
-        ]
-        update = mm_t(jnp.concatenate(mixed, axis=1), right_basis)
+    lefts = turn(near, left_all)
+    used = my_used[:, None, None]
+
+    def exchange(value, axis):
+        parts = jnp.split(value.astype(BF), n_fsdp, axis=axis)
+        return [parts[0]] + [swap(parts[i], 0, i) for i in range(1, n_fsdp)]
+
+    turned_list, weight_list = [], []
+    for slot in slots:
+        product = mm(owned_list[slot], rights[slot])
+        columns = jnp.concatenate(exchange(product, 1), axis=0)
+        turned = jnp.concatenate(exchange(t_mm(lefts[slot], columns), 0), axis=1)
+        turned_list.append(turned)
+        turned = turned.astype(F32)
+        first_step = BETA_DECAY * firsts[slot] + (1.0 - BETA_DECAY) * turned
+        second_step = BETA_DECAY * seconds[slot] + (1.0 - BETA_DECAY) * turned * turned
+        direction = first_step / (jnp.sqrt(second_step) + EPS_ADAM)
+        columns = jnp.concatenate(exchange(direction, 1), axis=0)
+        mixed = jnp.concatenate(exchange(mm(lefts[slot], columns), 0), axis=1)
+        update = mm_t(mixed, rights[slot])
         master = pick(blocks, 0, my_blocks[slot])
         weight_list.append(master - LEARN_RATE * (update + DECAY_WEIGHT * master))
-    used = my_used[:, None, None]
-    rotated = jnp.stack(rotated_list)
+    rotated = jnp.stack([regroup(near, turned) for turned in turned_list]).astype(F32)
     first_step = BETA_DECAY * block_first + (1.0 - BETA_DECAY) * rotated
     second_step = BETA_DECAY * block_second + (1.0 - BETA_DECAY) * rotated * rotated
     small_first_new = BETA_DECAY * small_first + (1.0 - BETA_DECAY) * small_grads

time: 835 us -> 812 us (0.972)
  waiting for transfers between devices: 335 us -> 245 us
  Pallas kernels: 28 us -> 60.6 us
  starting transfers between devices: 77.4 us -> 95.4 us
  other arithmetic: 97.4 us -> 112 us
    ppermute x77 -> x83, waiting for transfers between devices: 251 us -> 200 us  [swap(): return lax.ppermute(value, AXES, pairs)]
    all_gather x1, waiting for transfers between devices: 45.7 us -> 2.64 us  [fetch_shared(): fetched = lax.all_gather(own, 'fsdp', axis=1, tiled=True)]
    pallas_call x6 -> x12, Pallas kernels: 16 us -> 38.5 us  [regroup(): pl.pallas_call(kernel, grid_spec=pltpu.PrefetchScalarGridSpec(num_scalar_...]
    ppermute x77 -> x83, starting transfers between devices: 72.1 us -> 89.4 us  [swap(): return lax.ppermute(value, AXES, pairs)]
    pallas_call x0 -> x1, Pallas kernels: none -> 10.3 us  [turn(): pl.pallas_call(kernel, grid_spec=pltpu.PrefetchScalarGridSpec(num_scalar_...]
    dot_general x27 -> x18, matrix products: 44.9 us -> 40.7 us  [t_mm(): lax.dot_general(left, right, (((0,), (0,)), ((), ())), preferred_element_...]
    dot_general x24 -> x21, matrix products: 55.9 us -> 53 us  [mm(): return jnp.dot(left, right, preferred_element_type=F32)]
    unnamed x338 -> x350, local copies, waits for them, and re-layouts: 36.1 us -> 36.9 us
  transfers between devices with their start and end apart: 85 -> 92, of which waited for: 54 -> 42; matrix products, arithmetic and copies ran while one was open for 31% -> 34% of each run, Pallas kernels for 3% -> 8%
where the time goes in v4:
time: 812 us; the launch traced here: 803 us
  waiting for transfers between devices  245 us (30%)
  matrix products  175 us (22%)
  other arithmetic  112 us (14%)
  starting transfers between devices  95.4 us (12%)
  local copies, waits for them, and re-layouts  86.7 us (11%)
  Pallas kernels  60.6 us (7%)
  between operations  28.5 us (4%)
    ppermute x83, waiting for transfers between devices, swap(): return lax.ppermute(value, AXES, pairs)  200 us
    ppermute x83, starting transfers between devices, swap(): return lax.ppermute(value, AXES, pairs)  89.4 us
    dot_general x18, matrix products, mm_t(): lax.dot_general(left, right, (((1,), (1,)), ((), ())), preferred_element_...  63.3 us
    dot_general x21, matrix products, mm(): return jnp.dot(left, right, preferred_element_type=F32)  53 us
    dot_general x18, matrix products, t_mm(): lax.dot_general(left, right, (((0,), (0,)), ((), ())), preferred_element_...  40.7 us
    pallas_call x12, Pallas kernels, regroup(): pl.pallas_call(kernel, grid_spec=pltpu.PrefetchScalarGridSpec(num_scalar_...  38.5 us
    unnamed x350, local copies, waits for them, and re-layouts  36.9 us
    all_gather x1, waiting for transfers between devices, fetch_own(): fetched = lax.all_gather(own, 'fsdp', axis=1, tiled=True)  26.1 us
  transfers between devices with their start and end apart: 92, of which 42 were waited for; matrix products, arithmetic and copies ran while one was open for 34% of the time, Pallas kernels for 8%

profile of v4, /device:TPU:0, one launch (start us, length us, event | category | flops | bytes accessed | tf_op | source)
XLA Modules:
  0.0 803.1 jit_solution(7601611566346348779)
XLA Ops:
  7.2 3.5 dynamic-slice_convert_fusion.4
  11.9 3.6 dynamic-slice_convert_fusion
  15.5 5.6 convert.23
  24.5 3.8 regroup.12
  28.4 3.9 regroup.13
  32.2 4.1 regroup.14
  41.1 3.9 regroup.16
  52.6 3.2 regroup.19
  76.9 32.8 %collective-permute-done.1.arrived_ref = bf16[2,3,128,1024]{3,2,1,0:T(8,128)(2,1)} collective-permute-done((bf16[2,3,128,1024]{3,2,1,0:T(8,128)(2,1)S(1)}, bf16[2,3,128,1024]{3,2,1,0:T(8,128)(2,1)}, u32[]{:S(2)}, u32[]{:S(2)}) %collective-permute-start.1) | collective-permute-done | bytes 1572896 | tf_op jit(solution)/shard_map/ppermute | solution.py:40
  109.7 4.4 interleave.2
  114.1 28.2 %collective-permute-done.2.arrived_ref = bf16[2,3,128,1024]{3,2,1,0:T(8,128)(2,1)} collective-permute-done((bf16[2,3,128,1024]{3,2,1,0:T(8,128)(2,1)}, bf16[2,3,128,1024]{3,2,1,0:T(8,128)(2,1)}, u32[]{:S(2)}, u32[]{:S(2)}) %collective-permute-start.2) | collective-permute-done | bytes 1572896 | tf_op jit(solution)/shard_map/ppermute | solution.py:40
  142.2 4.5 interleave.3
  146.7 4.4 convolution_convert_fusion.18
  151.2 4.4 convolution_convert_fusion.17
  173.8 3.4 fusion.94
  178.2 4.2 multiply_convert_fusion.7
  183.9 3.2 fusion.100
  226.8 26.1 %all-gather.9.cloned.1.call-done = bf16[4,1024,1024]{2,1,0:T(8,128)(2,1)} async-done(((bf16[4,256,1024]{2,1,0:T(8,128)(2,1)}), bf16[4,1024,1024]{2,1,0:T(8,128)(2,1)}) %all-gather.9.cloned.1.call-update) | async-done | bytes 8388624 | tf_op jit(solution)/shard_map/all_gather | solution.py:414
  253.0 4.4 convolution_convert_fusion.15
  257.4 4.4 convolution_convert_fusion.16
  284.5 3.4 fusion.27
  288.0 3.7 fusion.35
  296.7 3.6 convolution_convert_fusion.14
  300.2 3.6 convolution_convert_fusion.13
  303.8 4.0 pad_maximum_fusion
  308.3 4.7 fusion.82
  313.1 4.2 convolution_add_fusion.1
  317.5 4.1 collective-permute-done.12
  327.4 6.0 fusion.274
  343.5 3.2 convolution_convert_fusion.8
  367.0 3.3 fusion.76
  370.4 4.1 multiply_reduce_fusion.3
  377.8 3.9 fusion.93
  384.4 6.8 multiply_reduce_fusion
  398.2 3.2 fusion.97
  401.4 3.9 add_convert_fusion.1
  405.3 3.2 fusion.72
  408.6 3.0 fusion.70
  411.6 3.4 fusion.272
  421.5 5.5 fusion.11
  427.0 4.4 convolution_convert_fusion.7
  431.4 3.5 fusion.19
  435.0 4.4 convolution_convert_fusion.6
  444.4 4.0 pad_maximum_fusion.1
  448.3 14.3 %reduce-scatter.15.cloned.1.call-done = bf16[1,3,128,1024]{3,2,1,0:T(8,128)(2,1)} async-done(((bf16[4,3,128,1024]{3,2,1,0:T(8,128)(2,1)}), bf16[1,3,128,1024]{3,2,1,0:T(8,128)(2,1)}) %reduce-scatter.15.cloned.1.call-update) | async-done | bytes 786448
  490.6 18.5 %collective-permute-done.30 = bf16[2,2,2,32,1024]{4,3,2,1,0:T(8,128)(2,1)} collective-permute-done((bf16[2,2,2,32,1024]{4,3,2,1,0:T(8,128)(2,1)}, bf16[2,2,2,32,1024]{4,3,2,1,0:T(8,128)(2,1)}, u32[]{:S(2)}, u32[]{:S(2)}) %collective-permute-start.30) | collective-permute-done | bytes 524320 | tf_op jit(solution)/shard_map/ppermute | solution.py:40
  514.6 3.6 collective-permute-start.28
  523.0 7.1 collective-permute-done.28
  536.5 4.9 add_convert_fusion
  549.3 6.0 collective-permute-done.34
  564.3 20.3 %collective-permute-done.22 = bf16[2,2,2,32,1024]{4,3,2,1,0:T(8,128)(2,1)S(1)} collective-permute-done((bf16[2,2,2,32,1024]{4,3,2,1,0:T(8,128)(2,1)S(1)}, bf16[2,2,2,32,1024]{4,3,2,1,0:T(8,128)(2,1)S(1)}, u32[]{:S(2)}, u32[]{:S(2)}) %collective-permute-start.22) | collective-permute-done | bytes 524320 | tf_op jit(solution)/shard_map/ppermute | solution.py:40
  592.1 4.1 collective-permute-done.23
  597.0 8.2 %collective-permute-done.21 = bf16[1,2,2,32,1024]{4,3,2,1,0:T(8,128)(2,1)S(1)} collective-permute-done((bf16[1,2,2,32,1024]{4,3,2,1,0:T(8,128)(2,1)S(1)}, bf16[1,2,2,32,1024]{4,3,2,1,0:T(8,128)(2,1)S(1)}, u32[]{:S(2)}, u32[]{:S(2)}) %collective-permute-start.21) | collective-permute-done | bytes 262176 | tf_op jit(solution)/shard_map/ppermute | solution.py:40
  620.1 8.7 %collective-permute-done.39 = bf16[2,2,1,32,1024]{4,3,1,2,0:T(8,128)(2,1)S(1)} collective-permute-done((bf16[2,2,1,32,1024]{4,3,1,2,0:T(8,128)(2,1)S(1)}, bf16[2,2,1,32,1024]{4,3,1,2,0:T(8,128)(2,1)S(1)}, u32[]{:S(2)}, u32[]{:S(2)}) %collective-permute-start.39) | collective-permute-done | bytes 262176 | tf_op jit(solution)/shard_map/ppermute | solution.py:40
  629.4 3.4 collective-permute-start.38
  632.8 3.3 collective-permute-done.40
  642.8 4.7 all-to-all-start
  647.8 3.0 fusion.58
  652.4 4.9 collective-permute-done.78
  658.6 4.6 collective-permute-done.79
  675.2 4.6 collective-permute-start.82
  681.8 6.2 collective-permute-done.82
  704.7 10.3 %turn.1 = bf16[3,1024,1024]{2,1,0:T(8,128)(2,1)} custom-call(s32[4]{0:T(128)} %iota_xor_fusion.starts_ref, bf16[3,1024,1024]{2,1,0:T(8,128)(2,1)} %all-gather.11.cloned.1.call-done.square_ref), custom_call_target="tpu_custom_call" | custom-call | bytes 12582912 | tf_op jit(solution)/shard_map/turn/pallas_call | solution.py:217
  791.7 4.4 fusion.42
  (753 shorter events, 376.8 us)
Async XLA Ops:
  7.2 60.2 %all-gather.5.cloned.1.call-start = ((), (), s32[]{:S(2)}) async-start(), calls=%async_computation.5 | async-start | bytes 5242880 | tf_op jit(solution)/shard_map/all_gather | solution.py:424
  11.8 162.0 %all-gather.7.cloned.1.call-start = ((), (), s32[]{:S(2)}) async-start(), calls=%async_computation.6 | async-start | bytes 16515072 | tf_op jit(solution)/shard_map/all_gather | solution.py:437
  15.5 237.5 %all-gather.9.cloned.1.call-start = ((), (), s32[]{:S(2)}) async-start(), calls=%async_computation.7 | async-start | bytes 10485760 | tf_op jit(solution)/shard_map/all_gather | solution.py:414
  72.2 37.5 %collective-permute-start.1 = (bf16[2,3,128,1024]{3,2,1,0:T(8,128)(2,1)S(1)}, bf16[2,3,128,1024]{3,2,1,0:T(8,128)(2,1)}, u32[]{:S(2)}, u32[]{:S(2)}) collective-permute-start(bf16[2,3,128,1024]{3,2,1,0:T(8,128)(2,1)S(1)} %pad_maximum_fusion.9), channel_id=1, source_target_pairs={{0,8},{1,9},{2,10},{3,11},{4,12},{5,13},{6,14},{7,15},{8,0},{9,1},... | collective-permute-start | bytes 4718600 | tf_op jit(solution)/shard_map/ppermute | solution.py:40
  75.1 67.1 %collective-permute-start.2 = (bf16[2,3,128,1024]{3,2,1,0:T(8,128)(2,1)}, bf16[2,3,128,1024]{3,2,1,0:T(8,128)(2,1)}, u32[]{:S(2)}, u32[]{:S(2)}) collective-permute-start(bf16[2,3,128,1024]{3,2,1,0:T(8,128)(2,1)} %pad_maximum_fusion.10), channel_id=1, source_target_pairs={{0,8},{1,9},{2,10},{3,11},{4,12},{5,13},{6,14},{7,15},{8,0},{9,1},... | collective-permute-start | bytes 4718600 | tf_op jit(solution)/shard_map/ppermute | solution.py:40
  76.1 70.7 %collective-permute-start = (bf16[512,1024]{0,1:T(8,128)(2,1)S(1)}, bf16[512,1024]{0,1:T(8,128)(2,1)}, u32[]{:S(2)}, u32[]{:S(2)}) collective-permute-start(bf16[512,1024]{0,1:T(8,128)(2,1)S(1)} %add_convert_fusion.6), channel_id=1, source_target_pairs={{0,4},{1,5},{2,6},{3,7},{4,0},{5,1},{6,2},{7,3},{8,12},{9,13},{10,... | collective-permute-start | bytes 3145736 | tf_op jit(solution)/shard_map/ppermute | solution.py:40
  164.8 240.5 %reduce-scatter.13.cloned.1.call-start = ((), (), s32[]{:S(2)}) async-start(), calls=%async_computation.9 | async-start | bytes 10485760
  226.7 26.2 %collective-permute-start.9 = (bf16[512,1024]{0,1:T(8,128)(2,1)S(1)}, bf16[512,1024]{0,1:T(8,128)(2,1)}, u32[]{:S(2)}, u32[]{:S(2)}) collective-permute-start(bf16[512,1024]{0,1:T(8,128)(2,1)S(1)} %add_convert_fusion.3), channel_id=1, source_target_pairs={{0,4},{1,5},{2,6},{3,7},{4,0},{5,1},{6,2},{7,3},{8,12},{9,13},{10,... | collective-permute-start | bytes 3145736 | tf_op jit(solution)/shard_map/ppermute | solution.py:40
  307.8 154.9 %reduce-scatter.15.cloned.1.call-start = ((), (), s32[]{:S(2)}) async-start(), calls=%async_computation.10 | async-start | bytes 3932160
  367.0 34.4 %collective-permute-start.18 = (bf16[4,3,128,1024]{3,2,1,0:T(8,128)(2,1)}, bf16[4,3,128,1024]{3,2,1,0:T(8,128)(2,1)}, u32[]{:S(2)}, u32[]{:S(2)}) collective-permute-start(bf16[4,3,128,1024]{3,2,1,0:T(8,128)(2,1)} %pad_maximum_fusion.3), channel_id=1, source_target_pairs={{0,4},{1,5},{2,6},{3,7},{4,0},{5,1},{6,2},{7,3},{8,12},{9,13},{10,... | collective-permute-start | bytes 9437192 | tf_op jit(solution)/shard_map/ppermute | solution.py:40
  419.2 137.8 %reduce-scatter.17.cloned.1.call-start = ((), (), s32[]{:S(2)}) async-start(), calls=%async_computation.11 | async-start | bytes 10485760
  462.7 146.0 %reduce-scatter.19.cloned.1.call-start = ((), (), s32[]{:S(2)}) async-start(), calls=%async_computation.12 | async-start | bytes 5242880
  475.5 61.1 %collective-permute-start.26 = (bf16[4,4,128,1024]{3,2,1,0:T(8,128)(2,1)}, bf16[4,4,128,1024]{3,2,1,0:T(8,128)(2,1)}, u32[]{:S(2)}, u32[]{:S(2)}) collective-permute-start(bf16[4,4,128,1024]{3,2,1,0:T(8,128)(2,1)} %pad_maximum_fusion.2), channel_id=1, source_target_pairs={{0,4},{1,5},{2,6},{3,7},{4,0},{5,1},{6,2},{7,3},{8,12},{9,13},{10,... | collective-permute-start | bytes 12582920 | tf_op jit(solution)/shard_map/ppermute | solution.py:40
  482.1 27.0 %collective-permute-start.30 = (bf16[2,2,2,32,1024]{4,3,2,1,0:T(8,128)(2,1)}, bf16[2,2,2,32,1024]{4,3,2,1,0:T(8,128)(2,1)}, u32[]{:S(2)}, u32[]{:S(2)}) collective-permute-start(bf16[2,2,2,32,1024]{4,3,2,1,0:T(8,128)(2,1)} %pad_maximum_fusion.16), channel_id=1, source_target_pairs={{0,16},{1,17},{2,18},{3,19},{4,20},{5,21},{6,22},{7,23},{8,24},{9,... | collective-permute-start | bytes 1572872 | tf_op jit(solution)/shard_map/ppermute | solution.py:40
  488.5 24.9 %collective-permute-start.27 = (bf16[2,2,2,32,1024]{4,3,2,1,0:T(8,128)(2,1)}, bf16[2,2,2,32,1024]{4,3,2,1,0:T(8,128)(2,1)}, u32[]{:S(2)}, u32[]{:S(2)}) collective-permute-start(bf16[2,2,2,32,1024]{4,3,2,1,0:T(8,128)(2,1)} %pad_maximum_fusion.15), channel_id=1, source_target_pairs={{0,8},{1,9},{2,10},{3,11},{4,12},{5,13},{6,14},{7,15},{8,0},{9,1},... | collective-permute-start | bytes 1572872 | tf_op jit(solution)/shard_map/ppermute | solution.py:40
  511.0 10.1 %collective-permute-start.31 = (bf16[1,2,2,32,1024]{4,3,2,1,0:T(8,128)(2,1)}, bf16[1,2,2,32,1024]{4,3,2,1,0:T(8,128)(2,1)S(1)}, u32[]{:S(2)}, u32[]{:S(2)}) collective-permute-start(bf16[1,2,2,32,1024]{4,3,2,1,0:T(8,128)(2,1)} %fusion.211), channel_id=1, source_target_pairs={{0,8},{1,9},{2,10},{3,11},{4,12},{5,13},{6,14},{7,15},{8,0},{9,1},... | collective-permute-start | bytes 786440 | tf_op jit(solution)/shard_map/ppermute | solution.py:40
  514.6 15.5 %collective-permute-start.28 = (bf16[1,2,2,32,1024]{4,3,2,1,0:T(8,128)(2,1)S(1)}, bf16[1,2,2,32,1024]{4,3,2,1,0:T(8,128)(2,1)S(1)}, u32[]{:S(2)}, u32[]{:S(2)}) collective-permute-start(bf16[1,2,2,32,1024]{4,3,2,1,0:T(8,128)(2,1)S(1)} %fusion.213), channel_id=1, source_target_pairs={{0,16},{1,17},{2,18},{3,19},{4,20},{5,21},{6,22},{7,23},{8,24},{9,... | collective-permute-start | bytes 786440 | tf_op jit(solution)/shard_map/ppermute | solution.py:40
  523.0 33.9 %collective-permute-start.32 = (bf16[2,32,1024]{2,1,0:T(8,128)(2,1)}, bf16[2,32,1024]{2,1,0:T(8,128)(2,1)S(1)}, u32[]{:S(2)}, u32[]{:S(2)}) collective-permute-start(bf16[2,32,1024]{2,1,0:T(8,128)(2,1)} %get-tuple-element.358), channel_id=1, source_target_pairs={{0,4},{1,5},{2,6},{3,7},{4,0},{5,1},{6,2},{7,3},{8,12},{9,13},{10,... | collective-permute-start | bytes 393224 | tf_op jit(solution)/shard_map/ppermute | solution.py:40
  532.0 24.9 %collective-permute-start.29 = (bf16[2,32,1024]{2,1,0:T(8,128)(2,1)}, bf16[2,32,1024]{2,1,0:T(8,128)(2,1)}, u32[]{:S(2)}, u32[]{:S(2)}) collective-permute-start(bf16[2,32,1024]{2,1,0:T(8,128)(2,1)} %get-tuple-element.360), channel_id=1, source_target_pairs={{0,4},{1,5},{2,6},{3,7},{4,0},{5,1},{6,2},{7,3},{8,12},{9,13},{10,... | collective-permute-start | bytes 393224 | tf_op jit(solution)/shard_map/ppermute | solution.py:40
  532.9 9.7 %collective-permute-start.35 = (bf16[2,1,1,32,1024]{4,3,2,1,0:T(8,128)(2,1)}, bf16[2,1,1,32,1024]{4,3,2,1,0:T(8,128)(2,1)}, u32[]{:S(2)}, u32[]{:S(2)}) collective-permute-start(bf16[2,1,1,32,1024]{4,3,2,1,0:T(8,128)(2,1)} %pad_maximum_fusion.23), channel_id=1, source_target_pairs={{0,16},{1,17},{2,18},{3,19},{4,20},{5,21},{6,22},{7,23},{8,24},{9,... | collective-permute-start | bytes 393224 | tf_op jit(solution)/shard_map/ppermute | solution.py:40
  533.8 12.5 %collective-permute-start.33 = (bf16[2,2,1,32,1024]{4,3,1,2,0:T(8,128)(2,1)}, bf16[2,2,1,32,1024]{4,3,1,2,0:T(8,128)(2,1)}, u32[]{:S(2)}, u32[]{:S(2)}) collective-permute-start(bf16[2,2,1,32,1024]{4,3,1,2,0:T(8,128)(2,1)} %pad_maximum_fusion.20), channel_id=1, source_target_pairs={{0,8},{1,9},{2,10},{3,11},{4,12},{5,13},{6,14},{7,15},{8,0},{9,1},... | collective-permute-start | bytes 786440 | tf_op jit(solution)/shard_map/ppermute | solution.py:40
  557.6 147.1 %all-gather.11.cloned.1.call-start = ((), (), s32[]{:S(2)}) async-start(), calls=%async_computation.8 | async-start | bytes 7864320 | tf_op jit(solution)/shard_map/all_gather | solution.py:606
  558.9 25.7 %collective-permute-start.22 = (bf16[2,2,2,32,1024]{4,3,2,1,0:T(8,128)(2,1)S(1)}, bf16[2,2,2,32,1024]{4,3,2,1,0:T(8,128)(2,1)S(1)}, u32[]{:S(2)}, u32[]{:S(2)}) collective-permute-start(bf16[2,2,2,32,1024]{4,3,2,1,0:T(8,128)(2,1)S(1)} %pad_maximum_fusion.14), channel_id=1, source_target_pairs={{0,16},{1,17},{2,18},{3,19},{4,20},{5,21},{6,22},{7,23},{8,24},{9,... | collective-permute-start | bytes 1572872 | tf_op jit(solution)/shard_map/ppermute | solution.py:40
  564.0 26.0 %collective-permute-start.20 = (bf16[2,2,2,32,1024]{4,3,2,1,0:T(8,128)(2,1)S(1)}, bf16[2,2,2,32,1024]{4,3,2,1,0:T(8,128)(2,1)S(1)}, u32[]{:S(2)}, u32[]{:S(2)}) collective-permute-start(bf16[2,2,2,32,1024]{4,3,2,1,0:T(8,128)(2,1)S(1)} %pad_maximum_fusion.13), channel_id=1, source_target_pairs={{0,8},{1,9},{2,10},{3,11},{4,12},{5,13},{6,14},{7,15},{8,0},{9,1},... | collective-permute-start | bytes 1572872 | tf_op jit(solution)/shard_map/ppermute | solution.py:40
  584.6 11.5 %collective-permute-start.23 = (bf16[1,2,2,32,1024]{4,3,2,1,0:T(8,128)(2,1)S(1)}, bf16[1,2,2,32,1024]{4,3,2,1,0:T(8,128)(2,1)S(1)}, u32[]{:S(2)}, u32[]{:S(2)}) collective-permute-start(bf16[1,2,2,32,1024]{4,3,2,1,0:T(8,128)(2,1)S(1)} %fusion.215), channel_id=1, source_target_pairs={{0,8},{1,9},{2,10},{3,11},{4,12},{5,13},{6,14},{7,15},{8,0},{9,1},... | collective-permute-start | bytes 786440 | tf_op jit(solution)/shard_map/ppermute | solution.py:40
  589.7 20.1 %collective-permute-start.41 = (f32[512,1024]{0,1:T(8,128)}, f32[512,1024]{0,1:T(8,128)}, u32[]{:S(2)}, u32[]{:S(2)}) collective-permute-start(f32[512,1024]{0,1:T(8,128)} %slice.629), channel_id=1, source_target_pairs={{0,4},{1,5},{2,6},{3,7},{4,0},{5,1},{6,2},{7,3},{8,12},{9,13},{10,... | collective-permute-start | bytes 6291464 | tf_op jit(solution)/shard_map/ppermute | solution.py:40
  590.1 15.1 %collective-permute-start.21 = (bf16[1,2,2,32,1024]{4,3,2,1,0:T(8,128)(2,1)S(1)}, bf16[1,2,2,32,1024]{4,3,2,1,0:T(8,128)(2,1)S(1)}, u32[]{:S(2)}, u32[]{:S(2)}) collective-permute-start(bf16[1,2,2,32,1024]{4,3,2,1,0:T(8,128)(2,1)S(1)} %fusion.217), channel_id=1, source_target_pairs={{0,16},{1,17},{2,18},{3,19},{4,20},{5,21},{6,22},{7,23},{8,24},{9,... | collective-permute-start | bytes 786440 | tf_op jit(solution)/shard_map/ppermute | solution.py:40
  597.0 11.8 %collective-permute-start.25 = (bf16[2,32,1024]{2,1,0:T(8,128)(2,1)S(1)}, bf16[2,32,1024]{2,1,0:T(8,128)(2,1)S(1)}, u32[]{:S(2)}, u32[]{:S(2)}) collective-permute-start(bf16[2,32,1024]{2,1,0:T(8,128)(2,1)S(1)} %get-tuple-element.362), channel_id=1, source_target_pairs={{0,4},{1,5},{2,6},{3,7},{4,0},{5,1},{6,2},{7,3},{8,12},{9,13},{10,... | collective-permute-start | bytes 393224 | tf_op jit(solution)/shard_map/ppermute | solution.py:40
  614.1 14.7 %collective-permute-start.39 = (bf16[2,2,1,32,1024]{4,3,1,2,0:T(8,128)(2,1)S(1)}, bf16[2,2,1,32,1024]{4,3,1,2,0:T(8,128)(2,1)S(1)}, u32[]{:S(2)}, u32[]{:S(2)}) collective-permute-start(bf16[2,2,1,32,1024]{4,3,1,2,0:T(8,128)(2,1)S(1)} %pad_maximum_fusion.22), channel_id=1, source_target_pairs={{0,16},{1,17},{2,18},{3,19},{4,20},{5,21},{6,22},{7,23},{8,24},{9,... | collective-permute-start | bytes 786440 | tf_op jit(solution)/shard_map/ppermute | solution.py:40
  616.6 12.7 %collective-permute-start.37 = (bf16[2,2,1,32,1024]{4,3,1,2,0:T(8,128)(2,1)S(1)}, bf16[2,2,1,32,1024]{4,3,1,2,0:T(8,128)(2,1)S(1)}, u32[]{:S(2)}, u32[]{:S(2)}) collective-permute-start(bf16[2,2,1,32,1024]{4,3,1,2,0:T(8,128)(2,1)S(1)} %pad_maximum_fusion.21), channel_id=1, source_target_pairs={{0,8},{1,9},{2,10},{3,11},{4,12},{5,13},{6,14},{7,15},{8,0},{9,1},... | collective-permute-start | bytes 786440 | tf_op jit(solution)/shard_map/ppermute | solution.py:40
  629.4 9.7 %collective-permute-start.38 = (bf16[1,2,1,32,1024]{4,3,1,2,0:T(8,128)(2,1)S(1)}, bf16[1,2,1,32,1024]{4,3,1,2,0:T(8,128)(2,1)S(1)}, u32[]{:S(2)}, u32[]{:S(2)}) collective-permute-start(bf16[1,2,1,32,1024]{4,3,1,2,0:T(8,128)(2,1)S(1)} %fusion.223), channel_id=1, source_target_pairs={{0,16},{1,17},{2,18},{3,19},{4,20},{5,21},{6,22},{7,23},{8,24},{9,... | collective-permute-start | bytes 393224 | tf_op jit(solution)/shard_map/ppermute | solution.py:40
  642.8 48.8 %all-to-all-start = ((bf16[8,3,32,1024]{3,2,1,0:T(8,128)(2,1)}), bf16[8,3,32,1024]{3,2,1,0:T(8,128)(2,1)}, u32[]{:S(2)}, u32[]{:S(2)}) async-start(bf16[8,3,32,1024]{3,2,1,0:T(8,128)(2,1)} %bitcast.545), calls=%async_computation | async-start | bytes 3145728 | tf_op jit(solution)/shard_map/all_to_all | solution.py:634
  664.6 10.6 %collective-permute-start.81 = (f32[15,1024]{1,0:T(8,128)S(1)}, f32[15,1024]{1,0:T(8,128)S(1)}, u32[]{:S(2)}, u32[]{:S(2)}) collective-permute-start(f32[15,1024]{1,0:T(8,128)S(1)} %add.884), channel_id=1, source_target_pairs={{0,8},{1,9},{2,10},{3,11},{4,12},{5,13},{6,14},{7,15},{8,0},{9,1},... | collective-permute-start | bytes 184328 | tf_op jit(solution)/shard_map/ppermute | solution.py:40
  675.2 12.8 %collective-permute-start.82 = (f32[15,1024]{1,0:T(8,128)S(1)}, f32[15,1024]{1,0:T(8,128)S(1)}, u32[]{:S(2)}, u32[]{:S(2)}) collective-permute-start(f32[15,1024]{1,0:T(8,128)S(1)} %add.885), channel_id=1, source_target_pairs={{0,16},{1,17},{2,18},{3,19},{4,20},{5,21},{6,22},{7,23},{8,24},{9,... | collective-permute-start | bytes 184328 | tf_op jit(solution)/shard_map/ppermute | solution.py:40
  695.4 19.6 %collective-permute-start.42 = (bf16[256,256]{1,0:T(8,128)(2,1)S(1)}, bf16[256,256]{1,0:T(8,128)(2,1)S(1)}, u32[]{:S(2)}, u32[]{:S(2)}) collective-permute-start(bf16[256,256]{1,0:T(8,128)(2,1)S(1)} %get-tuple-element.333), channel_id=1, source_target_pairs={{0,1},{1,0},{2,3},{3,2},{4,5},{5,4},{6,7},{7,6},{8,9},{9,8},{10,11... | collective-permute-start | bytes 393224 | tf_op jit(solution)/shard_map/ppermute | solution.py:40
  696.8 19.9 %collective-permute-start.43 = (bf16[256,256]{1,0:T(8,128)(2,1)S(1)}, bf16[256,256]{1,0:T(8,128)(2,1)S(1)}, u32[]{:S(2)}, u32[]{:S(2)}) collective-permute-start(bf16[256,256]{1,0:T(8,128)(2,1)S(1)} %get-tuple-element.332), channel_id=1, source_target_pairs={{0,2},{1,3},{2,0},{3,1},{4,6},{5,7},{6,4},{7,5},{8,10},{9,11},{10,... | collective-permute-start | bytes 393224 | tf_op jit(solution)/shard_map/ppermute | solution.py:40
  697.4 20.5 %collective-permute-start.44 = (bf16[256,256]{1,0:T(8,128)(2,1)S(1)}, bf16[256,256]{1,0:T(8,128)(2,1)S(1)}, u32[]{:S(2)}, u32[]{:S(2)}) collective-permute-start(bf16[256,256]{1,0:T(8,128)(2,1)S(1)} %get-tuple-element.331), channel_id=1, source_target_pairs={{0,3},{1,2},{2,1},{3,0},{4,7},{5,6},{6,5},{7,4},{8,11},{9,10},{10,... | collective-permute-start | bytes 393224 | tf_op jit(solution)/shard_map/ppermute | solution.py:40
  699.8 21.4 %collective-permute-start.48 = (bf16[256,256]{1,0:T(8,128)(2,1)S(1)}, bf16[256,256]{1,0:T(8,128)(2,1)S(1)}, u32[]{:S(2)}, u32[]{:S(2)}) collective-permute-start(bf16[256,256]{1,0:T(8,128)(2,1)S(1)} %get-tuple-element.341), channel_id=1, source_target_pairs={{0,1},{1,0},{2,3},{3,2},{4,5},{5,4},{6,7},{7,6},{8,9},{9,8},{10,11... | collective-permute-start | bytes 393224 | tf_op jit(solution)/shard_map/ppermute | solution.py:40
  701.1 21.7 %collective-permute-start.49 = (bf16[256,256]{1,0:T(8,128)(2,1)S(1)}, bf16[256,256]{1,0:T(8,128)(2,1)S(1)}, u32[]{:S(2)}, u32[]{:S(2)}) collective-permute-start(bf16[256,256]{1,0:T(8,128)(2,1)S(1)} %get-tuple-element.340), channel_id=1, source_target_pairs={{0,2},{1,3},{2,0},{3,1},{4,6},{5,7},{6,4},{7,5},{8,10},{9,11},{10,... | collective-permute-start | bytes 393224 | tf_op jit(solution)/shard_map/ppermute | solution.py:40
  715.0 9.0 %collective-permute-start.50 = (bf16[256,256]{1,0:T(8,128)(2,1)S(1)}, bf16[256,256]{1,0:T(8,128)(2,1)S(1)}, u32[]{:S(2)}, u32[]{:S(2)}) collective-permute-start(bf16[256,256]{1,0:T(8,128)(2,1)S(1)} %get-tuple-element.339), channel_id=1, source_target_pairs={{0,3},{1,2},{2,1},{3,0},{4,7},{5,6},{6,5},{7,4},{8,11},{9,10},{10,... | collective-permute-start | bytes 393224 | tf_op jit(solution)/shard_map/ppermute | solution.py:40
  716.7 9.6 %collective-permute-start.54 = (bf16[256,256]{1,0:T(8,128)(2,1)S(1)}, bf16[256,256]{1,0:T(8,128)(2,1)S(1)}, u32[]{:S(2)}, u32[]{:S(2)}) collective-permute-start(bf16[256,256]{1,0:T(8,128)(2,1)S(1)} %get-tuple-element.349), channel_id=1, source_target_pairs={{0,1},{1,0},{2,3},{3,2},{4,5},{5,4},{6,7},{7,6},{8,9},{9,8},{10,11... | collective-permute-start | bytes 393224 | tf_op jit(solution)/shard_map/ppermute | solution.py:40
  717.9 9.9 %collective-permute-start.55 = (bf16[256,256]{1,0:T(8,128)(2,1)S(1)}, bf16[256,256]{1,0:T(8,128)(2,1)S(1)}, u32[]{:S(2)}, u32[]{:S(2)}) collective-permute-start(bf16[256,256]{1,0:T(8,128)(2,1)S(1)} %get-tuple-element.348), channel_id=1, source_target_pairs={{0,2},{1,3},{2,0},{3,1},{4,6},{5,7},{6,4},{7,5},{8,10},{9,11},{10,... | collective-permute-start | bytes 393224 | tf_op jit(solution)/shard_map/ppermute | solution.py:40
  722.8 8.5 %collective-permute-start.45 = (bf16[256,256]{1,0:T(8,128)(2,1)S(1)}, bf16[256,256]{1,0:T(8,128)(2,1)S(1)}, u32[]{:S(2)}, u32[]{:S(2)}) collective-permute-start(bf16[256,256]{1,0:T(8,128)(2,1)S(1)} %get-tuple-element.329), channel_id=1, source_target_pairs={{0,1},{1,0},{2,3},{3,2},{4,5},{5,4},{6,7},{7,6},{8,9},{9,8},{10,11... | collective-permute-start | bytes 393224 | tf_op jit(solution)/shard_map/ppermute | solution.py:40
  724.0 8.8 %collective-permute-start.46 = (bf16[256,256]{1,0:T(8,128)(2,1)S(1)}, bf16[256,256]{1,0:T(8,128)(2,1)S(1)}, u32[]{:S(2)}, u32[]{:S(2)}) collective-permute-start(bf16[256,256]{1,0:T(8,128)(2,1)S(1)} %get-tuple-element.328), channel_id=1, source_target_pairs={{0,2},{1,3},{2,0},{3,1},{4,6},{5,7},{6,4},{7,5},{8,10},{9,11},{10,... | collective-permute-start | bytes 393224 | tf_op jit(solution)/shard_map/ppermute | solution.py:40
  727.8 13.1 %collective-permute-start.51 = (bf16[256,256]{1,0:T(8,128)(2,1)}, bf16[256,256]{1,0:T(8,128)(2,1)S(1)}, u32[]{:S(2)}, u32[]{:S(2)}) collective-permute-start(bf16[256,256]{1,0:T(8,128)(2,1)} %get-tuple-element.337), channel_id=1, source_target_pairs={{0,1},{1,0},{2,3},{3,2},{4,5},{5,4},{6,7},{7,6},{8,9},{9,8},{10,11... | collective-permute-start | bytes 393224 | tf_op jit(solution)/shard_map/ppermute | solution.py:40
  729.1 13.3 %collective-permute-start.52 = (bf16[256,256]{1,0:T(8,128)(2,1)}, bf16[256,256]{1,0:T(8,128)(2,1)}, u32[]{:S(2)}, u32[]{:S(2)}) collective-permute-start(bf16[256,256]{1,0:T(8,128)(2,1)} %get-tuple-element.336), channel_id=1, source_target_pairs={{0,2},{1,3},{2,0},{3,1},{4,6},{5,7},{6,4},{7,5},{8,10},{9,11},{10,... | collective-permute-start | bytes 393224 | tf_op jit(solution)/shard_map/ppermute | solution.py:40
  731.3 12.2 %collective-permute-start.53 = (bf16[256,256]{1,0:T(8,128)(2,1)}, bf16[256,256]{1,0:T(8,128)(2,1)S(1)}, u32[]{:S(2)}, u32[]{:S(2)}) collective-permute-start(bf16[256,256]{1,0:T(8,128)(2,1)} %get-tuple-element.335), channel_id=1, source_target_pairs={{0,3},{1,2},{2,1},{3,0},{4,7},{5,6},{6,5},{7,4},{8,11},{9,10},{10,... | collective-permute-start | bytes 393224 | tf_op jit(solution)/shard_map/ppermute | solution.py:40
  732.9 18.2 %collective-permute-start.57 = (bf16[256,256]{1,0:T(8,128)(2,1)}, bf16[256,256]{1,0:T(8,128)(2,1)S(1)}, u32[]{:S(2)}, u32[]{:S(2)}) collective-permute-start(bf16[256,256]{1,0:T(8,128)(2,1)} %get-tuple-element.345), channel_id=1, source_target_pairs={{0,1},{1,0},{2,3},{3,2},{4,5},{5,4},{6,7},{7,6},{8,9},{9,8},{10,11... | collective-permute-start | bytes 393224 | tf_op jit(solution)/shard_map/ppermute | solution.py:40
  734.1 18.4 %collective-permute-start.58 = (bf16[256,256]{1,0:T(8,128)(2,1)}, bf16[256,256]{1,0:T(8,128)(2,1)S(1)}, u32[]{:S(2)}, u32[]{:S(2)}) collective-permute-start(bf16[256,256]{1,0:T(8,128)(2,1)} %get-tuple-element.344), channel_id=1, source_target_pairs={{0,2},{1,3},{2,0},{3,1},{4,6},{5,7},{6,4},{7,5},{8,10},{9,11},{10,... | collective-permute-start | bytes 393224 | tf_op jit(solution)/shard_map/ppermute | solution.py:40
  740.9 12.8 %collective-permute-start.59 = (bf16[256,256]{1,0:T(8,128)(2,1)}, bf16[256,256]{1,0:T(8,128)(2,1)}, u32[]{:S(2)}, u32[]{:S(2)}) collective-permute-start(bf16[256,256]{1,0:T(8,128)(2,1)} %get-tuple-element.343), channel_id=1, source_target_pairs={{0,3},{1,2},{2,1},{3,0},{4,7},{5,6},{6,5},{7,4},{8,11},{9,10},{10,... | collective-permute-start | bytes 393224 | tf_op jit(solution)/shard_map/ppermute | solution.py:40
  742.4 18.5 %collective-permute-start.60 = (bf16[256,256]{1,0:T(8,128)(2,1)}, bf16[256,256]{1,0:T(8,128)(2,1)}, u32[]{:S(2)}, u32[]{:S(2)}) collective-permute-start(bf16[256,256]{1,0:T(8,128)(2,1)} %get-tuple-element.309), channel_id=1, source_target_pairs={{0,1},{1,0},{2,3},{3,2},{4,5},{5,4},{6,7},{7,6},{8,9},{9,8},{10,11... | collective-permute-start | bytes 393224 | tf_op jit(solution)/shard_map/ppermute | solution.py:40
  743.5 18.9 %collective-permute-start.61 = (bf16[256,256]{1,0:T(8,128)(2,1)}, bf16[256,256]{1,0:T(8,128)(2,1)}, u32[]{:S(2)}, u32[]{:S(2)}) collective-permute-start(bf16[256,256]{1,0:T(8,128)(2,1)} %get-tuple-element.308), channel_id=1, source_target_pairs={{0,2},{1,3},{2,0},{3,1},{4,6},{5,7},{6,4},{7,5},{8,10},{9,11},{10,... | collective-permute-start | bytes 393224 | tf_op jit(solution)/shard_map/ppermute | solution.py:40
  751.1 12.4 %collective-permute-start.62 = (bf16[256,256]{1,0:T(8,128)(2,1)}, bf16[256,256]{1,0:T(8,128)(2,1)}, u32[]{:S(2)}, u32[]{:S(2)}) collective-permute-start(bf16[256,256]{1,0:T(8,128)(2,1)} %get-tuple-element.307), channel_id=1, source_target_pairs={{0,3},{1,2},{2,1},{3,0},{4,7},{5,6},{6,5},{7,4},{8,11},{9,10},{10,... | collective-permute-start | bytes 393224 | tf_op jit(solution)/shard_map/ppermute | solution.py:40
  752.6 14.3 %collective-permute-start.66 = (bf16[256,256]{1,0:T(8,128)(2,1)}, bf16[256,256]{1,0:T(8,128)(2,1)}, u32[]{:S(2)}, u32[]{:S(2)}) collective-permute-start(bf16[256,256]{1,0:T(8,128)(2,1)} %get-tuple-element.317), channel_id=1, source_target_pairs={{0,1},{1,0},{2,3},{3,2},{4,5},{5,4},{6,7},{7,6},{8,9},{9,8},{10,11... | collective-permute-start | bytes 393224 | tf_op jit(solution)/shard_map/ppermute | solution.py:40
  753.7 14.8 %collective-permute-start.67 = (bf16[256,256]{1,0:T(8,128)(2,1)}, bf16[256,256]{1,0:T(8,128)(2,1)}, u32[]{:S(2)}, u32[]{:S(2)}) collective-permute-start(bf16[256,256]{1,0:T(8,128)(2,1)} %get-tuple-element.316), channel_id=1, source_target_pairs={{0,2},{1,3},{2,0},{3,1},{4,6},{5,7},{6,4},{7,5},{8,10},{9,11},{10,... | collective-permute-start | bytes 393224 | tf_op jit(solution)/shard_map/ppermute | solution.py:40
  760.9 8.7 %collective-permute-start.68 = (bf16[256,256]{1,0:T(8,128)(2,1)S(1)}, bf16[256,256]{1,0:T(8,128)(2,1)S(1)}, u32[]{:S(2)}, u32[]{:S(2)}) collective-permute-start(bf16[256,256]{1,0:T(8,128)(2,1)S(1)} %copy-done.100), channel_id=1, source_target_pairs={{0,3},{1,2},{2,1},{3,0},{4,7},{5,6},{6,5},{7,4},{8,11},{9,10},{10,... | collective-permute-start | bytes 393224 | tf_op jit(solution)/shard_map/ppermute | solution.py:40
  762.4 9.9 %collective-permute-start.72 = (bf16[256,256]{1,0:T(8,128)(2,1)S(1)}, bf16[256,256]{1,0:T(8,128)(2,1)S(1)}, u32[]{:S(2)}, u32[]{:S(2)}) collective-permute-start(bf16[256,256]{1,0:T(8,128)(2,1)S(1)} %get-tuple-element.325), channel_id=1, source_target_pairs={{0,1},{1,0},{2,3},{3,2},{4,5},{5,4},{6,7},{7,6},{8,9},{9,8},{10,11... | collective-permute-start | bytes 393224 | tf_op jit(solution)/shard_map/ppermute | solution.py:40
  763.5 10.3 %collective-permute-start.73 = (bf16[256,256]{1,0:T(8,128)(2,1)S(1)}, bf16[256,256]{1,0:T(8,128)(2,1)S(1)}, u32[]{:S(2)}, u32[]{:S(2)}) collective-permute-start(bf16[256,256]{1,0:T(8,128)(2,1)S(1)} %get-tuple-element.324), channel_id=1, source_target_pairs={{0,2},{1,3},{2,0},{3,1},{4,6},{5,7},{6,4},{7,5},{8,10},{9,11},{10,... | collective-permute-start | bytes 393224 | tf_op jit(solution)/shard_map/ppermute | solution.py:40
  766.9 8.0 collective-permute-start.74
  768.4 8.3 %collective-permute-start.63 = (bf16[256,256]{0,1:T(8,128)(2,1)S(1)}, bf16[256,256]{0,1:T(8,128)(2,1)S(1)}, u32[]{:S(2)}, u32[]{:S(2)}) collective-permute-start(bf16[256,256]{0,1:T(8,128)(2,1)S(1)} %get-tuple-element.305), channel_id=1, source_target_pairs={{0,1},{1,0},{2,3},{3,2},{4,5},{5,4},{6,7},{7,6},{8,9},{9,8},{10,11... | collective-permute-start | bytes 393224 | tf_op jit(solution)/shard_map/ppermute | solution.py:40
  769.6 8.7 %collective-permute-start.64 = (bf16[256,256]{0,1:T(8,128)(2,1)S(1)}, bf16[256,256]{0,1:T(8,128)(2,1)S(1)}, u32[]{:S(2)}, u32[]{:S(2)}) collective-permute-start(bf16[256,256]{0,1:T(8,128)(2,1)S(1)} %get-tuple-element.304), channel_id=1, source_target_pairs={{0,2},{1,3},{2,0},{3,1},{4,6},{5,7},{6,4},{7,5},{8,10},{9,11},{10,... | collective-permute-start | bytes 393224 | tf_op jit(solution)/shard_map/ppermute | solution.py:40
  773.8 9.3 %collective-permute-start.69 = (bf16[256,256]{0,1:T(8,128)(2,1)S(1)}, bf16[256,256]{0,1:T(8,128)(2,1)S(1)}, u32[]{:S(2)}, u32[]{:S(2)}) collective-permute-start(bf16[256,256]{0,1:T(8,128)(2,1)S(1)} %get-tuple-element.313), channel_id=1, source_target_pairs={{0,1},{1,0},{2,3},{3,2},{4,5},{5,4},{6,7},{7,6},{8,9},{9,8},{10,11... | collective-permute-start | bytes 393224 | tf_op jit(solution)/shard_map/ppermute | solution.py:40
  774.9 9.7 %collective-permute-start.70 = (bf16[256,256]{0,1:T(8,128)(2,1)S(1)}, bf16[256,256]{0,1:T(8,128)(2,1)S(1)}, u32[]{:S(2)}, u32[]{:S(2)}) collective-permute-start(bf16[256,256]{0,1:T(8,128)(2,1)S(1)} %get-tuple-element.312), channel_id=1, source_target_pairs={{0,2},{1,3},{2,0},{3,1},{4,6},{5,7},{6,4},{7,5},{8,10},{9,11},{10,... | collective-permute-start | bytes 393224 | tf_op jit(solution)/shard_map/ppermute | solution.py:40
  778.3 8.7 %collective-permute-start.75 = (bf16[256,256]{0,1:T(8,128)(2,1)S(1)}, bf16[256,256]{0,1:T(8,128)(2,1)S(1)}, u32[]{:S(2)}, u32[]{:S(2)}) collective-permute-start(bf16[256,256]{0,1:T(8,128)(2,1)S(1)} %get-tuple-element.321), channel_id=1, source_target_pairs={{0,1},{1,0},{2,3},{3,2},{4,5},{5,4},{6,7},{7,6},{8,9},{9,8},{10,11... | collective-permute-start | bytes 393224 | tf_op jit(solution)/shard_map/ppermute | solution.py:40
  (201 other events, 2220.1 us)
Sparse Core Ops, SparseCore 0:
  11.9 55.3 all-gather.4
  69.8 80.9 all-gather.6
  164.9 87.9 all-gather.8
  307.9 86.5 reduce-scatter.12
  419.3 43.3 reduce-scatter.14
  465.9 86.4 reduce-scatter.16
  557.1 51.5 reduce-scatter.18
  611.3 71.5 all-gather.10

commit v5 on v4

--- a/solution.py
+++ b/solution.py
@@ -210,19 +210,24 @@
     size = D // n_shards
 
     def kernel(starts_ref, square_ref, out_ref):
-        for place in range(n_shards):
-            at = pl.multiple_of(starts_ref[place] * size, size)
-            out_ref[0, :, place * size : (place + 1) * size] = square_ref[0, :, pl.ds(at, size)]
+        for row in range(n_shards):
+            rows = pl.ds(pl.multiple_of(starts_ref[row] * size, size), size)
+            for column in range(n_shards):
+                at = pl.multiple_of(starts_ref[column] * size, size)
+                out_ref[0, row * size : (row + 1) * size, column * size : (column + 1) * size] = (
+                    square_ref[0, rows, pl.ds(at, size)]
+                )
 
     return pl.pallas_call(
         kernel,
         grid_spec=pltpu.PrefetchScalarGridSpec(
             num_scalar_prefetch=1,
-            grid=(count, n_shards),
-            in_specs=[pl.BlockSpec((1, size, D), lambda b, i, s: (b, s[i], 0))],
-            out_specs=pl.BlockSpec((1, size, D), lambda b, i, s: (b, i, 0)),
+            grid=(count,),
+            in_specs=[pl.BlockSpec((1, D, D), lambda b, s: (b, 0, 0))],
+            out_specs=pl.BlockSpec((1, D, D), lambda b, s: (b, 0, 0)),
         ),
         out_shape=jax.ShapeDtypeStruct(square.shape, square.dtype),
+        compiler_params=pltpu.CompilerParams(vmem_limit_bytes=32 << 20),
         cost_estimate=pl.CostEstimate(
             flops=0, bytes_accessed=count * 4 * D * D, transcendentals=0
         ),
@@ -660,7 +665,8 @@
         update = mm_t(mixed, rights[slot])
         master = pick(blocks, 0, my_blocks[slot])
         weight_list.append(master - LEARN_RATE * (update + DECAY_WEIGHT * master))
-    rotated = jnp.stack([regroup(near, turned) for turned in turned_list]).astype(F32)
+    rotated = regroup(near, jnp.concatenate(turned_list, axis=0)).astype(F32)
+    rotated = rotated.reshape(capacity, rows_own, D)
     first_step = BETA_DECAY * block_first + (1.0 - BETA_DECAY) * rotated
     second_step = BETA_DECAY * block_second + (1.0 - BETA_DECAY) * rotated * rotated
     small_first_new = BETA_DECAY * small_first + (1.0 - BETA_DECAY) * small_grads

time: 812 us -> 806 us (level)
  Pallas kernels: 60.6 us -> 48 us
    pallas_call x1, Pallas kernels: 10.3 us -> 1.41 us  [turn(): pl.pallas_call(kernel, grid_spec=pltpu.PrefetchScalarGridSpec(num_scalar_...]
    pallas_call x12 -> x10, Pallas kernels: 38.5 us -> 34.5 us  [regroup(): pl.pallas_call(kernel, grid_spec=pltpu.PrefetchScalarGridSpec(num_scalar_...]
    unnamed x350 -> x348, local copies, waits for them, and re-layouts: 36.9 us -> 39.7 us
  transfers between devices with their start and end apart: 92 -> 92, of which waited for: 42 -> 49; matrix products, arithmetic and copies ran while one was open for 34% -> 34% of each run, Pallas kernels for 8% -> 6%
where the time goes in v5:
time: 806 us; the launch traced here: 798 us
  waiting for transfers between devices  246 us (31%)
  matrix products  173 us (21%)
  other arithmetic  117 us (15%)
  starting transfers between devices  98.5 us (12%)
  local copies, waits for them, and re-layouts  87.5 us (11%)
  Pallas kernels  48 us (6%)
  between operations  28.6 us (4%)
    ppermute x83, waiting for transfers between devices, swap(): return lax.ppermute(value, AXES, pairs)  201 us
    ppermute x83, starting transfers between devices, swap(): return lax.ppermute(value, AXES, pairs)  92.6 us
    dot_general x18, matrix products, mm_t(): lax.dot_general(left, right, (((1,), (1,)), ((), ())), preferred_element_...  62.8 us
    dot_general x21, matrix products, mm(): return jnp.dot(left, right, preferred_element_type=F32)  53.2 us
    unnamed x348, local copies, waits for them, and re-layouts  39.7 us
    dot_general x18, matrix products, t_mm(): lax.dot_general(left, right, (((0,), (0,)), ((), ())), preferred_element_...  39 us
    pallas_call x10, Pallas kernels, regroup(): pl.pallas_call(kernel, grid_spec=pltpu.PrefetchScalarGridSpec(num_scalar_...  34.5 us
    all_gather x1, waiting for transfers between devices, fetch_own(): fetched = lax.all_gather(own, 'fsdp', axis=1, tiled=True)  26.5 us
  transfers between devices with their start and end apart: 92, of which 49 were waited for; matrix products, arithmetic and copies ran while one was open for 34% of the time, Pallas kernels for 6%

profile of v5, /device:TPU:0, one launch (start us, length us, event | category | flops | bytes accessed | tf_op | source)
XLA Modules:
  0.0 798.4 jit_solution(18099326210320591929)
XLA Ops:
  7.2 3.5 dynamic-slice_convert_fusion.4
  11.9 3.6 dynamic-slice_convert_fusion
  15.5 5.6 convert.24
  24.6 3.8 regroup.10
  28.4 3.9 regroup.11
  32.3 4.1 regroup.12
  41.1 3.9 regroup.14
  52.7 3.2 regroup.17
  76.9 32.8 %collective-permute-done.1.arrived_ref = bf16[2,3,128,1024]{3,2,1,0:T(8,128)(2,1)} collective-permute-done((bf16[2,3,128,1024]{3,2,1,0:T(8,128)(2,1)S(1)}, bf16[2,3,128,1024]{3,2,1,0:T(8,128)(2,1)}, u32[]{:S(2)}, u32[]{:S(2)}) %collective-permute-start.1) | collective-permute-done | bytes 1572896 | tf_op jit(solution)/shard_map/ppermute | solution.py:40
  109.7 4.4 interleave.2
  114.1 28.2 %collective-permute-done.2.arrived_ref = bf16[2,3,128,1024]{3,2,1,0:T(8,128)(2,1)} collective-permute-done((bf16[2,3,128,1024]{3,2,1,0:T(8,128)(2,1)}, bf16[2,3,128,1024]{3,2,1,0:T(8,128)(2,1)}, u32[]{:S(2)}, u32[]{:S(2)}) %collective-permute-start.2) | collective-permute-done | bytes 1572896 | tf_op jit(solution)/shard_map/ppermute | solution.py:40
  142.2 4.7 interleave.3
  147.0 4.4 convolution_convert_fusion.18
  151.5 4.4 convolution_convert_fusion.17
  174.1 3.4 fusion.94
  178.2 4.2 multiply_convert_fusion.7
  184.0 3.2 fusion.100
  226.9 26.5 %all-gather.9.cloned.1.call-done = bf16[4,1024,1024]{2,1,0:T(8,128)(2,1)} async-done(((bf16[4,256,1024]{2,1,0:T(8,128)(2,1)}), bf16[4,1024,1024]{2,1,0:T(8,128)(2,1)}) %all-gather.9.cloned.1.call-update) | async-done | bytes 8388624 | tf_op jit(solution)/shard_map/all_gather | solution.py:419
  253.4 4.4 convolution_convert_fusion.15
  257.8 4.4 convolution_convert_fusion.16
  285.1 3.4 fusion.27
  288.6 3.6 fusion.35
  297.2 3.6 convolution_convert_fusion.14
  300.8 3.6 convolution_convert_fusion.13
  304.3 3.9 pad_maximum_fusion
  308.6 4.7 fusion.82
  313.3 4.0 convolution_add_fusion.1
  317.7 4.0 collective-permute-done.12
  327.3 5.9 fusion.274
  343.7 3.3 convolution_convert_fusion.8
  367.4 3.1 fusion.76
  370.5 4.1 multiply_reduce_fusion.3
  378.1 4.0 fusion.93
  384.5 6.8 multiply_reduce_fusion
  398.2 3.2 fusion.97
  401.4 3.9 add_convert_fusion.1
  405.4 3.2 fusion.72
  411.7 3.4 fusion.272
  421.6 5.5 fusion.11
  427.1 4.4 convolution_convert_fusion.7
  431.5 3.5 fusion.19
  435.1 4.4 convolution_convert_fusion.6
  444.4 4.0 pad_maximum_fusion.1
  448.4 14.3 %reduce-scatter.15.cloned.1.call-done = bf16[1,3,128,1024]{3,2,1,0:T(8,128)(2,1)} async-done(((bf16[4,3,128,1024]{3,2,1,0:T(8,128)(2,1)}), bf16[1,3,128,1024]{3,2,1,0:T(8,128)(2,1)}) %reduce-scatter.15.cloned.1.call-update) | async-done | bytes 786448
  490.9 18.4 %collective-permute-done.30 = bf16[2,2,2,32,1024]{4,3,2,1,0:T(8,128)(2,1)} collective-permute-done((bf16[2,2,2,32,1024]{4,3,2,1,0:T(8,128)(2,1)}, bf16[2,2,2,32,1024]{4,3,2,1,0:T(8,128)(2,1)}, u32[]{:S(2)}, u32[]{:S(2)}) %collective-permute-start.30) | collective-permute-done | bytes 524320 | tf_op jit(solution)/shard_map/ppermute | solution.py:40
  514.7 3.6 collective-permute-start.28
  518.3 3.3 collective-permute-done.31
  523.4 6.7 collective-permute-done.28
  536.5 4.9 add_convert_fusion
  549.3 5.9 collective-permute-done.34
  564.3 20.3 %collective-permute-done.22 = bf16[2,2,2,32,1024]{4,3,2,1,0:T(8,128)(2,1)S(1)} collective-permute-done((bf16[2,2,2,32,1024]{4,3,2,1,0:T(8,128)(2,1)S(1)}, bf16[2,2,2,32,1024]{4,3,2,1,0:T(8,128)(2,1)S(1)}, u32[]{:S(2)}, u32[]{:S(2)}) %collective-permute-start.22) | collective-permute-done | bytes 524320 | tf_op jit(solution)/shard_map/ppermute | solution.py:40
  592.2 4.0 collective-permute-done.23
  596.9 8.3 %collective-permute-done.21 = bf16[1,2,2,32,1024]{4,3,2,1,0:T(8,128)(2,1)S(1)} collective-permute-done((bf16[1,2,2,32,1024]{4,3,2,1,0:T(8,128)(2,1)S(1)}, bf16[1,2,2,32,1024]{4,3,2,1,0:T(8,128)(2,1)S(1)}, u32[]{:S(2)}, u32[]{:S(2)}) %collective-permute-start.21) | collective-permute-done | bytes 262176 | tf_op jit(solution)/shard_map/ppermute | solution.py:40
  620.0 8.7 %collective-permute-done.39 = bf16[2,2,1,32,1024]{4,3,1,2,0:T(8,128)(2,1)S(1)} collective-permute-done((bf16[2,2,1,32,1024]{4,3,1,2,0:T(8,128)(2,1)S(1)}, bf16[2,2,1,32,1024]{4,3,1,2,0:T(8,128)(2,1)S(1)}, u32[]{:S(2)}, u32[]{:S(2)}) %collective-permute-start.39) | collective-permute-done | bytes 262176 | tf_op jit(solution)/shard_map/ppermute | solution.py:40
  629.3 3.4 collective-permute-start.38
  632.7 3.3 collective-permute-done.40
  642.7 4.9 all-to-all-start
  652.5 4.9 collective-permute-done.78
  658.7 4.6 collective-permute-done.79
  675.3 4.5 collective-permute-start.82
  681.9 6.2 collective-permute-done.82
  739.8 10.6 %maximum_maximum_fusion.value_ref = bf16[768,1024]{1,0:T(8,128)(2,1)} fusion(bf16[256,256]{1,0:T(8,128)(2,1)S(1)} %collective-permute-done.59, bf16[256,256]{1,0:T(8,128)(2,1)S(1)} %collective-permute-done.58, bf16[256,256]{1,0:T(8,128)(2,1)S(1)} %collective-permute-done.57, bf16[256,256]{1,0:T(8,128)(2,1)S(1)} %get-tuple-element.342, ...), kind=kLoop, calls=%fused_computation.239 | loop fusion | flops 18874368 | bytes 3145728 | tf_op jit(solution)/shard_map/concatenate | solution.py:668
  750.5 3.7 regroup.19
  786.8 4.4 fusion.42
  (747 shorter events, 370.6 us)
Async XLA Ops:
  7.2 60.2 %all-gather.5.cloned.1.call-start = ((), (), s32[]{:S(2)}) async-start(), calls=%async_computation.5 | async-start | bytes 5242880 | tf_op jit(solution)/shard_map/all_gather | solution.py:429
  11.8 162.3 %all-gather.7.cloned.1.call-start = ((), (), s32[]{:S(2)}) async-start(), calls=%async_computation.6 | async-start | bytes 16515072 | tf_op jit(solution)/shard_map/all_gather | solution.py:442
  15.5 237.9 %all-gather.9.cloned.1.call-start = ((), (), s32[]{:S(2)}) async-start(), calls=%async_computation.7 | async-start | bytes 10485760 | tf_op jit(solution)/shard_map/all_gather | solution.py:419
  72.2 37.5 %collective-permute-start.1 = (bf16[2,3,128,1024]{3,2,1,0:T(8,128)(2,1)S(1)}, bf16[2,3,128,1024]{3,2,1,0:T(8,128)(2,1)}, u32[]{:S(2)}, u32[]{:S(2)}) collective-permute-start(bf16[2,3,128,1024]{3,2,1,0:T(8,128)(2,1)S(1)} %pad_maximum_fusion.9), channel_id=1, source_target_pairs={{0,8},{1,9},{2,10},{3,11},{4,12},{5,13},{6,14},{7,15},{8,0},{9,1},... | collective-permute-start | bytes 4718600 | tf_op jit(solution)/shard_map/ppermute | solution.py:40
  75.1 67.1 %collective-permute-start.2 = (bf16[2,3,128,1024]{3,2,1,0:T(8,128)(2,1)}, bf16[2,3,128,1024]{3,2,1,0:T(8,128)(2,1)}, u32[]{:S(2)}, u32[]{:S(2)}) collective-permute-start(bf16[2,3,128,1024]{3,2,1,0:T(8,128)(2,1)} %pad_maximum_fusion.10), channel_id=1, source_target_pairs={{0,8},{1,9},{2,10},{3,11},{4,12},{5,13},{6,14},{7,15},{8,0},{9,1},... | collective-permute-start | bytes 4718600 | tf_op jit(solution)/shard_map/ppermute | solution.py:40
  76.1 70.9 %collective-permute-start = (bf16[512,1024]{0,1:T(8,128)(2,1)S(1)}, bf16[512,1024]{0,1:T(8,128)(2,1)}, u32[]{:S(2)}, u32[]{:S(2)}) collective-permute-start(bf16[512,1024]{0,1:T(8,128)(2,1)S(1)} %add_convert_fusion.6), channel_id=1, source_target_pairs={{0,4},{1,5},{2,6},{3,7},{4,0},{5,1},{6,2},{7,3},{8,12},{9,13},{10,... | collective-permute-start | bytes 3145736 | tf_op jit(solution)/shard_map/ppermute | solution.py:40
  165.1 240.3 %reduce-scatter.13.cloned.1.call-start = ((), (), s32[]{:S(2)}) async-start(), calls=%async_computation.9 | async-start | bytes 10485760
  226.8 26.5 %collective-permute-start.9 = (bf16[512,1024]{0,1:T(8,128)(2,1)S(1)}, bf16[512,1024]{0,1:T(8,128)(2,1)}, u32[]{:S(2)}, u32[]{:S(2)}) collective-permute-start(bf16[512,1024]{0,1:T(8,128)(2,1)S(1)} %add_convert_fusion.3), channel_id=1, source_target_pairs={{0,4},{1,5},{2,6},{3,7},{4,0},{5,1},{6,2},{7,3},{8,12},{9,13},{10,... | collective-permute-start | bytes 3145736 | tf_op jit(solution)/shard_map/ppermute | solution.py:40
  308.3 154.5 %reduce-scatter.15.cloned.1.call-start = ((), (), s32[]{:S(2)}) async-start(), calls=%async_computation.10 | async-start | bytes 3932160
  367.3 34.2 %collective-permute-start.18 = (bf16[4,3,128,1024]{3,2,1,0:T(8,128)(2,1)}, bf16[4,3,128,1024]{3,2,1,0:T(8,128)(2,1)}, u32[]{:S(2)}, u32[]{:S(2)}) collective-permute-start(bf16[4,3,128,1024]{3,2,1,0:T(8,128)(2,1)} %pad_maximum_fusion.3), channel_id=1, source_target_pairs={{0,4},{1,5},{2,6},{3,7},{4,0},{5,1},{6,2},{7,3},{8,12},{9,13},{10,... | collective-permute-start | bytes 9437192 | tf_op jit(solution)/shard_map/ppermute | solution.py:40
  419.0 137.9 %reduce-scatter.17.cloned.1.call-start = ((), (), s32[]{:S(2)}) async-start(), calls=%async_computation.11 | async-start | bytes 10485760
  462.8 145.9 %reduce-scatter.19.cloned.1.call-start = ((), (), s32[]{:S(2)}) async-start(), calls=%async_computation.12 | async-start | bytes 5242880
  475.8 60.8 %collective-permute-start.26 = (bf16[4,4,128,1024]{3,2,1,0:T(8,128)(2,1)}, bf16[4,4,128,1024]{3,2,1,0:T(8,128)(2,1)}, u32[]{:S(2)}, u32[]{:S(2)}) collective-permute-start(bf16[4,4,128,1024]{3,2,1,0:T(8,128)(2,1)} %pad_maximum_fusion.2), channel_id=1, source_target_pairs={{0,4},{1,5},{2,6},{3,7},{4,0},{5,1},{6,2},{7,3},{8,12},{9,13},{10,... | collective-permute-start | bytes 12582920 | tf_op jit(solution)/shard_map/ppermute | solution.py:40
  482.3 27.0 %collective-permute-start.30 = (bf16[2,2,2,32,1024]{4,3,2,1,0:T(8,128)(2,1)}, bf16[2,2,2,32,1024]{4,3,2,1,0:T(8,128)(2,1)}, u32[]{:S(2)}, u32[]{:S(2)}) collective-permute-start(bf16[2,2,2,32,1024]{4,3,2,1,0:T(8,128)(2,1)} %pad_maximum_fusion.15), channel_id=1, source_target_pairs={{0,16},{1,17},{2,18},{3,19},{4,20},{5,21},{6,22},{7,23},{8,24},{9,... | collective-permute-start | bytes 1572872 | tf_op jit(solution)/shard_map/ppermute | solution.py:40
  488.8 24.7 %collective-permute-start.27 = (bf16[2,2,2,32,1024]{4,3,2,1,0:T(8,128)(2,1)}, bf16[2,2,2,32,1024]{4,3,2,1,0:T(8,128)(2,1)}, u32[]{:S(2)}, u32[]{:S(2)}) collective-permute-start(bf16[2,2,2,32,1024]{4,3,2,1,0:T(8,128)(2,1)} %pad_maximum_fusion.14), channel_id=1, source_target_pairs={{0,8},{1,9},{2,10},{3,11},{4,12},{5,13},{6,14},{7,15},{8,0},{9,1},... | collective-permute-start | bytes 1572872 | tf_op jit(solution)/shard_map/ppermute | solution.py:40
  511.2 10.4 %collective-permute-start.31 = (bf16[1,2,2,32,1024]{4,3,2,1,0:T(8,128)(2,1)}, bf16[1,2,2,32,1024]{4,3,2,1,0:T(8,128)(2,1)S(1)}, u32[]{:S(2)}, u32[]{:S(2)}) collective-permute-start(bf16[1,2,2,32,1024]{4,3,2,1,0:T(8,128)(2,1)} %fusion.211), channel_id=1, source_target_pairs={{0,8},{1,9},{2,10},{3,11},{4,12},{5,13},{6,14},{7,15},{8,0},{9,1},... | collective-permute-start | bytes 786440 | tf_op jit(solution)/shard_map/ppermute | solution.py:40
  514.7 15.5 %collective-permute-start.28 = (bf16[1,2,2,32,1024]{4,3,2,1,0:T(8,128)(2,1)S(1)}, bf16[1,2,2,32,1024]{4,3,2,1,0:T(8,128)(2,1)S(1)}, u32[]{:S(2)}, u32[]{:S(2)}) collective-permute-start(bf16[1,2,2,32,1024]{4,3,2,1,0:T(8,128)(2,1)S(1)} %fusion.213), channel_id=1, source_target_pairs={{0,16},{1,17},{2,18},{3,19},{4,20},{5,21},{6,22},{7,23},{8,24},{9,... | collective-permute-start | bytes 786440 | tf_op jit(solution)/shard_map/ppermute | solution.py:40
  523.4 33.5 %collective-permute-start.32 = (bf16[2,32,1024]{2,1,0:T(8,128)(2,1)}, bf16[2,32,1024]{2,1,0:T(8,128)(2,1)S(1)}, u32[]{:S(2)}, u32[]{:S(2)}) collective-permute-start(bf16[2,32,1024]{2,1,0:T(8,128)(2,1)} %get-tuple-element.358), channel_id=1, source_target_pairs={{0,4},{1,5},{2,6},{3,7},{4,0},{5,1},{6,2},{7,3},{8,12},{9,13},{10,... | collective-permute-start | bytes 393224 | tf_op jit(solution)/shard_map/ppermute | solution.py:40
  532.0 24.9 %collective-permute-start.29 = (bf16[2,32,1024]{2,1,0:T(8,128)(2,1)}, bf16[2,32,1024]{2,1,0:T(8,128)(2,1)}, u32[]{:S(2)}, u32[]{:S(2)}) collective-permute-start(bf16[2,32,1024]{2,1,0:T(8,128)(2,1)} %get-tuple-element.360), channel_id=1, source_target_pairs={{0,4},{1,5},{2,6},{3,7},{4,0},{5,1},{6,2},{7,3},{8,12},{9,13},{10,... | collective-permute-start | bytes 393224 | tf_op jit(solution)/shard_map/ppermute | solution.py:40
  532.9 9.7 %collective-permute-start.35 = (bf16[2,1,1,32,1024]{4,3,2,1,0:T(8,128)(2,1)}, bf16[2,1,1,32,1024]{4,3,2,1,0:T(8,128)(2,1)}, u32[]{:S(2)}, u32[]{:S(2)}) collective-permute-start(bf16[2,1,1,32,1024]{4,3,2,1,0:T(8,128)(2,1)} %pad_maximum_fusion.19), channel_id=1, source_target_pairs={{0,16},{1,17},{2,18},{3,19},{4,20},{5,21},{6,22},{7,23},{8,24},{9,... | collective-permute-start | bytes 393224 | tf_op jit(solution)/shard_map/ppermute | solution.py:40
  533.8 12.5 %collective-permute-start.33 = (bf16[2,2,1,32,1024]{4,3,1,2,0:T(8,128)(2,1)}, bf16[2,2,1,32,1024]{4,3,1,2,0:T(8,128)(2,1)}, u32[]{:S(2)}, u32[]{:S(2)}) collective-permute-start(bf16[2,2,1,32,1024]{4,3,1,2,0:T(8,128)(2,1)} %pad_maximum_fusion.16), channel_id=1, source_target_pairs={{0,8},{1,9},{2,10},{3,11},{4,12},{5,13},{6,14},{7,15},{8,0},{9,1},... | collective-permute-start | bytes 786440 | tf_op jit(solution)/shard_map/ppermute | solution.py:40
  557.5 147.3 %all-gather.11.cloned.1.call-start = ((), (), s32[]{:S(2)}) async-start(), calls=%async_computation.8 | async-start | bytes 7864320 | tf_op jit(solution)/shard_map/all_gather | solution.py:611
  558.9 25.7 %collective-permute-start.22 = (bf16[2,2,2,32,1024]{4,3,2,1,0:T(8,128)(2,1)S(1)}, bf16[2,2,2,32,1024]{4,3,2,1,0:T(8,128)(2,1)S(1)}, u32[]{:S(2)}, u32[]{:S(2)}) collective-permute-start(bf16[2,2,2,32,1024]{4,3,2,1,0:T(8,128)(2,1)S(1)} %pad_maximum_fusion.13), channel_id=1, source_target_pairs={{0,16},{1,17},{2,18},{3,19},{4,20},{5,21},{6,22},{7,23},{8,24},{9,... | collective-permute-start | bytes 1572872 | tf_op jit(solution)/shard_map/ppermute | solution.py:40
  564.0 26.0 %collective-permute-start.20 = (bf16[2,2,2,32,1024]{4,3,2,1,0:T(8,128)(2,1)S(1)}, bf16[2,2,2,32,1024]{4,3,2,1,0:T(8,128)(2,1)S(1)}, u32[]{:S(2)}, u32[]{:S(2)}) collective-permute-start(bf16[2,2,2,32,1024]{4,3,2,1,0:T(8,128)(2,1)S(1)} %pad_maximum_fusion.12), channel_id=1, source_target_pairs={{0,8},{1,9},{2,10},{3,11},{4,12},{5,13},{6,14},{7,15},{8,0},{9,1},... | collective-permute-start | bytes 1572872 | tf_op jit(solution)/shard_map/ppermute | solution.py:40
  584.6 11.5 %collective-permute-start.23 = (bf16[1,2,2,32,1024]{4,3,2,1,0:T(8,128)(2,1)S(1)}, bf16[1,2,2,32,1024]{4,3,2,1,0:T(8,128)(2,1)S(1)}, u32[]{:S(2)}, u32[]{:S(2)}) collective-permute-start(bf16[1,2,2,32,1024]{4,3,2,1,0:T(8,128)(2,1)S(1)} %fusion.215), channel_id=1, source_target_pairs={{0,8},{1,9},{2,10},{3,11},{4,12},{5,13},{6,14},{7,15},{8,0},{9,1},... | collective-permute-start | bytes 786440 | tf_op jit(solution)/shard_map/ppermute | solution.py:40
  589.8 19.9 %collective-permute-start.41 = (f32[512,1024]{0,1:T(8,128)}, f32[512,1024]{0,1:T(8,128)}, u32[]{:S(2)}, u32[]{:S(2)}) collective-permute-start(f32[512,1024]{0,1:T(8,128)} %slice.629), channel_id=1, source_target_pairs={{0,4},{1,5},{2,6},{3,7},{4,0},{5,1},{6,2},{7,3},{8,12},{9,13},{10,... | collective-permute-start | bytes 6291464 | tf_op jit(solution)/shard_map/ppermute | solution.py:40
  590.0 15.2 %collective-permute-start.21 = (bf16[1,2,2,32,1024]{4,3,2,1,0:T(8,128)(2,1)S(1)}, bf16[1,2,2,32,1024]{4,3,2,1,0:T(8,128)(2,1)S(1)}, u32[]{:S(2)}, u32[]{:S(2)}) collective-permute-start(bf16[1,2,2,32,1024]{4,3,2,1,0:T(8,128)(2,1)S(1)} %fusion.217), channel_id=1, source_target_pairs={{0,16},{1,17},{2,18},{3,19},{4,20},{5,21},{6,22},{7,23},{8,24},{9,... | collective-permute-start | bytes 786440 | tf_op jit(solution)/shard_map/ppermute | solution.py:40
  596.9 11.8 %collective-permute-start.25 = (bf16[2,32,1024]{2,1,0:T(8,128)(2,1)S(1)}, bf16[2,32,1024]{2,1,0:T(8,128)(2,1)S(1)}, u32[]{:S(2)}, u32[]{:S(2)}) collective-permute-start(bf16[2,32,1024]{2,1,0:T(8,128)(2,1)S(1)} %get-tuple-element.362), channel_id=1, source_target_pairs={{0,4},{1,5},{2,6},{3,7},{4,0},{5,1},{6,2},{7,3},{8,12},{9,13},{10,... | collective-permute-start | bytes 393224 | tf_op jit(solution)/shard_map/ppermute | solution.py:40
  614.0 14.7 %collective-permute-start.39 = (bf16[2,2,1,32,1024]{4,3,1,2,0:T(8,128)(2,1)S(1)}, bf16[2,2,1,32,1024]{4,3,1,2,0:T(8,128)(2,1)S(1)}, u32[]{:S(2)}, u32[]{:S(2)}) collective-permute-start(bf16[2,2,1,32,1024]{4,3,1,2,0:T(8,128)(2,1)S(1)} %pad_maximum_fusion.18), channel_id=1, source_target_pairs={{0,16},{1,17},{2,18},{3,19},{4,20},{5,21},{6,22},{7,23},{8,24},{9,... | collective-permute-start | bytes 786440 | tf_op jit(solution)/shard_map/ppermute | solution.py:40
  616.5 12.7 %collective-permute-start.37 = (bf16[2,2,1,32,1024]{4,3,1,2,0:T(8,128)(2,1)S(1)}, bf16[2,2,1,32,1024]{4,3,1,2,0:T(8,128)(2,1)S(1)}, u32[]{:S(2)}, u32[]{:S(2)}) collective-permute-start(bf16[2,2,1,32,1024]{4,3,1,2,0:T(8,128)(2,1)S(1)} %pad_maximum_fusion.17), channel_id=1, source_target_pairs={{0,8},{1,9},{2,10},{3,11},{4,12},{5,13},{6,14},{7,15},{8,0},{9,1},... | collective-permute-start | bytes 786440 | tf_op jit(solution)/shard_map/ppermute | solution.py:40
  629.3 9.7 %collective-permute-start.38 = (bf16[1,2,1,32,1024]{4,3,1,2,0:T(8,128)(2,1)S(1)}, bf16[1,2,1,32,1024]{4,3,1,2,0:T(8,128)(2,1)S(1)}, u32[]{:S(2)}, u32[]{:S(2)}) collective-permute-start(bf16[1,2,1,32,1024]{4,3,1,2,0:T(8,128)(2,1)S(1)} %fusion.223), channel_id=1, source_target_pairs={{0,16},{1,17},{2,18},{3,19},{4,20},{5,21},{6,22},{7,23},{8,24},{9,... | collective-permute-start | bytes 393224 | tf_op jit(solution)/shard_map/ppermute | solution.py:40
  642.7 49.0 %all-to-all-start = ((bf16[8,3,32,1024]{3,2,1,0:T(8,128)(2,1)}), bf16[8,3,32,1024]{3,2,1,0:T(8,128)(2,1)}, u32[]{:S(2)}, u32[]{:S(2)}) async-start(bf16[8,3,32,1024]{3,2,1,0:T(8,128)(2,1)} %bitcast.545), calls=%async_computation | async-start | bytes 3145728 | tf_op jit(solution)/shard_map/all_to_all | solution.py:639
  664.7 10.6 %collective-permute-start.81 = (f32[15,1024]{1,0:T(8,128)S(1)}, f32[15,1024]{1,0:T(8,128)S(1)}, u32[]{:S(2)}, u32[]{:S(2)}) collective-permute-start(f32[15,1024]{1,0:T(8,128)S(1)} %add.884), channel_id=1, source_target_pairs={{0,8},{1,9},{2,10},{3,11},{4,12},{5,13},{6,14},{7,15},{8,0},{9,1},... | collective-permute-start | bytes 184328 | tf_op jit(solution)/shard_map/ppermute | solution.py:40
  675.3 12.8 %collective-permute-start.82 = (f32[15,1024]{1,0:T(8,128)S(1)}, f32[15,1024]{1,0:T(8,128)S(1)}, u32[]{:S(2)}, u32[]{:S(2)}) collective-permute-start(f32[15,1024]{1,0:T(8,128)S(1)} %add.885), channel_id=1, source_target_pairs={{0,16},{1,17},{2,18},{3,19},{4,20},{5,21},{6,22},{7,23},{8,24},{9,... | collective-permute-start | bytes 184328 | tf_op jit(solution)/shard_map/ppermute | solution.py:40
  695.6 13.5 %collective-permute-start.42 = (bf16[256,256]{1,0:T(8,128)(2,1)S(1)}, bf16[256,256]{1,0:T(8,128)(2,1)S(1)}, u32[]{:S(2)}, u32[]{:S(2)}) collective-permute-start(bf16[256,256]{1,0:T(8,128)(2,1)S(1)} %get-tuple-element.333), channel_id=1, source_target_pairs={{0,1},{1,0},{2,3},{3,2},{4,5},{5,4},{6,7},{7,6},{8,9},{9,8},{10,11... | collective-permute-start | bytes 393224 | tf_op jit(solution)/shard_map/ppermute | solution.py:40
  696.9 13.8 %collective-permute-start.43 = (bf16[256,256]{1,0:T(8,128)(2,1)S(1)}, bf16[256,256]{1,0:T(8,128)(2,1)S(1)}, u32[]{:S(2)}, u32[]{:S(2)}) collective-permute-start(bf16[256,256]{1,0:T(8,128)(2,1)S(1)} %get-tuple-element.332), channel_id=1, source_target_pairs={{0,2},{1,3},{2,0},{3,1},{4,6},{5,7},{6,4},{7,5},{8,10},{9,11},{10,... | collective-permute-start | bytes 393224 | tf_op jit(solution)/shard_map/ppermute | solution.py:40
  697.5 14.4 %collective-permute-start.44 = (bf16[256,256]{1,0:T(8,128)(2,1)S(1)}, bf16[256,256]{1,0:T(8,128)(2,1)S(1)}, u32[]{:S(2)}, u32[]{:S(2)}) collective-permute-start(bf16[256,256]{1,0:T(8,128)(2,1)S(1)} %get-tuple-element.331), channel_id=1, source_target_pairs={{0,3},{1,2},{2,1},{3,0},{4,7},{5,6},{6,5},{7,4},{8,11},{9,10},{10,... | collective-permute-start | bytes 393224 | tf_op jit(solution)/shard_map/ppermute | solution.py:40
  699.9 13.6 %collective-permute-start.48 = (bf16[256,256]{1,0:T(8,128)(2,1)S(1)}, bf16[256,256]{1,0:T(8,128)(2,1)S(1)}, u32[]{:S(2)}, u32[]{:S(2)}) collective-permute-start(bf16[256,256]{1,0:T(8,128)(2,1)S(1)} %get-tuple-element.341), channel_id=1, source_target_pairs={{0,1},{1,0},{2,3},{3,2},{4,5},{5,4},{6,7},{7,6},{8,9},{9,8},{10,11... | collective-permute-start | bytes 393224 | tf_op jit(solution)/shard_map/ppermute | solution.py:40
  701.2 13.9 %collective-permute-start.49 = (bf16[256,256]{1,0:T(8,128)(2,1)S(1)}, bf16[256,256]{1,0:T(8,128)(2,1)S(1)}, u32[]{:S(2)}, u32[]{:S(2)}) collective-permute-start(bf16[256,256]{1,0:T(8,128)(2,1)S(1)} %get-tuple-element.340), channel_id=1, source_target_pairs={{0,2},{1,3},{2,0},{3,1},{4,6},{5,7},{6,4},{7,5},{8,10},{9,11},{10,... | collective-permute-start | bytes 393224 | tf_op jit(solution)/shard_map/ppermute | solution.py:40
  712.0 8.0 %collective-permute-start.55 = (bf16[256,256]{1,0:T(8,128)(2,1)S(1)}, bf16[256,256]{1,0:T(8,128)(2,1)S(1)}, u32[]{:S(2)}, u32[]{:S(2)}) collective-permute-start(bf16[256,256]{1,0:T(8,128)(2,1)S(1)} %get-tuple-element.348), channel_id=1, source_target_pairs={{0,2},{1,3},{2,0},{3,1},{4,6},{5,7},{6,4},{7,5},{8,10},{9,11},{10,... | collective-permute-start | bytes 393224 | tf_op jit(solution)/shard_map/ppermute | solution.py:40
  713.4 8.0 %collective-permute-start.56 = (bf16[256,256]{1,0:T(8,128)(2,1)S(1)}, bf16[256,256]{1,0:T(8,128)(2,1)S(1)}, u32[]{:S(2)}, u32[]{:S(2)}) collective-permute-start(bf16[256,256]{1,0:T(8,128)(2,1)S(1)} %get-tuple-element.347), channel_id=1, source_target_pairs={{0,3},{1,2},{2,1},{3,0},{4,7},{5,6},{6,5},{7,4},{8,11},{9,10},{10,... | collective-permute-start | bytes 393224 | tf_op jit(solution)/shard_map/ppermute | solution.py:40
  715.1 9.0 %collective-permute-start.45 = (bf16[256,256]{1,0:T(8,128)(2,1)S(1)}, bf16[256,256]{1,0:T(8,128)(2,1)S(1)}, u32[]{:S(2)}, u32[]{:S(2)}) collective-permute-start(bf16[256,256]{1,0:T(8,128)(2,1)S(1)} %get-tuple-element.329), channel_id=1, source_target_pairs={{0,1},{1,0},{2,3},{3,2},{4,5},{5,4},{6,7},{7,6},{8,9},{9,8},{10,11... | collective-permute-start | bytes 393224 | tf_op jit(solution)/shard_map/ppermute | solution.py:40
  716.4 9.3 %collective-permute-start.46 = (bf16[256,256]{1,0:T(8,128)(2,1)S(1)}, bf16[256,256]{1,0:T(8,128)(2,1)S(1)}, u32[]{:S(2)}, u32[]{:S(2)}) collective-permute-start(bf16[256,256]{1,0:T(8,128)(2,1)S(1)} %get-tuple-element.328), channel_id=1, source_target_pairs={{0,2},{1,3},{2,0},{3,1},{4,6},{5,7},{6,4},{7,5},{8,10},{9,11},{10,... | collective-permute-start | bytes 393224 | tf_op jit(solution)/shard_map/ppermute | solution.py:40
  718.5 8.7 %collective-permute-start.47 = (bf16[256,256]{1,0:T(8,128)(2,1)S(1)}, bf16[256,256]{1,0:T(8,128)(2,1)S(1)}, u32[]{:S(2)}, u32[]{:S(2)}) collective-permute-start(bf16[256,256]{1,0:T(8,128)(2,1)S(1)} %get-tuple-element.327), channel_id=1, source_target_pairs={{0,3},{1,2},{2,1},{3,0},{4,7},{5,6},{6,5},{7,4},{8,11},{9,10},{10,... | collective-permute-start | bytes 393224 | tf_op jit(solution)/shard_map/ppermute | solution.py:40
  720.0 10.0 %collective-permute-start.51 = (bf16[256,256]{1,0:T(8,128)(2,1)S(1)}, bf16[256,256]{1,0:T(8,128)(2,1)S(1)}, u32[]{:S(2)}, u32[]{:S(2)}) collective-permute-start(bf16[256,256]{1,0:T(8,128)(2,1)S(1)} %get-tuple-element.337), channel_id=1, source_target_pairs={{0,1},{1,0},{2,3},{3,2},{4,5},{5,4},{6,7},{7,6},{8,9},{9,8},{10,11... | collective-permute-start | bytes 393224 | tf_op jit(solution)/shard_map/ppermute | solution.py:40
  721.5 10.0 %collective-permute-start.52 = (bf16[256,256]{1,0:T(8,128)(2,1)S(1)}, bf16[256,256]{1,0:T(8,128)(2,1)S(1)}, u32[]{:S(2)}, u32[]{:S(2)}) collective-permute-start(bf16[256,256]{1,0:T(8,128)(2,1)S(1)} %get-tuple-element.336), channel_id=1, source_target_pairs={{0,2},{1,3},{2,0},{3,1},{4,6},{5,7},{6,4},{7,5},{8,10},{9,11},{10,... | collective-permute-start | bytes 393224 | tf_op jit(solution)/shard_map/ppermute | solution.py:40
  724.1 8.7 %collective-permute-start.53 = (bf16[256,256]{1,0:T(8,128)(2,1)S(1)}, bf16[256,256]{1,0:T(8,128)(2,1)S(1)}, u32[]{:S(2)}, u32[]{:S(2)}) collective-permute-start(bf16[256,256]{1,0:T(8,128)(2,1)S(1)} %get-tuple-element.335), channel_id=1, source_target_pairs={{0,3},{1,2},{2,1},{3,0},{4,7},{5,6},{6,5},{7,4},{8,11},{9,10},{10,... | collective-permute-start | bytes 393224 | tf_op jit(solution)/shard_map/ppermute | solution.py:40
  725.6 10.0 %collective-permute-start.57 = (bf16[256,256]{1,0:T(8,128)(2,1)S(1)}, bf16[256,256]{1,0:T(8,128)(2,1)S(1)}, u32[]{:S(2)}, u32[]{:S(2)}) collective-permute-start(bf16[256,256]{1,0:T(8,128)(2,1)S(1)} %get-tuple-element.345), channel_id=1, source_target_pairs={{0,1},{1,0},{2,3},{3,2},{4,5},{5,4},{6,7},{7,6},{8,9},{9,8},{10,11... | collective-permute-start | bytes 393224 | tf_op jit(solution)/shard_map/ppermute | solution.py:40
  727.1 10.0 %collective-permute-start.58 = (bf16[256,256]{1,0:T(8,128)(2,1)S(1)}, bf16[256,256]{1,0:T(8,128)(2,1)S(1)}, u32[]{:S(2)}, u32[]{:S(2)}) collective-permute-start(bf16[256,256]{1,0:T(8,128)(2,1)S(1)} %get-tuple-element.344), channel_id=1, source_target_pairs={{0,2},{1,3},{2,0},{3,1},{4,6},{5,7},{6,4},{7,5},{8,10},{9,11},{10,... | collective-permute-start | bytes 393224 | tf_op jit(solution)/shard_map/ppermute | solution.py:40
  730.0 8.5 %collective-permute-start.59 = (bf16[256,256]{1,0:T(8,128)(2,1)S(1)}, bf16[256,256]{1,0:T(8,128)(2,1)S(1)}, u32[]{:S(2)}, u32[]{:S(2)}) collective-permute-start(bf16[256,256]{1,0:T(8,128)(2,1)S(1)} %get-tuple-element.343), channel_id=1, source_target_pairs={{0,3},{1,2},{2,1},{3,0},{4,7},{5,6},{6,5},{7,4},{8,11},{9,10},{10,... | collective-permute-start | bytes 393224 | tf_op jit(solution)/shard_map/ppermute | solution.py:40
  731.4 24.7 %collective-permute-start.60 = (bf16[256,256]{1,0:T(8,128)(2,1)}, bf16[256,256]{1,0:T(8,128)(2,1)}, u32[]{:S(2)}, u32[]{:S(2)}) collective-permute-start(bf16[256,256]{1,0:T(8,128)(2,1)} %get-tuple-element.309), channel_id=1, source_target_pairs={{0,1},{1,0},{2,3},{3,2},{4,5},{5,4},{6,7},{7,6},{8,9},{9,8},{10,11... | collective-permute-start | bytes 393224 | tf_op jit(solution)/shard_map/ppermute | solution.py:40
  732.8 24.9 %collective-permute-start.61 = (bf16[256,256]{1,0:T(8,128)(2,1)}, bf16[256,256]{1,0:T(8,128)(2,1)}, u32[]{:S(2)}, u32[]{:S(2)}) collective-permute-start(bf16[256,256]{1,0:T(8,128)(2,1)} %get-tuple-element.308), channel_id=1, source_target_pairs={{0,2},{1,3},{2,0},{3,1},{4,6},{5,7},{6,4},{7,5},{8,10},{9,11},{10,... | collective-permute-start | bytes 393224 | tf_op jit(solution)/shard_map/ppermute | solution.py:40
  735.6 22.7 %collective-permute-start.62 = (bf16[256,256]{1,0:T(8,128)(2,1)}, bf16[256,256]{1,0:T(8,128)(2,1)}, u32[]{:S(2)}, u32[]{:S(2)}) collective-permute-start(bf16[256,256]{1,0:T(8,128)(2,1)} %get-tuple-element.307), channel_id=1, source_target_pairs={{0,3},{1,2},{2,1},{3,0},{4,7},{5,6},{6,5},{7,4},{8,11},{9,10},{10,... | collective-permute-start | bytes 393224 | tf_op jit(solution)/shard_map/ppermute | solution.py:40
  737.1 25.1 %collective-permute-start.66 = (bf16[256,256]{1,0:T(8,128)(2,1)}, bf16[256,256]{1,0:T(8,128)(2,1)}, u32[]{:S(2)}, u32[]{:S(2)}) collective-permute-start(bf16[256,256]{1,0:T(8,128)(2,1)} %get-tuple-element.317), channel_id=1, source_target_pairs={{0,1},{1,0},{2,3},{3,2},{4,5},{5,4},{6,7},{7,6},{8,9},{9,8},{10,11... | collective-permute-start | bytes 393224 | tf_op jit(solution)/shard_map/ppermute | solution.py:40
  738.5 25.3 %collective-permute-start.67 = (bf16[256,256]{1,0:T(8,128)(2,1)}, bf16[256,256]{1,0:T(8,128)(2,1)}, u32[]{:S(2)}, u32[]{:S(2)}) collective-permute-start(bf16[256,256]{1,0:T(8,128)(2,1)} %get-tuple-element.316), channel_id=1, source_target_pairs={{0,2},{1,3},{2,0},{3,1},{4,6},{5,7},{6,4},{7,5},{8,10},{9,11},{10,... | collective-permute-start | bytes 393224 | tf_op jit(solution)/shard_map/ppermute | solution.py:40
  756.1 8.2 %collective-permute-start.68 = (bf16[256,256]{1,0:T(8,128)(2,1)S(1)}, bf16[256,256]{1,0:T(8,128)(2,1)S(1)}, u32[]{:S(2)}, u32[]{:S(2)}) collective-permute-start(bf16[256,256]{1,0:T(8,128)(2,1)S(1)} %copy-done.99), channel_id=1, source_target_pairs={{0,3},{1,2},{2,1},{3,0},{4,7},{5,6},{6,5},{7,4},{8,11},{9,10},{10,... | collective-permute-start | bytes 393224 | tf_op jit(solution)/shard_map/ppermute | solution.py:40
  757.7 9.8 %collective-permute-start.72 = (bf16[256,256]{1,0:T(8,128)(2,1)S(1)}, bf16[256,256]{1,0:T(8,128)(2,1)S(1)}, u32[]{:S(2)}, u32[]{:S(2)}) collective-permute-start(bf16[256,256]{1,0:T(8,128)(2,1)S(1)} %get-tuple-element.325), channel_id=1, source_target_pairs={{0,1},{1,0},{2,3},{3,2},{4,5},{5,4},{6,7},{7,6},{8,9},{9,8},{10,11... | collective-permute-start | bytes 393224 | tf_op jit(solution)/shard_map/ppermute | solution.py:40
  758.3 10.8 %collective-permute-start.73 = (bf16[256,256]{1,0:T(8,128)(2,1)S(1)}, bf16[256,256]{1,0:T(8,128)(2,1)S(1)}, u32[]{:S(2)}, u32[]{:S(2)}) collective-permute-start(bf16[256,256]{1,0:T(8,128)(2,1)S(1)} %get-tuple-element.324), channel_id=1, source_target_pairs={{0,2},{1,3},{2,0},{3,1},{4,6},{5,7},{6,4},{7,5},{8,10},{9,11},{10,... | collective-permute-start | bytes 393224 | tf_op jit(solution)/shard_map/ppermute | solution.py:40
  763.7 8.2 %collective-permute-start.63 = (bf16[256,256]{0,1:T(8,128)(2,1)S(1)}, bf16[256,256]{0,1:T(8,128)(2,1)S(1)}, u32[]{:S(2)}, u32[]{:S(2)}) collective-permute-start(bf16[256,256]{0,1:T(8,128)(2,1)S(1)} %get-tuple-element.305), channel_id=1, source_target_pairs={{0,1},{1,0},{2,3},{3,2},{4,5},{5,4},{6,7},{7,6},{8,9},{9,8},{10,11... | collective-permute-start | bytes 393224 | tf_op jit(solution)/shard_map/ppermute | solution.py:40
  764.3 9.3 %collective-permute-start.64 = (bf16[256,256]{0,1:T(8,128)(2,1)S(1)}, bf16[256,256]{0,1:T(8,128)(2,1)S(1)}, u32[]{:S(2)}, u32[]{:S(2)}) collective-permute-start(bf16[256,256]{0,1:T(8,128)(2,1)S(1)} %get-tuple-element.304), channel_id=1, source_target_pairs={{0,2},{1,3},{2,0},{3,1},{4,6},{5,7},{6,4},{7,5},{8,10},{9,11},{10,... | collective-permute-start | bytes 393224 | tf_op jit(solution)/shard_map/ppermute | solution.py:40
  769.1 9.1 %collective-permute-start.69 = (bf16[256,256]{0,1:T(8,128)(2,1)S(1)}, bf16[256,256]{0,1:T(8,128)(2,1)S(1)}, u32[]{:S(2)}, u32[]{:S(2)}) collective-permute-start(bf16[256,256]{0,1:T(8,128)(2,1)S(1)} %get-tuple-element.313), channel_id=1, source_target_pairs={{0,1},{1,0},{2,3},{3,2},{4,5},{5,4},{6,7},{7,6},{8,9},{9,8},{10,11... | collective-permute-start | bytes 393224 | tf_op jit(solution)/shard_map/ppermute | solution.py:40
  769.7 10.1 %collective-permute-start.70 = (bf16[256,256]{0,1:T(8,128)(2,1)S(1)}, bf16[256,256]{0,1:T(8,128)(2,1)S(1)}, u32[]{:S(2)}, u32[]{:S(2)}) collective-permute-start(bf16[256,256]{0,1:T(8,128)(2,1)S(1)} %get-tuple-element.312), channel_id=1, source_target_pairs={{0,2},{1,3},{2,0},{3,1},{4,6},{5,7},{6,4},{7,5},{8,10},{9,11},{10,... | collective-permute-start | bytes 393224 | tf_op jit(solution)/shard_map/ppermute | solution.py:40
  771.9 8.0 %collective-permute-start.71 = (bf16[256,256]{0,1:T(8,128)(2,1)S(1)}, bf16[256,256]{0,1:T(8,128)(2,1)S(1)}, u32[]{:S(2)}, u32[]{:S(2)}) collective-permute-start(bf16[256,256]{0,1:T(8,128)(2,1)S(1)} %get-tuple-element.311), channel_id=1, source_target_pairs={{0,3},{1,2},{2,1},{3,0},{4,7},{5,6},{6,5},{7,4},{8,11},{9,10},{10,... | collective-permute-start | bytes 393224 | tf_op jit(solution)/shard_map/ppermute | solution.py:40
  773.6 8.6 %collective-permute-start.75 = (bf16[256,256]{0,1:T(8,128)(2,1)S(1)}, bf16[256,256]{0,1:T(8,128)(2,1)S(1)}, u32[]{:S(2)}, u32[]{:S(2)}) collective-permute-start(bf16[256,256]{0,1:T(8,128)(2,1)S(1)} %get-tuple-element.321), channel_id=1, source_target_pairs={{0,1},{1,0},{2,3},{3,2},{4,5},{5,4},{6,7},{7,6},{8,9},{9,8},{10,11... | collective-permute-start | bytes 393224 | tf_op jit(solution)/shard_map/ppermute | solution.py:40
  (200 other events, 2204.7 us)
Sparse Core Ops, SparseCore 0:
  11.9 55.3 all-gather.4
  69.9 80.9 all-gather.6
  165.2 88.1 all-gather.8
  308.4 86.5 reduce-scatter.12
  419.1 43.5 reduce-scatter.14
  466.0 86.4 reduce-scatter.16
  557.1 51.5 reduce-scatter.18
  611.3 71.5 all-gather.10
